TPU v7x, 256 devices: a whole 4x4x8 slice. The times are simulated.
256 devices in a mesh: section: 16 (over x, y), tp: 16 (over z, core).
Axes of the slice: x: 4, y: 4, z: 8, core: 2. Of those that a mesh axis runs over, the one named last changes fastest.
Arguments:
- partials: bfloat16 [16, 16, 128, 16384], P('section', 'tp'), may hold values from -6 to 6, as said below
- residual: bfloat16 [16, 128, 16384], P('section'), may hold values from -54 to 54
Outputs:
- mlp_input: bfloat16 [16, 128, 16384], P('section')
- next_hidden: bfloat16 [16, 128, 16384], P('section', 'tp')
Inputs may be any that keep to these rules, and one draw needn't show every extreme that they name: `partials`: every entry is a multiple of 1/64.
All inputs are finite; a program needn't handle non-finite values.
Results may differ from a plain program's by a relative error of at most 0.005.
Values may be sent and summed in bfloat16 or wider, within the bound.
No kernel may reach another device: no remote copies, remote signals or barrier semaphores. Data moves between devices by JAX's collectives and lax.ppermute only.
A program may use at most 128 MiB of HBM per device.

v0:
```python
import math

import jax
import jax.numpy as jnp
from jax import lax
from jax.sharding import PartitionSpec as P

BLOCK = 128


coded_peak = 448.0


def from_behind(block, axis, distance):
    devices = range(lax.axis_size(axis))
    route = [((i - distance) % len(devices), i) for i in devices]
    return lax.ppermute(block, axis, route)


def hadamard(order):
    index = jnp.arange(order, dtype=jnp.int32)
    common = jnp.bitwise_and(index[:, None], index[None, :])
    parity = jnp.zeros((order, order), jnp.int32)
    for bit_pos in range(int(math.log2(order))):
        parity = parity + jnp.bitwise_and(jnp.right_shift(common, bit_pos), 1)
    return (1 - 2 * jnp.bitwise_and(parity, 1)).astype(jnp.bfloat16)


def block_scale(peak_abs):
    scale = jnp.zeros_like(peak_abs) + 2.0 ** (-16)
    inverse = jnp.zeros_like(peak_abs) + 2.0**16
    for exponent in range(-16, 8):
        above = peak_abs > coded_peak * 2.0**exponent
        scale = jnp.where(above, 2.0 ** (exponent + 1), scale)
        inverse = jnp.where(above, 2.0 ** (-exponent - 1), inverse)
    return (scale, inverse)


def coarse_levels(values):
    magnitude = jnp.abs(values)
    quantum = jnp.zeros_like(magnitude) + 2.0 ** (-9)
    inverse = jnp.zeros_like(magnitude) + 2.0**9
    for exponent in range(-5, 9):
        above = magnitude >= 2.0**exponent
        quantum = jnp.where(above, 2.0 ** (exponent - 3), quantum)
        inverse = jnp.where(above, 2.0 ** (3 - exponent), inverse)
    levels = jnp.floor(magnitude * inverse + 0.5) * quantum
    return jnp.where(values < 0, -levels, levels)


def shards(partials, residual):
    hadamard_block = hadamard(BLOCK)
    local = partials[0, 0]
    stream = residual[0]
    rows_all, width = local.shape
    blocks = width // BLOCK
    rotated = jnp.dot(
        local.reshape(rows_all * blocks, BLOCK), hadamard_block, preferred_element_type=jnp.float32
    )
    rotated = rotated.reshape(rows_all, blocks, BLOCK)
    scale, inverse = block_scale(jnp.max(jnp.abs(rotated), axis=2))
    scales = scale.astype(jnp.bfloat16)
    coded = coarse_levels(rotated * inverse[:, :, None]).astype(jnp.bfloat16)
    ranks = lax.axis_size("tp")
    place = lax.axis_index("tp")
    share = width // ranks
    values = (
        lax.all_to_all(coded, "tp", split_axis=1, concat_axis=1, tiled=True).astype(jnp.float32)
        * lax.all_to_all(scales, "tp", split_axis=1, concat_axis=1, tiled=True).astype(jnp.float32)[
            :, :, None
        ]
    )
    values = values.reshape(values.shape[0], ranks, blocks // ranks, BLOCK)
    summed = (jnp.sum(values, axis=1) * BLOCK ** (-0.5)).reshape(values.shape[0], share)
    own_part = lax.dynamic_slice_in_dim(stream, place * share, share, 1)
    hidden = (own_part.astype(jnp.float32) + summed).astype(jnp.bfloat16)
    hidden_f = hidden.astype(jnp.float32)
    squares = lax.psum(jnp.sum(hidden_f * hidden_f, axis=1), "tp")
    inv_rms = lax.rsqrt(squares / width + 1e-05)
    normed = (hidden_f * inv_rms[:, None]).astype(jnp.bfloat16)
    mlp_input = lax.all_gather(normed, "tp", axis=1, tiled=True)
    outgoing = lax.all_to_all(hidden, "tp", split_axis=0, concat_axis=1, tiled=True)
    incoming = from_behind(outgoing, "section", 1)
    return (mlp_input[None], incoming[None])


def solution(mesh):
    placed = (P("section", "tp", None, None), P("section", None, None))
    return jax.shard_map(
        shards,
        mesh=mesh,
        in_specs=placed,
        out_specs=(P("section", None, None), P("section", "tp", None)),
        check_vma=False,
    )
```

profile of v0, /device:TPU:1, one launch (start us, length us, event | category | flops | bytes accessed | tf_op | source)
XLA Modules:
  0.0 267.6 jit_solution(17610443563323252731)
XLA Ops:
  7.2 7.4 %reshape_squeeze.3 = bf16[16384,128]{1,0:T(8,128)(2,1)} reshape(bf16[1,1,128,16384]{3,2,1,0:T(8,128)(2,1)} %param.2) | data formatting | bytes 8388608 | tf_op jit(solution)/shard_map/reshape;squeeze | solution.py:58
  14.5 6.7 %fusion.1 = (f32[16384]{0:T(1024)S(1)}, f32[128,16384]{1,0:T(8,128)}) fusion(bf16[16384,128]{1,0:T(8,128)(2,1)} %reshape_squeeze.3), kind=kOutput, calls=%fused_computation.4 | convolution fusion | flops 541458432 | bytes 12648448 | tf_op jit(solution)/shard_map/dot_general | solution.py:57
  21.3 0.2 select_select_fusion
  21.4 0.2 fusion.15
  21.6 0.6 gt.465
  22.3 0.5 copy.28
  22.8 0.6 gt.466
  23.4 0.5 copy.27
  24.0 0.6 gt.467
  24.6 0.5 copy.26
  25.1 0.6 gt.468
  25.8 0.5 copy.25
  26.3 0.6 gt.469
  26.9 0.5 copy.24
  27.4 0.6 gt.470
  28.1 0.5 copy.23
  28.6 0.6 gt.471
  29.2 0.5 copy.22
  29.8 0.6 gt.472
  30.4 0.5 copy.21
  30.9 0.6 gt.473
  31.6 0.5 copy.19
  32.1 0.6 reshape.323
  32.7 0.4 copy.20
  33.1 0.7 select_convert_fusion
  33.8 10.0 %all-to-all-start.1 = ((bf16[128,16,8]{0,2,1:T(8,128)(2,1)}), bf16[128,16,8]{0,2,1:T(8,128)(2,1)S(1)}, u32[]{:S(2)}, u32[]{:S(2)}) async-start(bf16[128,16,8]{0,2,1:T(8,128)(2,1)} %select_convert_fusion), calls=%async_computation.1 | async-start | bytes 65536 | tf_op jit(solution)/shard_map/all_to_all | solution.py:69
  43.8 8.1 %copy.30 = f32[16,8,128,128]{3,2,1,0:T(8,128)} copy(f32[16,8,128,128]{3,1,2,0:T(8,128)} %bitcast.74) | data formatting | bytes 16777216
  51.9 9.4 %copy.17 = f32[128,128,128]{2,0,1:T(8,128)} copy(f32[128,128,128]{1,0,2:T(8,128)} %bitcast.75) | data formatting | bytes 16777216 | tf_op jit(solution)/shard_map/reshape | solution.py:60
  61.3 0.1 copy.16
  61.4 17.8 %fusion = bf16[128,128,128]{2,0,1:T(8,128)(2,1)} fusion(f32[128,128,128]{2,0,1:T(8,128)} %copy.17, f32[128,128]{0,1:T(8,128)S(1)} %copy.16), kind=kLoop, calls=%fused_computation.1 | loop fusion | flops 109051904 | bytes 12648448 | tf_op jit(solution)/shard_map/convert_element_type | solution.py:63
  79.2 0.0 all-to-all-done.1
  79.2 7.2 %all-to-all-start = ((bf16[128,128,128]{2,0,1:T(8,128)(2,1)}), bf16[128,128,128]{2,0,1:T(8,128)(2,1)}, u32[]{:S(2)}, u32[]{:S(2)}) async-start(bf16[128,128,128]{2,0,1:T(8,128)(2,1)} %fusion), calls=%async_computation | async-start | bytes 8388608 | tf_op jit(solution)/shard_map/all_to_all | solution.py:68
  86.4 0.0 all-gather.2.cloned.1.call-start
  86.5 0.1 copy.29
  86.6 93.4 %all-to-all-done = bf16[128,128,128]{2,0,1:T(8,128)(2,1)} async-done(((bf16[128,128,128]{2,0,1:T(8,128)(2,1)}), bf16[128,128,128]{2,0,1:T(8,128)(2,1)}, u32[]{:S(2)}, u32[]{:S(2)}) %all-to-all-start) | async-done | bytes 4194336 | tf_op jit(solution)/shard_map/all_to_all | solution.py:68
  180.0 4.5 %bitcast_reduce_fusion = f32[128,8,128]{2,1,0:T(8,128)S(1)} fusion(bf16[128,128,128]{2,0,1:T(8,128)(2,1)} %all-to-all-done, f32[128,128]{1,0:T(8,128)S(1)} %copy.29), kind=kLoop, calls=%fused_computation.2 | loop fusion | flops 6160384 | bytes 4784128 | tf_op jit(solution)/shard_map/reduce_sum | solution.py:74
  184.6 1.1 fusion.2
  185.7 23.8 %psum.7 = f32[128]{0:T(128)S(1)} all-reduce(f32[128]{0:T(128)S(1)} %get-tuple-element.2), channel_id=1, replica_groups=mesh['section'=16,'tp'=16] {'tp'}, use_global_device_ids=true, to_apply=%region_3.4 | all-reduce | flops 128 | bytes 1024 | tf_op jit(solution)/shard_map/psum | solution.py:78
  209.5 0.8 fusion.3
  210.3 0.0 all-gather.2.cloned.1.call-update
  210.3 0.1 mul.67
  210.4 1.0 fusion.7
  211.4 19.5 %all_to_all.27 = bf16[16,8,1024]{2,1,0:T(8,128)(2,1)S(1)} all-to-all(bf16[16,8,1024]{2,1,0:T(8,128)(2,1)S(1)} %fusion.7), channel_id=1, replica_groups=mesh['section'=16,'tp'=16] {'tp'}, dimensions={0} | all-to-all | bytes 524288 | tf_op jit(solution)/shard_map/all_to_all | solution.py:82
  231.0 1.4 collective-permute-start
  232.4 9.6 %collective-permute-done = bf16[8,16384]{1,0:T(8,128)(2,1)S(1)} collective-permute-done((bf16[8,16384]{1,0:T(8,128)(2,1)S(1)}, bf16[8,16384]{1,0:T(8,128)(2,1)S(1)}, u32[]{:S(2)}, u32[]{:S(2)}) %collective-permute-start) | collective-permute-done | bytes 262176 | tf_op jit(solution)/shard_map/ppermute | solution.py:17
  242.0 13.5 %all-gather.2.cloned.1.call-done = bf16[128,16384]{1,0:T(8,128)(2,1)} async-done(((bf16[128,1024]{1,0:T(8,128)(2,1)}), bf16[128,16384]{1,0:T(8,128)(2,1)}) %all-gather.2.cloned.1.call-update) | async-done | bytes 4194320 | tf_op jit(solution)/shard_map/all_gather | solution.py:81
  255.5 4.6 %copy.37 = bf16[1,128,16384]{2,1,0:T(8,128)(2,1)} copy(bf16[1,128,16384]{2,1,0:T(8,128)(2,1)} %bitcast.77) | data formatting | bytes 8388608
  260.0 0.7 copy.38
  (3 shorter events, 0.1 us)
Async XLA Ops:
  33.8 45.4 %all-to-all-start.1 = ((bf16[128,16,8]{0,2,1:T(8,128)(2,1)}), bf16[128,16,8]{0,2,1:T(8,128)(2,1)S(1)}, u32[]{:S(2)}, u32[]{:S(2)}) async-start(bf16[128,16,8]{0,2,1:T(8,128)(2,1)} %select_convert_fusion), calls=%async_computation.1 | async-start | bytes 65536 | tf_op jit(solution)/shard_map/all_to_all | solution.py:69
  79.2 100.8 %all-to-all-start = ((bf16[128,128,128]{2,0,1:T(8,128)(2,1)}), bf16[128,128,128]{2,0,1:T(8,128)(2,1)}, u32[]{:S(2)}, u32[]{:S(2)}) async-start(bf16[128,128,128]{2,0,1:T(8,128)(2,1)} %fusion), calls=%async_computation | async-start | bytes 8388608 | tf_op jit(solution)/shard_map/all_to_all | solution.py:68
  86.4 169.0 %all-gather.2.cloned.1.call-start = ((), (), s32[]{:S(2)}) async-start(), calls=%async_computation.3 | async-start | bytes 4456448 | tf_op jit(solution)/shard_map/all_gather | solution.py:81
  231.0 11.0 %collective-permute-start = (bf16[8,16384]{1,0:T(8,128)(2,1)S(1)}, bf16[8,16384]{1,0:T(8,128)(2,1)S(1)}, u32[]{:S(2)}, u32[]{:S(2)}) collective-permute-start(bf16[8,16384]{1,0:T(8,128)(2,1)S(1)} %bitcast.79), channel_id=1, source_target_pairs={{240,0},{0,16},{16,32},{32,48},{48,64},{64,80},{80,96},{96,112},{1... | collective-permute-start | bytes 786440 | tf_op jit(solution)/shard_map/ppermute | solution.py:17
Sparse Core Ops, SparseCore 0:
  210.5 44.9 all-gather.1
where the time goes:
time: 268 us
  waiting for transfers between devices  117 us (44%)
  blocking collectives  43.3 us (16%)
  local copies, waits for them, and re-layouts  41.8 us (16%)
  other arithmetic  26.4 us (10%)
  starting transfers between devices  18.6 us (7%)
  between operations  14.2 us (5%)
  matrix products  6.73 us (3%)
    all_to_all x1, waiting for transfers between devices, shards(): lax.all_to_all(coded, 'tp', split_axis=1, concat_axis=1, tiled=True)  93.4 us
    psum x1, blocking collectives, shards(): squares = lax.psum(jnp.sum(hidden_f * hidden_f, axis=1), 'tp')  23.8 us
    all_to_all x1, blocking collectives, shards(): lax.all_to_all(hidden, 'tp', split_axis=0, concat_axis=1, tiled=True)  19.5 us
    convert_element_type x1, other arithmetic, shards(): coded = coarse_levels(rotated * inverse[:, :, None]).astype(jnp.bfloat16)  17.8 us
    all_gather x1, waiting for transfers between devices, shards(): mlp_input = lax.all_gather(normed, 'tp', axis=1, tiled=True)  13.5 us
    unnamed x3, local copies, waits for them, and re-layouts  13.3 us
    gt x18, local copies, waits for them, and re-layouts, block_scale(): above = peak_abs > coded_peak * 2.0 ** exponent  10.4 us
    all_to_all x1, starting transfers between devices, shards(): lax.all_to_all(scales, 'tp', split_axis=1, concat_axis=1, tiled=True)  9.98 us
  transfers between devices with their start and end apart: 4, of which 3 were waited for; matrix products, arithmetic and copies ran while one was open for 14% of the time, Pallas kernels for 0%

commit v1 on v0

v1 whole, which is shorter than its diff:
```python
import jax
import jax.numpy as jnp
import numpy as np
from jax import lax
from jax.experimental import pallas as pl
from jax.experimental.pallas import tpu as pltpu
from jax.sharding import PartitionSpec as P

BLOCK = 128
D = 16384
HALF = D // 2
PIECES = 2
COLS = HALF // PIECES
CHIPS = 8
FAR = CHIPS // 2
OWN = 8
GROUP = 2 * OWN
UNIT = 2048
VMEM = pl.BlockSpec(memory_space=pltpu.VMEM)
ANY = pl.BlockSpec(memory_space=pl.ANY)
GRANT = pltpu.CompilerParams(vmem_limit_bytes=16 * 2**20)


SMALL = pl.CostEstimate(flops=1, bytes_accessed=1, transcendentals=0)


def position():
    place = lax.axis_index("tp")
    core = lax.rem(place, 2)
    return place // 2, core, 1 - 2 * core


def chip_at(chip, offset):
    return lax.rem(chip + offset + CHIPS, CHIPS)


def hadamard():
    i = lax.broadcasted_iota(jnp.int32, (BLOCK, BLOCK), 0)
    j = lax.broadcasted_iota(jnp.int32, (BLOCK, BLOCK), 1)
    common = i & j
    common = common ^ (common >> 4)
    common = common ^ (common >> 2)
    common = common ^ (common >> 1)
    return (1 - 2 * (common & 1)).astype(jnp.float32).astype(jnp.bfloat16)


def small_limit(peak):
    target = peak * np.float32(1.5 * (1.0 - 2.0**-19) / 448.0 / 32.0)
    wide = target * np.float32(2.0**23 + 1.0)
    return wide - (wide - target)


def code(rotated):
    size = jnp.abs(rotated)
    limit = small_limit(jnp.max(size, axis=1, keepdims=True))
    nudged = rotated * np.float32(1.0 + 2.0**-20)
    wide = nudged * np.float32(2.0**20 + 1.0)
    wide = jnp.where(size < limit, limit * np.float32(1.5 * 2.0**19), wide)
    return wide - (wide - nudged)


def coded_half(held, slot, store):
    h = hadamard()
    for start in range(0, HALF, UNIT):
        cols = range(start, start + UNIT, BLOCK)
        x = jnp.concatenate([held[slot, :, b : b + BLOCK] for b in cols], axis=0)
        values = code(jnp.dot(x, h, preferred_element_type=jnp.float32))
        for i, b in enumerate(cols):
            at = slice(b % COLS, b % COLS + BLOCK)
            store(b // COLS, at, values[i * GROUP : (i + 1) * GROUP])


def code_group(held, group, out, first, halves):
    for i in range(halves):

        def store(piece, at, values, base=i * PIECES):
            out[base + piece, :, at] = values.astype(jnp.bfloat16)

        coded_half(held, 2 * group + (first + i) % 2, store)


def far_kernel(x_ref, stream_ref, keep, send, held, rows, arrived):
    chip, core, _ = position()
    far = chip_at(chip, FAR)

    def fetch(ref, group, half, target, slot):
        source = ref.at[
            pl.ds(pl.multiple_of(group * GROUP, GROUP), GROUP), half * HALF : (half + 1) * HALF
        ]
        return pltpu.make_async_copy(source, target, arrived.at[slot])

    copies = []
    for i in (4, 3, 5, 2, 6, 1, 7, 0):
        group = chip_at(chip, i)
        for half in range(2):
            copies.append(fetch(x_ref, group, half, held.at[2 * group + half], len(copies)))
    for half in range(2):
        copies.append(fetch(stream_ref, chip, half, rows.at[half], len(copies)))
    for copy in copies:
        copy.start()
    for copy in copies[:2]:
        copy.wait()
    code_group(held, far, keep, core, 1)
    code_group(held, far, send, 1 - core, 1)
    for copy in copies[2:]:
        copy.wait()


def code_far(local, stream):
    part = jax.ShapeDtypeStruct((PIECES, GROUP, COLS), jnp.bfloat16)
    whole = jax.ShapeDtypeStruct((2 * CHIPS, GROUP, HALF), jnp.bfloat16)
    rows = jax.ShapeDtypeStruct((2, GROUP, HALF), jnp.bfloat16)
    return pl.pallas_call(
        far_kernel,
        out_shape=(part, part, whole, rows),
        in_specs=[pl.BlockSpec(memory_space=pltpu.HBM)] * 2,
        out_specs=(VMEM,) * 4,
        scratch_shapes=[pltpu.SemaphoreType.DMA((2 * CHIPS + 2,))],
        compiler_params=GRANT,
        cost_estimate=SMALL,
    )(local, stream)


def code_kernel(k, held, keep, send):
    chip, core, way = position()
    code_group(held, chip_at(chip, way * k), keep, core, 2)
    code_group(held, chip_at(chip, -way * k), send, 1 - core, 2)


def code_rows(held, k, after):
    part = jax.ShapeDtypeStruct((2 * PIECES, GROUP, COLS), jnp.bfloat16)
    return pl.pallas_call(
        lambda held_ref, _, *refs: code_kernel(k, held_ref, *refs),
        out_shape=(part, part),
        in_specs=[VMEM, ANY],
        out_specs=(VMEM, VMEM),
        compiler_params=GRANT,
        cost_estimate=SMALL,
    )(held, after)


def own_kernel(held, stream, near_ref, send_ref, rows_ref):
    chip, core, _ = position()
    first = core == 0
    for half in range(2):

        def store(piece, at, values, half=half):
            top, low = values[:OWN], values[OWN:]
            mine = jnp.where(first, top, low).astype(jnp.bfloat16)
            theirs = jnp.where(first, low, top).astype(jnp.bfloat16)
            near_ref[((half + core) % 2) * PIECES + piece, :, at] = mine
            send_ref[((half + 1 - core) % 2) * PIECES + piece, :, at] = theirs

        coded_half(held, 2 * chip + half, store)
        for i in range(PIECES):
            rows = stream[half, :, i * COLS : (i + 1) * COLS].astype(jnp.float32)
            rows = jnp.where(first, rows[:OWN], rows[OWN:])
            rows_ref[((half + core) % 2) * PIECES + i] = rows.astype(jnp.bfloat16)


def own_rows(held, stream, after):
    part = jax.ShapeDtypeStruct((2 * PIECES, OWN, COLS), jnp.bfloat16)
    return pl.pallas_call(
        lambda held_ref, stream_ref, _, *refs: own_kernel(held_ref, stream_ref, *refs),
        out_shape=(part, part, part),
        in_specs=[VMEM, VMEM, ANY],
        out_specs=(VMEM,) * 3,
        compiler_params=GRANT,
        cost_estimate=SMALL,
    )(held, stream, after)


def add_kernel(i, keep, got, *rest):
    total = keep[i].astype(jnp.float32) + got[i].astype(jnp.float32)
    for arrived in rest[:-1]:
        total = total + arrived[...].astype(jnp.float32)
    rest[-1][...] = total.astype(jnp.bfloat16)


def add(i, keep, got, arrived):
    blocks = [keep, got] + ([] if arrived is None else [arrived])
    return pl.pallas_call(
        lambda *refs: add_kernel(i, *refs),
        out_shape=jax.ShapeDtypeStruct((GROUP, COLS), jnp.bfloat16),
        in_specs=[VMEM] * len(blocks),
        out_specs=VMEM,
        compiler_params=GRANT,
        cost_estimate=SMALL,
    )(*blocks)


def last_add_kernel(half, keep, got, arrived, same, cross):
    first = position()[1] == 0
    for j in range(PIECES):
        i = half * PIECES + j
        total = keep[i].astype(jnp.float32) + got[i].astype(jnp.float32)
        total = total + arrived[j][...].astype(jnp.float32)
        top, low = total[:OWN], total[OWN:]
        same[j] = jnp.where(first, top, low).astype(jnp.bfloat16)
        cross[j] = jnp.where(first, low, top).astype(jnp.bfloat16)


def last_add(half, keep, got, arrived):
    part = jax.ShapeDtypeStruct((PIECES, OWN, COLS), jnp.bfloat16)
    return pl.pallas_call(
        lambda *refs: last_add_kernel(
            half, refs[0], refs[1], refs[2:-2], *refs[-2:]
        ),
        out_shape=(part, part),
        in_specs=[VMEM] * (PIECES + 2),
        out_specs=(VMEM, VMEM),
        compiler_params=GRANT,
        cost_estimate=SMALL,
    )(keep, got, *arrived)


def norm_kernel(near, rows, got, same0, same1, cross0, cross1, hidden_ref, out0, out1):
    sames, crosses = (same0, same1), (cross1, cross0)
    f32 = jnp.float32
    squares = jnp.zeros((OWN, COLS), f32)
    for half in range(2):
        for j in range(PIECES):
            i = half * PIECES + j
            total = near[i].astype(f32) + got[i].astype(f32)
            total = total + sames[half][j].astype(f32) + crosses[half][j].astype(f32)
            hidden = rows[i].astype(f32) + total * np.float32(BLOCK**-0.5)
            hidden = hidden.astype(jnp.bfloat16)
            hidden_ref[i] = hidden
            hidden = hidden.astype(f32)
            squares = squares + hidden * hidden
    mean = jnp.sum(squares, axis=1, keepdims=True) / D
    inv_rms = lax.rsqrt(mean + np.float32(1e-05))
    for half, out in enumerate((out0, out1)):
        for j in range(PIECES):
            hidden = hidden_ref[half * PIECES + j].astype(f32)
            out[j] = (hidden * inv_rms).astype(jnp.bfloat16)


def norm(*blocks):
    part = jax.ShapeDtypeStruct((PIECES, OWN, COLS), jnp.bfloat16)
    return pl.pallas_call(
        norm_kernel,
        out_shape=(jax.ShapeDtypeStruct((2 * PIECES, OWN, COLS), jnp.bfloat16), part, part),
        in_specs=[VMEM] * len(blocks),
        out_specs=(VMEM,) * 3,
        compiler_params=GRANT,
        cost_estimate=SMALL,
    )(*blocks)


def join_kernel(count, *refs):
    at = 0
    for ref in refs[:count]:
        n = ref.shape[0]
        refs[-1][at : at + n] = ref[...]
        at += n


def join(blocks, after):
    n = sum(b.shape[0] for b in blocks)
    return pl.pallas_call(
        lambda *refs: join_kernel(len(blocks), *refs),
        out_shape=jax.ShapeDtypeStruct((n, OWN, COLS), jnp.bfloat16),
        in_specs=[VMEM] * len(blocks) + [ANY] * len(after),
        out_specs=VMEM,
        compiler_params=GRANT,
        cost_estimate=SMALL,
    )(*blocks, *after)


def put_kernel(places, aliased, *refs):
    sems, out, done = refs[-1], refs[-2], refs[-3]
    blocks = refs[aliased : aliased + len(places)]
    incoming = refs[-4]
    done[...] = jnp.zeros_like(done)
    chip, core, way = position()
    copies = []
    for block, held in zip(blocks, places):
        for i, (offset, rows, half) in enumerate(held):
            for j in range(PIECES):
                cols = pl.ds(pl.multiple_of(((core + half) % 2) * HALF + j * COLS, COLS), COLS)
                if offset is None:
                    target = incoming.at[0, :, cols]
                else:
                    owner = 2 * chip_at(chip, way * offset) + (core + rows) % 2
                    target = out.at[owner, :, cols]
                copies.append(
                    pltpu.make_async_copy(block.at[i * PIECES + j], target, sems.at[len(copies)])
                )
    for copy in copies:
        copy.start()
    for copy in copies:
        copy.wait()


def put(out, blocks, places):
    copies = PIECES * sum(len(p) for p in places)
    held = [] if out is None else [pltpu.with_memory_space_constraint(out, pltpu.HBM)]
    whole = pltpu.HBM((2 * CHIPS, OWN, D), jnp.bfloat16)
    rows = pltpu.HBM((1, OWN, D), jnp.bfloat16)
    done = jax.ShapeDtypeStruct((8, BLOCK), jnp.float32)
    with_rows = any(p[0] is None for held_places in places for p in held_places)
    outs = [rows, done, whole] if with_rows else [done, whole]
    space = pl.BlockSpec(memory_space=pltpu.HBM)
    return pl.pallas_call(
        lambda *refs: put_kernel(places, len(held), *refs),
        out_shape=outs,
        in_specs=[space] * len(held) + [VMEM] * len(blocks),
        out_specs=[space] * (len(outs) - 2) + [VMEM, space],
        scratch_shapes=[pltpu.SemaphoreType.DMA((copies,))],
        input_output_aliases={0: len(outs) - 1} if held else {},
        compiler_params=GRANT,
        cost_estimate=SMALL,
    )(*held, *blocks)


def shards(partials, residual):
    local = pltpu.with_memory_space_constraint(partials[0, 0], pltpu.HBM)
    stream = pltpu.with_memory_space_constraint(residual[0], pltpu.HBM)
    n = 2 * CHIPS

    def onward(block, cross=False):
        route = [(i, (i + 2 - 4 * (i % 2)) % n) for i in range(n)]
        return lax.ppermute(block, "tp", [(i, j ^ 1) if cross else (i, j) for i, j in route])

    def other_core(block):
        return lax.ppermute(block, "tp", [(i, i ^ 1) for i in range(n)])

    moving = [None] * (2 * PIECES)
    keep, send, held, rows = code_far(local, stream)
    for k in range(FAR, 1, -1):
        got = other_core(send)
        sums = [add(i, keep, got, moving[i]) for i in range(keep.shape[0])]
        keep, send = code_rows(held, k - 1, send)
        moving = [onward(block) for block in sums] + moving[len(sums) :]
    got = other_core(send)
    near, send, rows = own_rows(held, rows, send)
    same, cross = [], []
    for half in (0, 1):
        span = slice(half * PIECES, (half + 1) * PIECES)
        mine, theirs = last_add(half, keep, got, moving[span])
        same.append(onward(mine))
        cross.append(onward(theirs, True))
    hidden, *normed = norm(near, rows, other_core(send), *same, *cross)

    sections = lax.axis_size("section")
    theirs = [other_core(normed[1]), other_core(normed[0])]
    hidden = join([hidden], theirs[:1])
    incoming = lax.ppermute(hidden, "section", [(i, (i + 1) % sections) for i in range(sections)])

    moving = normed + theirs
    blocks = list(moving)
    places = [[(0, rows, half)] for rows in (0, 1) for half in (0, 1)]
    out = None
    joined, joined_places = [], []
    for k in range(1, FAR + 1):
        kept = [(rows, half) for rows in (0, 1) for half in (0, 1) if half == 0 or k < FAR]
        ready = [moving[2 * rows + half] for rows, half in kept]
        if k == 2:
            ready[-1] = join(ready[-1:], [incoming])
        moving = [onward(block) for block in ready]
        blocks += moving
        places += [[(-k, rows, half)] for rows, half in kept]
        if k == FAR - 1:
            blocks.append(incoming)
            places.append([(None, 0, 0), (None, 0, 1)])
            incoming, _, out = put(out, blocks, places)
            blocks, places = [], []
        joined += moving
        joined_places += [(k, 1 - rows, 1 - half) for rows, half in kept]
    blocks.append(other_core(join(joined, [])))
    places.append(joined_places)
    _, out = put(out, blocks, places)
    return (out.reshape(1, 2 * CHIPS * OWN, D), incoming)


def solution(mesh):
    placed = (P("section", "tp", None, None), P("section", None, None))
    return jax.shard_map(
        shards,
        mesh=mesh,
        in_specs=placed,
        out_specs=(P("section", None, None), P("section", "tp", None)),
        check_vma=False,
    )
```

time: 268 us -> 77.3 us (0.29)
  waiting for transfers between devices: 117 us -> 9.06 us
  blocking collectives: 43.3 us -> 0 us
  local copies, waits for them, and re-layouts: 41.8 us -> 0 us
  starting transfers between devices: 18.6 us -> 54.3 us
  other arithmetic: 26.4 us -> 0 us
  between operations: 14.2 us -> 1.01 us
  Pallas kernels: 0 us -> 12.8 us
  matrix products: 6.73 us -> 0 us
    all_to_all x2 -> x0, waiting for transfers between devices: 93.4 us -> none  [the longest x1 93.4 us: shards(): lax.all_to_all(coded, 'tp', split_axis=1, concat_axis=1, tiled=True)]
    ppermute x1 -> x37, starting transfers between devices: 1.4 us -> 54.3 us  [the longest x28 43.9 us: onward(): lax.ppermute(block, 'tp', [(i, j ^ 1) if cross else (i, j) for i, j in ro...]
    psum x1 -> x0, blocking collectives: 23.8 us -> none  [shards(): squares = lax.psum(jnp.sum(hidden_f * hidden_f, axis=1), 'tp')]
    convert_element_type x5 -> x0, other arithmetic: 20.4 us -> none  [the longest x1 17.8 us: shards(): coded = coarse_levels(rotated * inverse[:, :, None]).astype(jnp.bfloat16)]
    all_to_all x1 -> x0, blocking collectives: 19.5 us -> none  [shards(): lax.all_to_all(hidden, 'tp', split_axis=0, concat_axis=1, tiled=True)]
    all_to_all x2 -> x0, starting transfers between devices: 17.2 us -> none  [the longest x1 9.98 us: shards(): lax.all_to_all(scales, 'tp', split_axis=1, concat_axis=1, tiled=True)]
    all_gather x1 -> x0, waiting for transfers between devices: 13.5 us -> none  [shards(): mlp_input = lax.all_gather(normed, 'tp', axis=1, tiled=True)]
    unnamed x3 -> x0, local copies, waits for them, and re-layouts: 13.3 us -> none
  transfers between devices with their start and end apart: 4 -> 37, of which waited for: 3 -> 8; matrix products, arithmetic and copies ran while one was open for 14% -> 0% of each run, Pallas kernels for 0% -> 8%
where the time goes in v1:
time: 77.3 us
  starting transfers between devices  54.3 us (70%)
  Pallas kernels  12.8 us (17%)
  waiting for transfers between devices  9.06 us (12%)
  between operations  1.01 us (1%)
    ppermute x28, starting transfers between devices, onward(): lax.ppermute(block, 'tp', [(i, j ^ 1) if cross else (i, j) for i, j in ro...  43.9 us
    ppermute x8, starting transfers between devices, other_core(): return lax.ppermute(block, 'tp', [(i, i ^ 1) for i in range(n)])  9.01 us
    ppermute x28, waiting for transfers between devices, onward(): lax.ppermute(block, 'tp', [(i, j ^ 1) if cross else (i, j) for i, j in ro...  7.62 us
    pallas_call x2, Pallas kernels, put(): pl.pallas_call(lambda *refs: put_kernel(places, len(held), *refs), out_sh...  4.43 us
    pallas_call x3, Pallas kernels, code_rows(): pl.pallas_call(lambda held_ref, _, *refs: code_kernel(k, held_ref, *refs)...  3.85 us
    pallas_call x1, Pallas kernels, code_far(): pl.pallas_call(far_kernel, out_shape=(part, part, whole, rows), in_specs=...  2.47 us
  transfers between devices with their start and end apart: 37, of which 8 were waited for; matrix products, arithmetic and copies ran while one was open for 0% of the time, Pallas kernels for 8%

profile of v1, /device:TPU:1, one launch (start us, length us, event | category | flops | bytes accessed | tf_op | source)
XLA Modules:
  0.0 77.3 jit_solution(12191273300181987765)
XLA Ops:
  0.6 2.5 %shard_map.41 = (bf16[2,16,4096]{2,1,0:T(8,128)(2,1)S(1)}, bf16[2,16,4096]{2,1,0:T(8,128)(2,1)S(1)}, bf16[16,16,8192]{2,1,0:T(8,128)(2,1)S(1)}, bf16[2,16,8192]{2,1,0:T(8,128)(2,1)S(1)}) custom-call(bf16[128,16384]{1,0:T(8,128)(2,1)} %bitcast.4, bf16[128,16384]{1,0:T(8,128)(2,1)} %bitcast.5), custom_call_target="tpu_custom_call" | custom-call | flops 1 | bytes 1 | tf_op jit(solution)/shard_map/pallas_call | solution.py:113
  3.1 1.3 %shard_map.42 = (bf16[4,16,4096]{2,1,0:T(8,128)(2,1)S(1)}, bf16[4,16,4096]{2,1,0:T(8,128)(2,1)S(1)}) custom-call(bf16[16,16,8192]{2,1,0:T(8,128)(2,1)S(1)} %get-tuple-element.25.held_ref, bf16[2,16,4096]{2,1,0:T(8,128)(2,1)S(1)} %get-tuple-element.27._), custom_call_target="tpu_custom_call" | custom-call | flops 1 | bytes 1 | tf_op jit(solution)/shard_map/pallas_call | solution.py:132
  4.4 3.3 %collective-permute-start.3 = (bf16[4,16,4096]{2,1,0:T(8,128)(2,1)S(1)}, bf16[4,16,4096]{2,1,0:T(8,128)(2,1)S(1)}, u32[]{:S(2)}, u32[]{:S(2)}) collective-permute-start(bf16[4,16,4096]{2,1,0:T(8,128)(2,1)S(1)} %get-tuple-element.28._), channel_id=1, source_target_pairs={{0,1},{1,0},{2,3},{3,2},{4,5},{5,4},{6,7},{7,6},{8,9},{9,8},{10,11... | collective-permute-start | bytes 1572872 | tf_op jit(solution)/shard_map/ppermute | solution.py:327
  7.7 1.3 %shard_map.43 = (bf16[4,16,4096]{2,1,0:T(8,128)(2,1)S(1)}, bf16[4,16,4096]{2,1,0:T(8,128)(2,1)S(1)}) custom-call(bf16[16,16,8192]{2,1,0:T(8,128)(2,1)S(1)} %get-tuple-element.25.held_ref, bf16[4,16,4096]{2,1,0:T(8,128)(2,1)S(1)} %get-tuple-element.28._), custom_call_target="tpu_custom_call" | custom-call | flops 1 | bytes 1 | tf_op jit(solution)/shard_map/pallas_call | solution.py:132
  9.1 0.5 collective-permute-start.4
  9.6 1.3 %shard_map.44 = (bf16[4,16,4096]{2,1,0:T(8,128)(2,1)S(1)}, bf16[4,16,4096]{2,1,0:T(8,128)(2,1)S(1)}) custom-call(bf16[16,16,8192]{2,1,0:T(8,128)(2,1)S(1)} %get-tuple-element.25.held_ref, bf16[4,16,4096]{2,1,0:T(8,128)(2,1)S(1)} %get-tuple-element.29._), custom_call_target="tpu_custom_call" | custom-call | flops 1 | bytes 1 | tf_op jit(solution)/shard_map/pallas_call | solution.py:132
  10.9 0.2 collective-permute-start.1
  11.1 0.3 collective-permute-done.4.refs_1_
  11.4 3.9 %collective-permute-start.5 = (bf16[16,4096]{1,0:T(8,128)(2,1)S(1)}, bf16[16,4096]{1,0:T(8,128)(2,1)S(1)}, u32[]{:S(2)}, u32[]{:S(2)}) collective-permute-start(bf16[16,4096]{1,0:T(8,128)(2,1)S(1)} %shard_map.46), channel_id=1, source_target_pairs={{0,2},{1,15},{2,4},{3,1},{4,6},{5,3},{6,8},{7,5},{8,10},{9,7},{10,... | collective-permute-start | bytes 393224 | tf_op jit(solution)/shard_map/ppermute | solution.py:324
  15.4 0.8 %collective-permute-start.8 = (bf16[16,4096]{1,0:T(8,128)(2,1)S(1)}, bf16[16,4096]{1,0:T(8,128)(2,1)S(1)}, u32[]{:S(2)}, u32[]{:S(2)}) collective-permute-start(bf16[16,4096]{1,0:T(8,128)(2,1)S(1)} %shard_map.49), channel_id=1, source_target_pairs={{0,2},{1,15},{2,4},{3,1},{4,6},{5,3},{6,8},{7,5},{8,10},{9,7},{10,... | collective-permute-start | bytes 393224 | tf_op jit(solution)/shard_map/ppermute | solution.py:324
  16.2 0.8 %collective-permute-start.12 = (bf16[16,4096]{1,0:T(8,128)(2,1)S(1)}, bf16[16,4096]{1,0:T(8,128)(2,1)S(1)}, u32[]{:S(2)}, u32[]{:S(2)}) collective-permute-start(bf16[16,4096]{1,0:T(8,128)(2,1)S(1)} %shard_map.53), channel_id=1, source_target_pairs={{0,2},{1,15},{2,4},{3,1},{4,6},{5,3},{6,8},{7,5},{8,10},{9,7},{10,... | collective-permute-start | bytes 393224 | tf_op jit(solution)/shard_map/ppermute | solution.py:324
  17.1 0.2 collective-permute-done.5.refs_2_
  17.3 3.1 %collective-permute-start.14 = (bf16[16,4096]{1,0:T(8,128)(2,1)S(1)}, bf16[16,4096]{1,0:T(8,128)(2,1)S(1)}, u32[]{:S(2)}, u32[]{:S(2)}) collective-permute-start(bf16[16,4096]{1,0:T(8,128)(2,1)S(1)} %shard_map.55), channel_id=1, source_target_pairs={{0,2},{1,15},{2,4},{3,1},{4,6},{5,3},{6,8},{7,5},{8,10},{9,7},{10,... | collective-permute-start | bytes 393224 | tf_op jit(solution)/shard_map/ppermute | solution.py:324
  20.4 1.3 %collective-permute-start.6 = (bf16[16,4096]{1,0:T(8,128)(2,1)S(1)}, bf16[16,4096]{1,0:T(8,128)(2,1)S(1)}, u32[]{:S(2)}, u32[]{:S(2)}) collective-permute-start(bf16[16,4096]{1,0:T(8,128)(2,1)S(1)} %shard_map.47), channel_id=1, source_target_pairs={{0,2},{1,15},{2,4},{3,1},{4,6},{5,3},{6,8},{7,5},{8,10},{9,7},{10,... | collective-permute-start | bytes 393224 | tf_op jit(solution)/shard_map/ppermute | solution.py:324
  22.0 1.5 %collective-permute-start.13 = (bf16[16,4096]{1,0:T(8,128)(2,1)S(1)}, bf16[16,4096]{1,0:T(8,128)(2,1)S(1)}, u32[]{:S(2)}, u32[]{:S(2)}) collective-permute-start(bf16[16,4096]{1,0:T(8,128)(2,1)S(1)} %shard_map.54), channel_id=1, source_target_pairs={{0,2},{1,15},{2,4},{3,1},{4,6},{5,3},{6,8},{7,5},{8,10},{9,7},{10,... | collective-permute-start | bytes 393224 | tf_op jit(solution)/shard_map/ppermute | solution.py:324
  23.6 2.0 %collective-permute-start.15 = (bf16[16,4096]{1,0:T(8,128)(2,1)S(1)}, bf16[16,4096]{1,0:T(8,128)(2,1)S(1)}, u32[]{:S(2)}, u32[]{:S(2)}) collective-permute-start(bf16[16,4096]{1,0:T(8,128)(2,1)S(1)} %shard_map.56), channel_id=1, source_target_pairs={{0,2},{1,15},{2,4},{3,1},{4,6},{5,3},{6,8},{7,5},{8,10},{9,7},{10,... | collective-permute-start | bytes 393224 | tf_op jit(solution)/shard_map/ppermute | solution.py:324
  25.5 0.9 %shard_map.45 = (bf16[4,8,4096]{2,1,0:T(8,128)(2,1)S(1)}, bf16[4,8,4096]{2,1,0:T(8,128)(2,1)S(1)}, bf16[4,8,4096]{2,1,0:T(8,128)(2,1)S(1)}) custom-call(bf16[16,16,8192]{2,1,0:T(8,128)(2,1)S(1)} %get-tuple-element.25.held_ref, bf16[2,16,8192]{2,1,0:T(8,128)(2,1)S(1)} %get-tuple-element.26.stream_ref, bf16[4,16,4096]{2,1,0:T(8,128)(2,1)S(1)} %get-tuple-element.30._), custom_call_target="tpu_custom_call" | custom-call | flops 1 | bytes 1 | tf_op jit(solution)/shard_map/pallas_call | solution.py:163
  26.5 0.5 collective-permute-start.7
  27.0 1.3 %collective-permute-start.10 = (bf16[16,4096]{1,0:T(8,128)(2,1)S(1)}, bf16[16,4096]{1,0:T(8,128)(2,1)S(1)}, u32[]{:S(2)}, u32[]{:S(2)}) collective-permute-start(bf16[16,4096]{1,0:T(8,128)(2,1)S(1)} %shard_map.51), channel_id=1, source_target_pairs={{0,2},{1,15},{2,4},{3,1},{4,6},{5,3},{6,8},{7,5},{8,10},{9,7},{10,... | collective-permute-start | bytes 393224 | tf_op jit(solution)/shard_map/ppermute | solution.py:324
  28.4 1.0 %collective-permute-start = (bf16[4,8,4096]{2,1,0:T(8,128)(2,1)S(1)}, bf16[4,8,4096]{2,1,0:T(8,128)(2,1)S(1)}, u32[]{:S(2)}, u32[]{:S(2)}) collective-permute-start(bf16[4,8,4096]{2,1,0:T(8,128)(2,1)S(1)} %get-tuple-element.33), channel_id=1, source_target_pairs={{0,1},{1,0},{2,3},{3,2},{4,5},{5,4},{6,7},{7,6},{8,9},{9,8},{10,11... | collective-permute-start | bytes 786440 | tf_op jit(solution)/shard_map/ppermute | solution.py:327
  29.5 1.9 %collective-permute-start.16 = (bf16[2,8,4096]{2,1,0:T(8,128)(2,1)S(1)}, bf16[2,8,4096]{2,1,0:T(8,128)(2,1)S(1)}, u32[]{:S(2)}, u32[]{:S(2)}) collective-permute-start(bf16[2,8,4096]{2,1,0:T(8,128)(2,1)S(1)} %get-tuple-element.39), channel_id=1, source_target_pairs={{0,2},{1,15},{2,4},{3,1},{4,6},{5,3},{6,8},{7,5},{8,10},{9,7},{10,... | collective-permute-start | bytes 393224 | tf_op jit(solution)/shard_map/ppermute | solution.py:324
  31.4 3.5 %collective-permute-start.18 = (bf16[2,8,4096]{2,1,0:T(8,128)(2,1)S(1)}, bf16[2,8,4096]{2,1,0:T(8,128)(2,1)S(1)}, u32[]{:S(2)}, u32[]{:S(2)}) collective-permute-start(bf16[2,8,4096]{2,1,0:T(8,128)(2,1)S(1)} %get-tuple-element.41), channel_id=1, source_target_pairs={{0,3},{1,14},{2,5},{3,0},{4,7},{5,2},{6,9},{7,4},{8,11},{9,6},{10,... | collective-permute-start | bytes 393224 | tf_op jit(solution)/shard_map/ppermute | solution.py:324
  35.1 3.5 %collective-permute-start.17 = (bf16[2,8,4096]{2,1,0:T(8,128)(2,1)S(1)}, bf16[2,8,4096]{2,1,0:T(8,128)(2,1)S(1)}, u32[]{:S(2)}, u32[]{:S(2)}) collective-permute-start(bf16[2,8,4096]{2,1,0:T(8,128)(2,1)S(1)} %get-tuple-element.40), channel_id=1, source_target_pairs={{0,3},{1,14},{2,5},{3,0},{4,7},{5,2},{6,9},{7,4},{8,11},{9,6},{10,... | collective-permute-start | bytes 393224 | tf_op jit(solution)/shard_map/ppermute | solution.py:324
  38.6 0.4 collective-permute-done.18.cross1
  39.0 3.7 %collective-permute-done.17.cross0 = bf16[2,8,4096]{2,1,0:T(8,128)(2,1)S(1)} collective-permute-done((bf16[2,8,4096]{2,1,0:T(8,128)(2,1)S(1)}, bf16[2,8,4096]{2,1,0:T(8,128)(2,1)S(1)}, u32[]{:S(2)}, u32[]{:S(2)}) %collective-permute-start.17) | collective-permute-done | bytes 131104 | tf_op jit(solution)/shard_map/ppermute | solution.py:324
  42.7 0.4 shard_map.58
  43.2 1.7 %collective-permute-start.21 = (bf16[2,8,4096]{2,1,0:T(8,128)(2,1)S(1)}, bf16[2,8,4096]{2,1,0:T(8,128)(2,1)S(1)}, u32[]{:S(2)}, u32[]{:S(2)}) collective-permute-start(bf16[2,8,4096]{2,1,0:T(8,128)(2,1)S(1)} %get-tuple-element.42.refs_0_), channel_id=1, source_target_pairs={{0,2},{1,15},{2,4},{3,1},{4,6},{5,3},{6,8},{7,5},{8,10},{9,7},{10,... | collective-permute-start | bytes 393224 | tf_op jit(solution)/shard_map/ppermute | solution.py:324
  44.8 1.0 %collective-permute-start.23 = (bf16[2,8,4096]{2,1,0:T(8,128)(2,1)S(1)}, bf16[2,8,4096]{2,1,0:T(8,128)(2,1)S(1)}, u32[]{:S(2)}, u32[]{:S(2)}) collective-permute-start(bf16[2,8,4096]{2,1,0:T(8,128)(2,1)S(1)} %collective-permute-done.19.refs_1_.refs_2_), channel_id=1, source_target_pairs={{0,2},{1,15},{2,4},{3,1},{4,6},{5,3},{6,8},{7,5},{8,10},{9,7},{10,... | collective-permute-start | bytes 393224 | tf_op jit(solution)/shard_map/ppermute | solution.py:324
  45.8 1.4 %collective-permute-start.28 = (bf16[4,8,4096]{2,1,0:T(8,128)(2,1)S(1)}, bf16[4,8,4096]{2,1,0:T(8,128)(2,1)S(1)}, u32[]{:S(2)}, u32[]{:S(2)}) collective-permute-start(bf16[4,8,4096]{2,1,0:T(8,128)(2,1)S(1)} %shard_map.59), channel_id=1, source_target_pairs={{0,16},{16,32},{32,48},{48,64},{64,80},{80,96},{96,112},{112,128},... | collective-permute-start | bytes 786440 | tf_op jit(solution)/shard_map/ppermute | solution.py:349
  47.2 1.8 %collective-permute-start.22 = (bf16[2,8,4096]{2,1,0:T(8,128)(2,1)S(1)}, bf16[2,8,4096]{2,1,0:T(8,128)(2,1)S(1)}, u32[]{:S(2)}, u32[]{:S(2)}) collective-permute-start(bf16[2,8,4096]{2,1,0:T(8,128)(2,1)S(1)} %get-tuple-element.43.refs_1_), channel_id=1, source_target_pairs={{0,2},{1,15},{2,4},{3,1},{4,6},{5,3},{6,8},{7,5},{8,10},{9,7},{10,... | collective-permute-start | bytes 393224 | tf_op jit(solution)/shard_map/ppermute | solution.py:324
  49.0 0.8 %collective-permute-start.25 = (bf16[2,8,4096]{2,1,0:T(8,128)(2,1)S(1)}, bf16[2,8,4096]{2,1,0:T(8,128)(2,1)S(1)}, u32[]{:S(2)}, u32[]{:S(2)}) collective-permute-start(bf16[2,8,4096]{2,1,0:T(8,128)(2,1)S(1)} %collective-permute-done.21.refs_4_.refs_0_), channel_id=1, source_target_pairs={{0,2},{1,15},{2,4},{3,1},{4,6},{5,3},{6,8},{7,5},{8,10},{9,7},{10,... | collective-permute-start | bytes 393224 | tf_op jit(solution)/shard_map/ppermute | solution.py:324
  49.9 1.4 %collective-permute-start.27 = (bf16[2,8,4096]{2,1,0:T(8,128)(2,1)S(1)}, bf16[2,8,4096]{2,1,0:T(8,128)(2,1)S(1)}, u32[]{:S(2)}, u32[]{:S(2)}) collective-permute-start(bf16[2,8,4096]{2,1,0:T(8,128)(2,1)S(1)} %collective-permute-done.23.refs_6_.refs_2_), channel_id=1, source_target_pairs={{0,2},{1,15},{2,4},{3,1},{4,6},{5,3},{6,8},{7,5},{8,10},{9,7},{10,... | collective-permute-start | bytes 393224 | tf_op jit(solution)/shard_map/ppermute | solution.py:324
  51.3 3.0 %collective-permute-start.26 = (bf16[2,8,4096]{2,1,0:T(8,128)(2,1)S(1)}, bf16[2,8,4096]{2,1,0:T(8,128)(2,1)S(1)}, u32[]{:S(2)}, u32[]{:S(2)}) collective-permute-start(bf16[2,8,4096]{2,1,0:T(8,128)(2,1)S(1)} %collective-permute-done.22.refs_5_.refs_1_), channel_id=1, source_target_pairs={{0,2},{1,15},{2,4},{3,1},{4,6},{5,3},{6,8},{7,5},{8,10},{9,7},{10,... | collective-permute-start | bytes 393224 | tf_op jit(solution)/shard_map/ppermute | solution.py:324
  54.3 1.4 %collective-permute-start.30 = (bf16[2,8,4096]{2,1,0:T(8,128)(2,1)S(1)}, bf16[2,8,4096]{2,1,0:T(8,128)(2,1)S(1)}, u32[]{:S(2)}, u32[]{:S(2)}) collective-permute-start(bf16[2,8,4096]{2,1,0:T(8,128)(2,1)S(1)} %collective-permute-done.25.refs_8_.refs_4_), channel_id=1, source_target_pairs={{0,2},{1,15},{2,4},{3,1},{4,6},{5,3},{6,8},{7,5},{8,10},{9,7},{10,... | collective-permute-start | bytes 393224 | tf_op jit(solution)/shard_map/ppermute | solution.py:324
  55.7 1.4 %collective-permute-start.32 = (bf16[2,8,4096]{2,1,0:T(8,128)(2,1)S(1)}, bf16[2,8,4096]{2,1,0:T(8,128)(2,1)S(1)}, u32[]{:S(2)}, u32[]{:S(2)}) collective-permute-start(bf16[2,8,4096]{2,1,0:T(8,128)(2,1)S(1)} %collective-permute-done.27.refs_10_.refs_6_), channel_id=1, source_target_pairs={{0,2},{1,15},{2,4},{3,1},{4,6},{5,3},{6,8},{7,5},{8,10},{9,7},{10,... | collective-permute-start | bytes 393224 | tf_op jit(solution)/shard_map/ppermute | solution.py:324
  57.2 2.1 %collective-permute-start.29 = (bf16[2,8,4096]{2,1,0:T(8,128)(2,1)S(1)}, bf16[2,8,4096]{2,1,0:T(8,128)(2,1)S(1)}, u32[]{:S(2)}, u32[]{:S(2)}) collective-permute-start(bf16[2,8,4096]{2,1,0:T(8,128)(2,1)S(1)} %shard_map.60), channel_id=1, source_target_pairs={{0,2},{1,15},{2,4},{3,1},{4,6},{5,3},{6,8},{7,5},{8,10},{9,7},{10,... | collective-permute-start | bytes 393224 | tf_op jit(solution)/shard_map/ppermute | solution.py:324
  59.3 0.8 collective-permute-start.31
  60.1 1.0 %collective-permute-start.34 = (bf16[2,8,4096]{2,1,0:T(8,128)(2,1)S(1)}, bf16[2,8,4096]{2,1,0:T(8,128)(2,1)S(1)}, u32[]{:S(2)}, u32[]{:S(2)}) collective-permute-start(bf16[2,8,4096]{2,1,0:T(8,128)(2,1)S(1)} %collective-permute-done.30.refs_12_.refs_8_), channel_id=1, source_target_pairs={{0,2},{1,15},{2,4},{3,1},{4,6},{5,3},{6,8},{7,5},{8,10},{9,7},{10,... | collective-permute-start | bytes 393224 | tf_op jit(solution)/shard_map/ppermute | solution.py:324
  61.1 1.4 %collective-permute-start.35 = (bf16[2,8,4096]{2,1,0:T(8,128)(2,1)S(1)}, bf16[2,8,4096]{2,1,0:T(8,128)(2,1)S(1)}, u32[]{:S(2)}, u32[]{:S(2)}) collective-permute-start(bf16[2,8,4096]{2,1,0:T(8,128)(2,1)S(1)} %collective-permute-done.32.refs_14_.refs_10_), channel_id=1, source_target_pairs={{0,2},{1,15},{2,4},{3,1},{4,6},{5,3},{6,8},{7,5},{8,10},{9,7},{10,... | collective-permute-start | bytes 393224 | tf_op jit(solution)/shard_map/ppermute | solution.py:324
  62.5 1.8 %collective-permute-start.33 = (bf16[2,8,4096]{2,1,0:T(8,128)(2,1)S(1)}, bf16[2,8,4096]{2,1,0:T(8,128)(2,1)S(1)}, u32[]{:S(2)}, u32[]{:S(2)}) collective-permute-start(bf16[2,8,4096]{2,1,0:T(8,128)(2,1)S(1)} %collective-permute-done.29.refs_11_.refs_7_), channel_id=1, source_target_pairs={{0,2},{1,15},{2,4},{3,1},{4,6},{5,3},{6,8},{7,5},{8,10},{9,7},{10,... | collective-permute-start | bytes 393224 | tf_op jit(solution)/shard_map/ppermute | solution.py:324
  64.3 0.5 collective-permute-done.34.refs_12_.refs_1_
  64.8 1.3 %collective-permute-done.35.refs_13_.refs_2_ = bf16[2,8,4096]{2,1,0:T(8,128)(2,1)S(1)} collective-permute-done((bf16[2,8,4096]{2,1,0:T(8,128)(2,1)S(1)}, bf16[2,8,4096]{2,1,0:T(8,128)(2,1)S(1)}, u32[]{:S(2)}, u32[]{:S(2)}) %collective-permute-start.35) | collective-permute-done | bytes 131104 | tf_op jit(solution)/shard_map/ppermute | solution.py:324
  66.1 1.5 %collective-permute-done.33.refs_15_.refs_11_ = bf16[2,8,4096]{2,1,0:T(8,128)(2,1)S(1)} collective-permute-done((bf16[2,8,4096]{2,1,0:T(8,128)(2,1)S(1)}, bf16[2,8,4096]{2,1,0:T(8,128)(2,1)S(1)}, u32[]{:S(2)}, u32[]{:S(2)}) %collective-permute-start.33) | collective-permute-done | bytes 131104 | tf_op jit(solution)/shard_map/ppermute | solution.py:324
  67.6 0.1 shard_map.62
  67.7 3.8 %collective-permute-start.36 = (bf16[28,8,4096]{2,1,0:T(8,128)(2,1)S(1)}, bf16[28,8,4096]{2,1,0:T(8,128)(2,1)S(1)}, u32[]{:S(2)}, u32[]{:S(2)}) collective-permute-start(bf16[28,8,4096]{2,1,0:T(8,128)(2,1)S(1)} %shard_map.62), channel_id=1, source_target_pairs={{0,1},{1,0},{2,3},{3,2},{4,5},{5,4},{6,7},{7,6},{8,9},{9,8},{10,11... | collective-permute-start | bytes 5505032 | tf_op jit(solution)/shard_map/ppermute | solution.py:327
  71.5 2.3 %shard_map.61 = (bf16[1,8,16384]{2,1,0:T(8,128)(2,1)}, f32[8,128]{1,0:T(8,128)}, bf16[16,8,16384]{2,1,0:T(8,128)(2,1)}) custom-call(bf16[2,8,4096]{2,1,0:T(8,128)(2,1)S(1)} %get-tuple-element.42.refs_0_, bf16[2,8,4096]{2,1,0:T(8,128)(2,1)S(1)} %get-tuple-element.43.refs_1_, bf16[2,8,4096]{2,1,0:T(8,128)(2,1)S(1)} %collective-permute-done.19.refs_1_.refs_2_, ...), custom_call_target="tpu_custom_call" | custom-call | flops 1 | bytes 1 | tf_op jit(solution)/shard_map/pallas_call | solution.py:305
  73.8 1.1 %collective-permute-done.36.refs_3_ = bf16[28,8,4096]{2,1,0:T(8,128)(2,1)S(1)} collective-permute-done((bf16[28,8,4096]{2,1,0:T(8,128)(2,1)S(1)}, bf16[28,8,4096]{2,1,0:T(8,128)(2,1)S(1)}, u32[]{:S(2)}, u32[]{:S(2)}) %collective-permute-start.36) | collective-permute-done | bytes 1835040 | tf_op jit(solution)/shard_map/ppermute | solution.py:327
  74.9 2.2 %shard_map.63 = (f32[8,128]{1,0:T(8,128)}, bf16[16,8,16384]{2,1,0:T(8,128)(2,1)}) custom-call(bf16[16,8,16384]{2,1,0:T(8,128)(2,1)} %get-tuple-element.45.refs_0_, bf16[2,8,4096]{2,1,0:T(8,128)(2,1)S(1)} %collective-permute-done.34.refs_12_.refs_1_, ...), custom_call_target="tpu_custom_call", output_to_operand_aliasing={{1}: (0, {})} | custom-call | flops 1 | bytes 1 | tf_op jit(solution)/shard_map/pallas_call | solution.py:305
  (49 shorter events, 1.2 us)
Async XLA Ops:
  4.4 11.8 %collective-permute-start.3 = (bf16[4,16,4096]{2,1,0:T(8,128)(2,1)S(1)}, bf16[4,16,4096]{2,1,0:T(8,128)(2,1)S(1)}, u32[]{:S(2)}, u32[]{:S(2)}) collective-permute-start(bf16[4,16,4096]{2,1,0:T(8,128)(2,1)S(1)} %get-tuple-element.28._), channel_id=1, source_target_pairs={{0,1},{1,0},{2,3},{3,2},{4,5},{5,4},{6,7},{7,6},{8,9},{9,8},{10,11... | collective-permute-start | bytes 1572872 | tf_op jit(solution)/shard_map/ppermute | solution.py:327
  9.0 12.8 %collective-permute-start.2 = (bf16[4,16,4096]{2,1,0:T(8,128)(2,1)S(1)}, bf16[4,16,4096]{2,1,0:T(8,128)(2,1)S(1)}, u32[]{:S(2)}, u32[]{:S(2)}) collective-permute-start(bf16[4,16,4096]{2,1,0:T(8,128)(2,1)S(1)} %get-tuple-element.29._), channel_id=1, source_target_pairs={{0,1},{1,0},{2,3},{3,2},{4,5},{5,4},{6,7},{7,6},{8,9},{9,8},{10,11... | collective-permute-start | bytes 1572872 | tf_op jit(solution)/shard_map/ppermute | solution.py:327
  9.1 2.3 %collective-permute-start.4 = (bf16[2,16,4096]{2,1,0:T(8,128)(2,1)S(1)}, bf16[2,16,4096]{2,1,0:T(8,128)(2,1)S(1)}, u32[]{:S(2)}, u32[]{:S(2)}) collective-permute-start(bf16[2,16,4096]{2,1,0:T(8,128)(2,1)S(1)} %get-tuple-element.27._), channel_id=1, source_target_pairs={{0,1},{1,0},{2,3},{3,2},{4,5},{5,4},{6,7},{7,6},{8,9},{9,8},{10,11... | collective-permute-start | bytes 786440 | tf_op jit(solution)/shard_map/ppermute | solution.py:327
  10.9 17.4 %collective-permute-start.1 = (bf16[4,16,4096]{2,1,0:T(8,128)(2,1)S(1)}, bf16[4,16,4096]{2,1,0:T(8,128)(2,1)S(1)}, u32[]{:S(2)}, u32[]{:S(2)}) collective-permute-start(bf16[4,16,4096]{2,1,0:T(8,128)(2,1)S(1)} %get-tuple-element.30._), channel_id=1, source_target_pairs={{0,1},{1,0},{2,3},{3,2},{4,5},{5,4},{6,7},{7,6},{8,9},{9,8},{10,11... | collective-permute-start | bytes 1572872 | tf_op jit(solution)/shard_map/ppermute | solution.py:327
  11.4 5.9 %collective-permute-start.5 = (bf16[16,4096]{1,0:T(8,128)(2,1)S(1)}, bf16[16,4096]{1,0:T(8,128)(2,1)S(1)}, u32[]{:S(2)}, u32[]{:S(2)}) collective-permute-start(bf16[16,4096]{1,0:T(8,128)(2,1)S(1)} %shard_map.46), channel_id=1, source_target_pairs={{0,2},{1,15},{2,4},{3,1},{4,6},{5,3},{6,8},{7,5},{8,10},{9,7},{10,... | collective-permute-start | bytes 393224 | tf_op jit(solution)/shard_map/ppermute | solution.py:324
  15.4 5.0 %collective-permute-start.8 = (bf16[16,4096]{1,0:T(8,128)(2,1)S(1)}, bf16[16,4096]{1,0:T(8,128)(2,1)S(1)}, u32[]{:S(2)}, u32[]{:S(2)}) collective-permute-start(bf16[16,4096]{1,0:T(8,128)(2,1)S(1)} %shard_map.49), channel_id=1, source_target_pairs={{0,2},{1,15},{2,4},{3,1},{4,6},{5,3},{6,8},{7,5},{8,10},{9,7},{10,... | collective-permute-start | bytes 393224 | tf_op jit(solution)/shard_map/ppermute | solution.py:324
  16.2 5.7 %collective-permute-start.12 = (bf16[16,4096]{1,0:T(8,128)(2,1)S(1)}, bf16[16,4096]{1,0:T(8,128)(2,1)S(1)}, u32[]{:S(2)}, u32[]{:S(2)}) collective-permute-start(bf16[16,4096]{1,0:T(8,128)(2,1)S(1)} %shard_map.53), channel_id=1, source_target_pairs={{0,2},{1,15},{2,4},{3,1},{4,6},{5,3},{6,8},{7,5},{8,10},{9,7},{10,... | collective-permute-start | bytes 393224 | tf_op jit(solution)/shard_map/ppermute | solution.py:324
  17.3 6.2 %collective-permute-start.14 = (bf16[16,4096]{1,0:T(8,128)(2,1)S(1)}, bf16[16,4096]{1,0:T(8,128)(2,1)S(1)}, u32[]{:S(2)}, u32[]{:S(2)}) collective-permute-start(bf16[16,4096]{1,0:T(8,128)(2,1)S(1)} %shard_map.55), channel_id=1, source_target_pairs={{0,2},{1,15},{2,4},{3,1},{4,6},{5,3},{6,8},{7,5},{8,10},{9,7},{10,... | collective-permute-start | bytes 393224 | tf_op jit(solution)/shard_map/ppermute | solution.py:324
  20.4 6.0 %collective-permute-start.6 = (bf16[16,4096]{1,0:T(8,128)(2,1)S(1)}, bf16[16,4096]{1,0:T(8,128)(2,1)S(1)}, u32[]{:S(2)}, u32[]{:S(2)}) collective-permute-start(bf16[16,4096]{1,0:T(8,128)(2,1)S(1)} %shard_map.47), channel_id=1, source_target_pairs={{0,2},{1,15},{2,4},{3,1},{4,6},{5,3},{6,8},{7,5},{8,10},{9,7},{10,... | collective-permute-start | bytes 393224 | tf_op jit(solution)/shard_map/ppermute | solution.py:324
  21.8 5.1 %collective-permute-start.9 = (bf16[16,4096]{1,0:T(8,128)(2,1)S(1)}, bf16[16,4096]{1,0:T(8,128)(2,1)S(1)}, u32[]{:S(2)}, u32[]{:S(2)}) collective-permute-start(bf16[16,4096]{1,0:T(8,128)(2,1)S(1)} %shard_map.50), channel_id=1, source_target_pairs={{0,2},{1,15},{2,4},{3,1},{4,6},{5,3},{6,8},{7,5},{8,10},{9,7},{10,... | collective-permute-start | bytes 393224 | tf_op jit(solution)/shard_map/ppermute | solution.py:324
  22.0 7.4 %collective-permute-start.13 = (bf16[16,4096]{1,0:T(8,128)(2,1)S(1)}, bf16[16,4096]{1,0:T(8,128)(2,1)S(1)}, u32[]{:S(2)}, u32[]{:S(2)}) collective-permute-start(bf16[16,4096]{1,0:T(8,128)(2,1)S(1)} %shard_map.54), channel_id=1, source_target_pairs={{0,2},{1,15},{2,4},{3,1},{4,6},{5,3},{6,8},{7,5},{8,10},{9,7},{10,... | collective-permute-start | bytes 393224 | tf_op jit(solution)/shard_map/ppermute | solution.py:324
  23.6 5.8 %collective-permute-start.15 = (bf16[16,4096]{1,0:T(8,128)(2,1)S(1)}, bf16[16,4096]{1,0:T(8,128)(2,1)S(1)}, u32[]{:S(2)}, u32[]{:S(2)}) collective-permute-start(bf16[16,4096]{1,0:T(8,128)(2,1)S(1)} %shard_map.56), channel_id=1, source_target_pairs={{0,2},{1,15},{2,4},{3,1},{4,6},{5,3},{6,8},{7,5},{8,10},{9,7},{10,... | collective-permute-start | bytes 393224 | tf_op jit(solution)/shard_map/ppermute | solution.py:324
  26.5 8.4 %collective-permute-start.7 = (bf16[16,4096]{1,0:T(8,128)(2,1)S(1)}, bf16[16,4096]{1,0:T(8,128)(2,1)S(1)}, u32[]{:S(2)}, u32[]{:S(2)}) collective-permute-start(bf16[16,4096]{1,0:T(8,128)(2,1)S(1)} %shard_map.48), channel_id=1, source_target_pairs={{0,2},{1,15},{2,4},{3,1},{4,6},{5,3},{6,8},{7,5},{8,10},{9,7},{10,... | collective-permute-start | bytes 393224 | tf_op jit(solution)/shard_map/ppermute | solution.py:324
  27.0 7.9 %collective-permute-start.10 = (bf16[16,4096]{1,0:T(8,128)(2,1)S(1)}, bf16[16,4096]{1,0:T(8,128)(2,1)S(1)}, u32[]{:S(2)}, u32[]{:S(2)}) collective-permute-start(bf16[16,4096]{1,0:T(8,128)(2,1)S(1)} %shard_map.51), channel_id=1, source_target_pairs={{0,2},{1,15},{2,4},{3,1},{4,6},{5,3},{6,8},{7,5},{8,10},{9,7},{10,... | collective-permute-start | bytes 393224 | tf_op jit(solution)/shard_map/ppermute | solution.py:324
  28.4 10.3 %collective-permute-start = (bf16[4,8,4096]{2,1,0:T(8,128)(2,1)S(1)}, bf16[4,8,4096]{2,1,0:T(8,128)(2,1)S(1)}, u32[]{:S(2)}, u32[]{:S(2)}) collective-permute-start(bf16[4,8,4096]{2,1,0:T(8,128)(2,1)S(1)} %get-tuple-element.33), channel_id=1, source_target_pairs={{0,1},{1,0},{2,3},{3,2},{4,5},{5,4},{6,7},{7,6},{8,9},{9,8},{10,11... | collective-permute-start | bytes 786440 | tf_op jit(solution)/shard_map/ppermute | solution.py:327
  29.5 9.1 %collective-permute-start.16 = (bf16[2,8,4096]{2,1,0:T(8,128)(2,1)S(1)}, bf16[2,8,4096]{2,1,0:T(8,128)(2,1)S(1)}, u32[]{:S(2)}, u32[]{:S(2)}) collective-permute-start(bf16[2,8,4096]{2,1,0:T(8,128)(2,1)S(1)} %get-tuple-element.39), channel_id=1, source_target_pairs={{0,2},{1,15},{2,4},{3,1},{4,6},{5,3},{6,8},{7,5},{8,10},{9,7},{10,... | collective-permute-start | bytes 393224 | tf_op jit(solution)/shard_map/ppermute | solution.py:324
  31.4 7.6 %collective-permute-start.18 = (bf16[2,8,4096]{2,1,0:T(8,128)(2,1)S(1)}, bf16[2,8,4096]{2,1,0:T(8,128)(2,1)S(1)}, u32[]{:S(2)}, u32[]{:S(2)}) collective-permute-start(bf16[2,8,4096]{2,1,0:T(8,128)(2,1)S(1)} %get-tuple-element.41), channel_id=1, source_target_pairs={{0,3},{1,14},{2,5},{3,0},{4,7},{5,2},{6,9},{7,4},{8,11},{9,6},{10,... | collective-permute-start | bytes 393224 | tf_op jit(solution)/shard_map/ppermute | solution.py:324
  35.0 3.9 %collective-permute-start.11 = (bf16[2,8,4096]{2,1,0:T(8,128)(2,1)S(1)}, bf16[2,8,4096]{2,1,0:T(8,128)(2,1)S(1)}, u32[]{:S(2)}, u32[]{:S(2)}) collective-permute-start(bf16[2,8,4096]{2,1,0:T(8,128)(2,1)S(1)} %get-tuple-element.38), channel_id=1, source_target_pairs={{0,2},{1,15},{2,4},{3,1},{4,6},{5,3},{6,8},{7,5},{8,10},{9,7},{10,... | collective-permute-start | bytes 393224 | tf_op jit(solution)/shard_map/ppermute | solution.py:324
  35.1 7.5 %collective-permute-start.17 = (bf16[2,8,4096]{2,1,0:T(8,128)(2,1)S(1)}, bf16[2,8,4096]{2,1,0:T(8,128)(2,1)S(1)}, u32[]{:S(2)}, u32[]{:S(2)}) collective-permute-start(bf16[2,8,4096]{2,1,0:T(8,128)(2,1)S(1)} %get-tuple-element.40), channel_id=1, source_target_pairs={{0,3},{1,14},{2,5},{3,0},{4,7},{5,2},{6,9},{7,4},{8,11},{9,6},{10,... | collective-permute-start | bytes 393224 | tf_op jit(solution)/shard_map/ppermute | solution.py:324
  43.1 1.8 %collective-permute-start.19 = (bf16[2,8,4096]{2,1,0:T(8,128)(2,1)S(1)}, bf16[2,8,4096]{2,1,0:T(8,128)(2,1)S(1)}, u32[]{:S(2)}, u32[]{:S(2)}) collective-permute-start(bf16[2,8,4096]{2,1,0:T(8,128)(2,1)S(1)} %get-tuple-element.43.refs_1_), channel_id=1, source_target_pairs={{0,1},{1,0},{2,3},{3,2},{4,5},{5,4},{6,7},{7,6},{8,9},{9,8},{10,11... | collective-permute-start | bytes 393224 | tf_op jit(solution)/shard_map/ppermute | solution.py:327
  43.2 5.8 %collective-permute-start.21 = (bf16[2,8,4096]{2,1,0:T(8,128)(2,1)S(1)}, bf16[2,8,4096]{2,1,0:T(8,128)(2,1)S(1)}, u32[]{:S(2)}, u32[]{:S(2)}) collective-permute-start(bf16[2,8,4096]{2,1,0:T(8,128)(2,1)S(1)} %get-tuple-element.42.refs_0_), channel_id=1, source_target_pairs={{0,2},{1,15},{2,4},{3,1},{4,6},{5,3},{6,8},{7,5},{8,10},{9,7},{10,... | collective-permute-start | bytes 393224 | tf_op jit(solution)/shard_map/ppermute | solution.py:324
  44.8 5.0 %collective-permute-start.23 = (bf16[2,8,4096]{2,1,0:T(8,128)(2,1)S(1)}, bf16[2,8,4096]{2,1,0:T(8,128)(2,1)S(1)}, u32[]{:S(2)}, u32[]{:S(2)}) collective-permute-start(bf16[2,8,4096]{2,1,0:T(8,128)(2,1)S(1)} %collective-permute-done.19.refs_1_.refs_2_), channel_id=1, source_target_pairs={{0,2},{1,15},{2,4},{3,1},{4,6},{5,3},{6,8},{7,5},{8,10},{9,7},{10,... | collective-permute-start | bytes 393224 | tf_op jit(solution)/shard_map/ppermute | solution.py:324
  45.8 5.4 %collective-permute-start.20 = (bf16[2,8,4096]{2,1,0:T(8,128)(2,1)S(1)}, bf16[2,8,4096]{2,1,0:T(8,128)(2,1)S(1)}, u32[]{:S(2)}, u32[]{:S(2)}) collective-permute-start(bf16[2,8,4096]{2,1,0:T(8,128)(2,1)S(1)} %get-tuple-element.42.refs_0_), channel_id=1, source_target_pairs={{0,1},{1,0},{2,3},{3,2},{4,5},{5,4},{6,7},{7,6},{8,9},{9,8},{10,11... | collective-permute-start | bytes 393224 | tf_op jit(solution)/shard_map/ppermute | solution.py:327
  45.8 11.3 %collective-permute-start.28 = (bf16[4,8,4096]{2,1,0:T(8,128)(2,1)S(1)}, bf16[4,8,4096]{2,1,0:T(8,128)(2,1)S(1)}, u32[]{:S(2)}, u32[]{:S(2)}) collective-permute-start(bf16[4,8,4096]{2,1,0:T(8,128)(2,1)S(1)} %shard_map.59), channel_id=1, source_target_pairs={{0,16},{16,32},{32,48},{48,64},{64,80},{80,96},{96,112},{112,128},... | collective-permute-start | bytes 786440 | tf_op jit(solution)/shard_map/ppermute | solution.py:349
  47.2 4.1 %collective-permute-start.22 = (bf16[2,8,4096]{2,1,0:T(8,128)(2,1)S(1)}, bf16[2,8,4096]{2,1,0:T(8,128)(2,1)S(1)}, u32[]{:S(2)}, u32[]{:S(2)}) collective-permute-start(bf16[2,8,4096]{2,1,0:T(8,128)(2,1)S(1)} %get-tuple-element.43.refs_1_), channel_id=1, source_target_pairs={{0,2},{1,15},{2,4},{3,1},{4,6},{5,3},{6,8},{7,5},{8,10},{9,7},{10,... | collective-permute-start | bytes 393224 | tf_op jit(solution)/shard_map/ppermute | solution.py:324
  49.0 5.3 %collective-permute-start.25 = (bf16[2,8,4096]{2,1,0:T(8,128)(2,1)S(1)}, bf16[2,8,4096]{2,1,0:T(8,128)(2,1)S(1)}, u32[]{:S(2)}, u32[]{:S(2)}) collective-permute-start(bf16[2,8,4096]{2,1,0:T(8,128)(2,1)S(1)} %collective-permute-done.21.refs_4_.refs_0_), channel_id=1, source_target_pairs={{0,2},{1,15},{2,4},{3,1},{4,6},{5,3},{6,8},{7,5},{8,10},{9,7},{10,... | collective-permute-start | bytes 393224 | tf_op jit(solution)/shard_map/ppermute | solution.py:324
  49.9 5.9 %collective-permute-start.27 = (bf16[2,8,4096]{2,1,0:T(8,128)(2,1)S(1)}, bf16[2,8,4096]{2,1,0:T(8,128)(2,1)S(1)}, u32[]{:S(2)}, u32[]{:S(2)}) collective-permute-start(bf16[2,8,4096]{2,1,0:T(8,128)(2,1)S(1)} %collective-permute-done.23.refs_6_.refs_2_), channel_id=1, source_target_pairs={{0,2},{1,15},{2,4},{3,1},{4,6},{5,3},{6,8},{7,5},{8,10},{9,7},{10,... | collective-permute-start | bytes 393224 | tf_op jit(solution)/shard_map/ppermute | solution.py:324
  51.3 5.9 %collective-permute-start.24 = (bf16[2,8,4096]{2,1,0:T(8,128)(2,1)S(1)}, bf16[2,8,4096]{2,1,0:T(8,128)(2,1)S(1)}, u32[]{:S(2)}, u32[]{:S(2)}) collective-permute-start(bf16[2,8,4096]{2,1,0:T(8,128)(2,1)S(1)} %collective-permute-done.20.refs_3_), channel_id=1, source_target_pairs={{0,2},{1,15},{2,4},{3,1},{4,6},{5,3},{6,8},{7,5},{8,10},{9,7},{10,... | collective-permute-start | bytes 393224 | tf_op jit(solution)/shard_map/ppermute | solution.py:324
  51.3 8.0 %collective-permute-start.26 = (bf16[2,8,4096]{2,1,0:T(8,128)(2,1)S(1)}, bf16[2,8,4096]{2,1,0:T(8,128)(2,1)S(1)}, u32[]{:S(2)}, u32[]{:S(2)}) collective-permute-start(bf16[2,8,4096]{2,1,0:T(8,128)(2,1)S(1)} %collective-permute-done.22.refs_5_.refs_1_), channel_id=1, source_target_pairs={{0,2},{1,15},{2,4},{3,1},{4,6},{5,3},{6,8},{7,5},{8,10},{9,7},{10,... | collective-permute-start | bytes 393224 | tf_op jit(solution)/shard_map/ppermute | solution.py:324
  54.3 5.7 %collective-permute-start.30 = (bf16[2,8,4096]{2,1,0:T(8,128)(2,1)S(1)}, bf16[2,8,4096]{2,1,0:T(8,128)(2,1)S(1)}, u32[]{:S(2)}, u32[]{:S(2)}) collective-permute-start(bf16[2,8,4096]{2,1,0:T(8,128)(2,1)S(1)} %collective-permute-done.25.refs_8_.refs_4_), channel_id=1, source_target_pairs={{0,2},{1,15},{2,4},{3,1},{4,6},{5,3},{6,8},{7,5},{8,10},{9,7},{10,... | collective-permute-start | bytes 393224 | tf_op jit(solution)/shard_map/ppermute | solution.py:324
  55.7 5.3 %collective-permute-start.32 = (bf16[2,8,4096]{2,1,0:T(8,128)(2,1)S(1)}, bf16[2,8,4096]{2,1,0:T(8,128)(2,1)S(1)}, u32[]{:S(2)}, u32[]{:S(2)}) collective-permute-start(bf16[2,8,4096]{2,1,0:T(8,128)(2,1)S(1)} %collective-permute-done.27.refs_10_.refs_6_), channel_id=1, source_target_pairs={{0,2},{1,15},{2,4},{3,1},{4,6},{5,3},{6,8},{7,5},{8,10},{9,7},{10,... | collective-permute-start | bytes 393224 | tf_op jit(solution)/shard_map/ppermute | solution.py:324
  57.2 5.3 %collective-permute-start.29 = (bf16[2,8,4096]{2,1,0:T(8,128)(2,1)S(1)}, bf16[2,8,4096]{2,1,0:T(8,128)(2,1)S(1)}, u32[]{:S(2)}, u32[]{:S(2)}) collective-permute-start(bf16[2,8,4096]{2,1,0:T(8,128)(2,1)S(1)} %shard_map.60), channel_id=1, source_target_pairs={{0,2},{1,15},{2,4},{3,1},{4,6},{5,3},{6,8},{7,5},{8,10},{9,7},{10,... | collective-permute-start | bytes 393224 | tf_op jit(solution)/shard_map/ppermute | solution.py:324
  59.3 5.0 %collective-permute-start.31 = (bf16[2,8,4096]{2,1,0:T(8,128)(2,1)S(1)}, bf16[2,8,4096]{2,1,0:T(8,128)(2,1)S(1)}, u32[]{:S(2)}, u32[]{:S(2)}) collective-permute-start(bf16[2,8,4096]{2,1,0:T(8,128)(2,1)S(1)} %collective-permute-done.26.refs_9_.refs_5_), channel_id=1, source_target_pairs={{0,2},{1,15},{2,4},{3,1},{4,6},{5,3},{6,8},{7,5},{8,10},{9,7},{10,... | collective-permute-start | bytes 393224 | tf_op jit(solution)/shard_map/ppermute | solution.py:324
  60.1 4.7 %collective-permute-start.34 = (bf16[2,8,4096]{2,1,0:T(8,128)(2,1)S(1)}, bf16[2,8,4096]{2,1,0:T(8,128)(2,1)S(1)}, u32[]{:S(2)}, u32[]{:S(2)}) collective-permute-start(bf16[2,8,4096]{2,1,0:T(8,128)(2,1)S(1)} %collective-permute-done.30.refs_12_.refs_8_), channel_id=1, source_target_pairs={{0,2},{1,15},{2,4},{3,1},{4,6},{5,3},{6,8},{7,5},{8,10},{9,7},{10,... | collective-permute-start | bytes 393224 | tf_op jit(solution)/shard_map/ppermute | solution.py:324
  61.1 5.1 %collective-permute-start.35 = (bf16[2,8,4096]{2,1,0:T(8,128)(2,1)S(1)}, bf16[2,8,4096]{2,1,0:T(8,128)(2,1)S(1)}, u32[]{:S(2)}, u32[]{:S(2)}) collective-permute-start(bf16[2,8,4096]{2,1,0:T(8,128)(2,1)S(1)} %collective-permute-done.32.refs_14_.refs_10_), channel_id=1, source_target_pairs={{0,2},{1,15},{2,4},{3,1},{4,6},{5,3},{6,8},{7,5},{8,10},{9,7},{10,... | collective-permute-start | bytes 393224 | tf_op jit(solution)/shard_map/ppermute | solution.py:324
  62.5 5.1 %collective-permute-start.33 = (bf16[2,8,4096]{2,1,0:T(8,128)(2,1)S(1)}, bf16[2,8,4096]{2,1,0:T(8,128)(2,1)S(1)}, u32[]{:S(2)}, u32[]{:S(2)}) collective-permute-start(bf16[2,8,4096]{2,1,0:T(8,128)(2,1)S(1)} %collective-permute-done.29.refs_11_.refs_7_), channel_id=1, source_target_pairs={{0,2},{1,15},{2,4},{3,1},{4,6},{5,3},{6,8},{7,5},{8,10},{9,7},{10,... | collective-permute-start | bytes 393224 | tf_op jit(solution)/shard_map/ppermute | solution.py:324
  67.7 7.2 %collective-permute-start.36 = (bf16[28,8,4096]{2,1,0:T(8,128)(2,1)S(1)}, bf16[28,8,4096]{2,1,0:T(8,128)(2,1)S(1)}, u32[]{:S(2)}, u32[]{:S(2)}) collective-permute-start(bf16[28,8,4096]{2,1,0:T(8,128)(2,1)S(1)} %shard_map.62), channel_id=1, source_target_pairs={{0,1},{1,0},{2,3},{3,2},{4,5},{5,4},{6,7},{7,6},{8,9},{9,8},{10,11... | collective-permute-start | bytes 5505032 | tf_op jit(solution)/shard_map/ppermute | solution.py:327

commit v2 on v1

--- a/solution.py
+++ b/solution.py
@@ -214,7 +214,7 @@
     )(keep, got, *arrived)
 
 
-def norm_kernel(near, rows, got, same0, same1, cross0, cross1, hidden_ref, out0, out1):
+def norm_kernel(near, rows, got, same0, same1, cross0, cross1, hidden_ref, whole, out0, out1):
     sames, crosses = (same0, same1), (cross1, cross0)
     f32 = jnp.float32
     squares = jnp.zeros((OWN, COLS), f32)
@@ -233,19 +233,38 @@
     for half, out in enumerate((out0, out1)):
         for j in range(PIECES):
             hidden = hidden_ref[half * PIECES + j].astype(f32)
-            out[j] = (hidden * inv_rms).astype(jnp.bfloat16)
+            normed = (hidden * inv_rms).astype(jnp.bfloat16)
+            out[j] = normed
+            whole[half * PIECES + j] = normed
 
 
 def norm(*blocks):
     part = jax.ShapeDtypeStruct((PIECES, OWN, COLS), jnp.bfloat16)
     return pl.pallas_call(
         norm_kernel,
-        out_shape=(jax.ShapeDtypeStruct((2 * PIECES, OWN, COLS), jnp.bfloat16), part, part),
+        out_shape=(jax.ShapeDtypeStruct((2 * PIECES, OWN, COLS), jnp.bfloat16),) * 2 + (part, part),
         in_specs=[VMEM] * len(blocks),
-        out_specs=(VMEM,) * 3,
+        out_specs=(VMEM,) * 4,
         compiler_params=GRANT,
         cost_estimate=SMALL,
     )(*blocks)
+
+
+def split_kernel(block, low, high):
+    low[...] = block[:PIECES]
+    high[...] = block[PIECES:]
+
+
+def split(block):
+    part = jax.ShapeDtypeStruct((PIECES, OWN, COLS), jnp.bfloat16)
+    return pl.pallas_call(
+        split_kernel,
+        out_shape=(part, part),
+        in_specs=[VMEM],
+        out_specs=(VMEM, VMEM),
+        compiler_params=GRANT,
+        cost_estimate=SMALL,
+    )(block)
 
 
 def join_kernel(count, *refs):
@@ -293,7 +312,7 @@
         copy.wait()
 
 
-def put(out, blocks, places):
+def put(out, blocks, places, after):
     copies = PIECES * sum(len(p) for p in places)
     held = [] if out is None else [pltpu.with_memory_space_constraint(out, pltpu.HBM)]
     whole = pltpu.HBM((2 * CHIPS, OWN, D), jnp.bfloat16)
@@ -303,15 +322,15 @@
     outs = [rows, done, whole] if with_rows else [done, whole]
     space = pl.BlockSpec(memory_space=pltpu.HBM)
     return pl.pallas_call(
-        lambda *refs: put_kernel(places, len(held), *refs),
+        lambda *refs: put_kernel(places, len(held) + len(after), *refs),
         out_shape=outs,
-        in_specs=[space] * len(held) + [VMEM] * len(blocks),
+        in_specs=[space] * len(held) + [ANY] * len(after) + [VMEM] * len(blocks),
         out_specs=[space] * (len(outs) - 2) + [VMEM, space],
         scratch_shapes=[pltpu.SemaphoreType.DMA((copies,))],
         input_output_aliases={0: len(outs) - 1} if held else {},
         compiler_params=GRANT,
         cost_estimate=SMALL,
-    )(*held, *blocks)
+    )(*held, *after, *blocks)
 
 
 def shards(partials, residual):
@@ -330,9 +349,11 @@
     keep, send, held, rows = code_far(local, stream)
     for k in range(FAR, 1, -1):
         got = other_core(send)
-        sums = [add(i, keep, got, moving[i]) for i in range(keep.shape[0])]
+        order = [i for i in (0, 1, 2, 3) if i < keep.shape[0]]
+        sums = {i: add(i, keep, got, moving[i]) for i in order}
         keep, send = code_rows(held, k - 1, send)
-        moving = [onward(block) for block in sums] + moving[len(sums) :]
+        for i in order:
+            moving[i] = onward(sums[i])
     got = other_core(send)
     near, send, rows = own_rows(held, rows, send)
     same, cross = [], []
@@ -341,36 +362,49 @@
         mine, theirs = last_add(half, keep, got, moving[span])
         same.append(onward(mine))
         cross.append(onward(theirs, True))
-    hidden, *normed = norm(near, rows, other_core(send), *same, *cross)
+    hidden, whole, *normed = norm(near, rows, other_core(send), *same, *cross)
 
     sections = lax.axis_size("section")
-    theirs = [other_core(normed[1]), other_core(normed[0])]
-    hidden = join([hidden], theirs[:1])
-    incoming = lax.ppermute(hidden, "section", [(i, (i + 1) % sections) for i in range(sections)])
+    theirs = list(split(other_core(whole)))[::-1]
 
     moving = normed + theirs
     blocks = list(moving)
     places = [[(0, rows, half)] for rows in (0, 1) for half in (0, 1)]
-    out = None
     joined, joined_places = [], []
     for k in range(1, FAR + 1):
-        kept = [(rows, half) for rows in (0, 1) for half in (0, 1) if half == 0 or k < FAR]
+        kept = [(rows, half) for rows, half in [(0, 0), (0, 1), (1, 0), (1, 1)] if half == 0 or k < FAR]
         ready = [moving[2 * rows + half] for rows, half in kept]
-        if k == 2:
+        if k == FAR:
             ready[-1] = join(ready[-1:], [incoming])
-        moving = [onward(block) for block in ready]
-        blocks += moving
-        places += [[(-k, rows, half)] for rows, half in kept]
-        if k == FAR - 1:
-            blocks.append(incoming)
-            places.append([(None, 0, 0), (None, 0, 1)])
-            incoming, _, out = put(out, blocks, places)
-            blocks, places = [], []
-        joined += moving
+        for (rows, half), block in zip(kept, ready):
+            moving[2 * rows + half] = onward(block)
+        arrived = [moving[2 * rows + half] for rows, half in kept]
+        if k == 1:
+            hidden = join([hidden], arrived[2:3])
+            incoming = lax.ppermute(
+                hidden, "section", [(i, (i + 1) % sections) for i in range(sections)]
+            )
+        if k == FAR:
+            swapped = other_core(join(joined[:8], []))
+            swapped_places, joined, joined_places = joined_places[:8], joined[8:], joined_places[8:]
+            early = put(None, blocks, places, arrived[:1])
+            blocks, places = late, late_places
+        joined += arrived
         joined_places += [(k, 1 - rows, 1 - half) for rows, half in kept]
-    blocks.append(other_core(join(joined, [])))
-    places.append(joined_places)
-    _, out = put(out, blocks, places)
+        if k < FAR - 1:
+            blocks += arrived
+            places += [[(-k, rows, half)] for rows, half in kept]
+            if k == 1:
+                blocks.append(incoming)
+                places.append([(None, 0, 0), (None, 0, 1)])
+            late, late_places = [], []
+        else:
+            late += arrived
+            late_places += [[(-k, rows, half)] for rows, half in kept]
+    incoming, token, out = early
+    last = other_core(join(joined, [token]))
+    _, out = put(out, blocks + [swapped], places + [swapped_places], [])
+    _, out = put(out, [last], [joined_places], [])
     return (out.reshape(1, 2 * CHIPS * OWN, D), incoming)
 
 

time: 77.3 us -> 76.7 us (level)
  starting transfers between devices: 54.3 us -> 52.9 us
    ppermute x28, starting transfers between devices: 43.9 us -> 40.3 us  [onward(): lax.ppermute(block, 'tp', [(i, j ^ 1) if cross else (i, j) for i, j in ro...]
    ppermute x8, starting transfers between devices: 9.01 us -> 11.2 us  [other_core(): return lax.ppermute(block, 'tp', [(i, i ^ 1) for i in range(n)])]
    ppermute x8, waiting for transfers between devices: 1.44 us -> 0.31 us  [other_core(): return lax.ppermute(block, 'tp', [(i, i ^ 1) for i in range(n)])]
    pallas_call x2 -> x4, Pallas kernels: 4.43 us -> 5.08 us  [the longest x3 5.06 us: put(): pl.pallas_call(lambda *refs: put_kernel(places, len(held) + len(after), *...]
  transfers between devices with their start and end apart: 37 -> 37, of which waited for: 8 -> 9; matrix products, arithmetic and copies ran while one was open for 0% -> 0% of each run, Pallas kernels for 8% -> 10%
where the time goes in v2:
time: 76.7 us; the launch traced here: 76.6 us
  starting transfers between devices  52.9 us (69%)
  Pallas kernels  13.5 us (18%)
  waiting for transfers between devices  9.11 us (12%)
  between operations  1.05 us (1%)
    ppermute x28, starting transfers between devices, onward(): lax.ppermute(block, 'tp', [(i, j ^ 1) if cross else (i, j) for i, j in ro...  40.3 us
    ppermute x8, starting transfers between devices, other_core(): return lax.ppermute(block, 'tp', [(i, i ^ 1) for i in range(n)])  11.2 us
    ppermute x28, waiting for transfers between devices, onward(): lax.ppermute(block, 'tp', [(i, j ^ 1) if cross else (i, j) for i, j in ro...  8.15 us
    pallas_call x3, Pallas kernels, put(): pl.pallas_call(lambda *refs: put_kernel(places, len(held) + len(after), *...  5.06 us
    pallas_call x3, Pallas kernels, code_rows(): pl.pallas_call(lambda held_ref, _, *refs: code_kernel(k, held_ref, *refs)...  3.85 us
    pallas_call x1, Pallas kernels, code_far(): pl.pallas_call(far_kernel, out_shape=(part, part, whole, rows), in_specs=...  2.47 us
  transfers between devices with their start and end apart: 37, of which 9 were waited for; matrix products, arithmetic and copies ran while one was open for 0% of the time, Pallas kernels for 10%

profile of v2, /device:TPU:1, one launch (start us, length us, event | category | flops | bytes accessed | tf_op | source)
XLA Modules:
  0.0 76.6 jit_solution(7265388624856663421)
XLA Ops:
  0.6 2.5 %shard_map.41 = (bf16[2,16,4096]{2,1,0:T(8,128)(2,1)S(1)}, bf16[2,16,4096]{2,1,0:T(8,128)(2,1)S(1)}, bf16[16,16,8192]{2,1,0:T(8,128)(2,1)S(1)}, bf16[2,16,8192]{2,1,0:T(8,128)(2,1)S(1)}) custom-call(bf16[128,16384]{1,0:T(8,128)(2,1)} %bitcast.4, bf16[128,16384]{1,0:T(8,128)(2,1)} %bitcast.5), custom_call_target="tpu_custom_call" | custom-call | flops 1 | bytes 1 | tf_op jit(solution)/shard_map/pallas_call | solution.py:113
  3.1 1.3 %shard_map.42 = (bf16[4,16,4096]{2,1,0:T(8,128)(2,1)S(1)}, bf16[4,16,4096]{2,1,0:T(8,128)(2,1)S(1)}) custom-call(bf16[16,16,8192]{2,1,0:T(8,128)(2,1)S(1)} %get-tuple-element.30.held_ref, bf16[2,16,4096]{2,1,0:T(8,128)(2,1)S(1)} %get-tuple-element.32._), custom_call_target="tpu_custom_call" | custom-call | flops 1 | bytes 1 | tf_op jit(solution)/shard_map/pallas_call | solution.py:132
  4.4 3.3 %collective-permute-start.3 = (bf16[4,16,4096]{2,1,0:T(8,128)(2,1)S(1)}, bf16[4,16,4096]{2,1,0:T(8,128)(2,1)S(1)}, u32[]{:S(2)}, u32[]{:S(2)}) collective-permute-start(bf16[4,16,4096]{2,1,0:T(8,128)(2,1)S(1)} %get-tuple-element.33._), channel_id=1, source_target_pairs={{0,1},{1,0},{2,3},{3,2},{4,5},{5,4},{6,7},{7,6},{8,9},{9,8},{10,11... | collective-permute-start | bytes 1572872 | tf_op jit(solution)/shard_map/ppermute | solution.py:346
  7.7 1.3 %shard_map.43 = (bf16[4,16,4096]{2,1,0:T(8,128)(2,1)S(1)}, bf16[4,16,4096]{2,1,0:T(8,128)(2,1)S(1)}) custom-call(bf16[16,16,8192]{2,1,0:T(8,128)(2,1)S(1)} %get-tuple-element.30.held_ref, bf16[4,16,4096]{2,1,0:T(8,128)(2,1)S(1)} %get-tuple-element.33._), custom_call_target="tpu_custom_call" | custom-call | flops 1 | bytes 1 | tf_op jit(solution)/shard_map/pallas_call | solution.py:132
  9.1 0.5 collective-permute-start.4
  9.6 1.3 %shard_map.44 = (bf16[4,16,4096]{2,1,0:T(8,128)(2,1)S(1)}, bf16[4,16,4096]{2,1,0:T(8,128)(2,1)S(1)}) custom-call(bf16[16,16,8192]{2,1,0:T(8,128)(2,1)S(1)} %get-tuple-element.30.held_ref, bf16[4,16,4096]{2,1,0:T(8,128)(2,1)S(1)} %get-tuple-element.34._), custom_call_target="tpu_custom_call" | custom-call | flops 1 | bytes 1 | tf_op jit(solution)/shard_map/pallas_call | solution.py:132
  10.9 0.2 collective-permute-start.1
  11.1 0.3 collective-permute-done.4.refs_1_
  11.4 3.9 %collective-permute-start.5 = (bf16[16,4096]{1,0:T(8,128)(2,1)S(1)}, bf16[16,4096]{1,0:T(8,128)(2,1)S(1)}, u32[]{:S(2)}, u32[]{:S(2)}) collective-permute-start(bf16[16,4096]{1,0:T(8,128)(2,1)S(1)} %shard_map.46), channel_id=1, source_target_pairs={{0,2},{1,15},{2,4},{3,1},{4,6},{5,3},{6,8},{7,5},{8,10},{9,7},{10,... | collective-permute-start | bytes 393224 | tf_op jit(solution)/shard_map/ppermute | solution.py:343
  15.4 0.8 %collective-permute-start.8 = (bf16[16,4096]{1,0:T(8,128)(2,1)S(1)}, bf16[16,4096]{1,0:T(8,128)(2,1)S(1)}, u32[]{:S(2)}, u32[]{:S(2)}) collective-permute-start(bf16[16,4096]{1,0:T(8,128)(2,1)S(1)} %shard_map.49), channel_id=1, source_target_pairs={{0,2},{1,15},{2,4},{3,1},{4,6},{5,3},{6,8},{7,5},{8,10},{9,7},{10,... | collective-permute-start | bytes 393224 | tf_op jit(solution)/shard_map/ppermute | solution.py:343
  16.2 0.8 %collective-permute-start.12 = (bf16[16,4096]{1,0:T(8,128)(2,1)S(1)}, bf16[16,4096]{1,0:T(8,128)(2,1)S(1)}, u32[]{:S(2)}, u32[]{:S(2)}) collective-permute-start(bf16[16,4096]{1,0:T(8,128)(2,1)S(1)} %shard_map.53), channel_id=1, source_target_pairs={{0,2},{1,15},{2,4},{3,1},{4,6},{5,3},{6,8},{7,5},{8,10},{9,7},{10,... | collective-permute-start | bytes 393224 | tf_op jit(solution)/shard_map/ppermute | solution.py:343
  17.1 0.2 collective-permute-done.5.refs_2_
  17.3 3.1 %collective-permute-start.14 = (bf16[16,4096]{1,0:T(8,128)(2,1)S(1)}, bf16[16,4096]{1,0:T(8,128)(2,1)S(1)}, u32[]{:S(2)}, u32[]{:S(2)}) collective-permute-start(bf16[16,4096]{1,0:T(8,128)(2,1)S(1)} %shard_map.55), channel_id=1, source_target_pairs={{0,2},{1,15},{2,4},{3,1},{4,6},{5,3},{6,8},{7,5},{8,10},{9,7},{10,... | collective-permute-start | bytes 393224 | tf_op jit(solution)/shard_map/ppermute | solution.py:343
  20.4 1.3 %collective-permute-start.6 = (bf16[16,4096]{1,0:T(8,128)(2,1)S(1)}, bf16[16,4096]{1,0:T(8,128)(2,1)S(1)}, u32[]{:S(2)}, u32[]{:S(2)}) collective-permute-start(bf16[16,4096]{1,0:T(8,128)(2,1)S(1)} %shard_map.47), channel_id=1, source_target_pairs={{0,2},{1,15},{2,4},{3,1},{4,6},{5,3},{6,8},{7,5},{8,10},{9,7},{10,... | collective-permute-start | bytes 393224 | tf_op jit(solution)/shard_map/ppermute | solution.py:343
  22.0 1.5 %collective-permute-start.13 = (bf16[16,4096]{1,0:T(8,128)(2,1)S(1)}, bf16[16,4096]{1,0:T(8,128)(2,1)S(1)}, u32[]{:S(2)}, u32[]{:S(2)}) collective-permute-start(bf16[16,4096]{1,0:T(8,128)(2,1)S(1)} %shard_map.54), channel_id=1, source_target_pairs={{0,2},{1,15},{2,4},{3,1},{4,6},{5,3},{6,8},{7,5},{8,10},{9,7},{10,... | collective-permute-start | bytes 393224 | tf_op jit(solution)/shard_map/ppermute | solution.py:343
  23.6 2.0 %collective-permute-start.15 = (bf16[16,4096]{1,0:T(8,128)(2,1)S(1)}, bf16[16,4096]{1,0:T(8,128)(2,1)S(1)}, u32[]{:S(2)}, u32[]{:S(2)}) collective-permute-start(bf16[16,4096]{1,0:T(8,128)(2,1)S(1)} %shard_map.56), channel_id=1, source_target_pairs={{0,2},{1,15},{2,4},{3,1},{4,6},{5,3},{6,8},{7,5},{8,10},{9,7},{10,... | collective-permute-start | bytes 393224 | tf_op jit(solution)/shard_map/ppermute | solution.py:343
  25.5 0.9 %shard_map.45 = (bf16[4,8,4096]{2,1,0:T(8,128)(2,1)S(1)}, bf16[4,8,4096]{2,1,0:T(8,128)(2,1)S(1)}, bf16[4,8,4096]{2,1,0:T(8,128)(2,1)S(1)}) custom-call(bf16[16,16,8192]{2,1,0:T(8,128)(2,1)S(1)} %get-tuple-element.30.held_ref, bf16[2,16,8192]{2,1,0:T(8,128)(2,1)S(1)} %get-tuple-element.31.stream_ref, bf16[4,16,4096]{2,1,0:T(8,128)(2,1)S(1)} %get-tuple-element.35._), custom_call_target="tpu_custom_call" | custom-call | flops 1 | bytes 1 | tf_op jit(solution)/shard_map/pallas_call | solution.py:163
  26.5 0.5 collective-permute-start.7
  27.0 1.3 %collective-permute-start.10 = (bf16[16,4096]{1,0:T(8,128)(2,1)S(1)}, bf16[16,4096]{1,0:T(8,128)(2,1)S(1)}, u32[]{:S(2)}, u32[]{:S(2)}) collective-permute-start(bf16[16,4096]{1,0:T(8,128)(2,1)S(1)} %shard_map.51), channel_id=1, source_target_pairs={{0,2},{1,15},{2,4},{3,1},{4,6},{5,3},{6,8},{7,5},{8,10},{9,7},{10,... | collective-permute-start | bytes 393224 | tf_op jit(solution)/shard_map/ppermute | solution.py:343
  28.4 1.0 %collective-permute-start = (bf16[4,8,4096]{2,1,0:T(8,128)(2,1)S(1)}, bf16[4,8,4096]{2,1,0:T(8,128)(2,1)S(1)}, u32[]{:S(2)}, u32[]{:S(2)}) collective-permute-start(bf16[4,8,4096]{2,1,0:T(8,128)(2,1)S(1)} %get-tuple-element.38), channel_id=1, source_target_pairs={{0,1},{1,0},{2,3},{3,2},{4,5},{5,4},{6,7},{7,6},{8,9},{9,8},{10,11... | collective-permute-start | bytes 786440 | tf_op jit(solution)/shard_map/ppermute | solution.py:346
  29.5 1.9 %collective-permute-start.16 = (bf16[2,8,4096]{2,1,0:T(8,128)(2,1)S(1)}, bf16[2,8,4096]{2,1,0:T(8,128)(2,1)S(1)}, u32[]{:S(2)}, u32[]{:S(2)}) collective-permute-start(bf16[2,8,4096]{2,1,0:T(8,128)(2,1)S(1)} %get-tuple-element.44), channel_id=1, source_target_pairs={{0,2},{1,15},{2,4},{3,1},{4,6},{5,3},{6,8},{7,5},{8,10},{9,7},{10,... | collective-permute-start | bytes 393224 | tf_op jit(solution)/shard_map/ppermute | solution.py:343
  31.4 3.5 %collective-permute-start.18 = (bf16[2,8,4096]{2,1,0:T(8,128)(2,1)S(1)}, bf16[2,8,4096]{2,1,0:T(8,128)(2,1)S(1)}, u32[]{:S(2)}, u32[]{:S(2)}) collective-permute-start(bf16[2,8,4096]{2,1,0:T(8,128)(2,1)S(1)} %get-tuple-element.46), channel_id=1, source_target_pairs={{0,3},{1,14},{2,5},{3,0},{4,7},{5,2},{6,9},{7,4},{8,11},{9,6},{10,... | collective-permute-start | bytes 393224 | tf_op jit(solution)/shard_map/ppermute | solution.py:343
  35.1 3.5 %collective-permute-start.17 = (bf16[2,8,4096]{2,1,0:T(8,128)(2,1)S(1)}, bf16[2,8,4096]{2,1,0:T(8,128)(2,1)S(1)}, u32[]{:S(2)}, u32[]{:S(2)}) collective-permute-start(bf16[2,8,4096]{2,1,0:T(8,128)(2,1)S(1)} %get-tuple-element.45), channel_id=1, source_target_pairs={{0,3},{1,14},{2,5},{3,0},{4,7},{5,2},{6,9},{7,4},{8,11},{9,6},{10,... | collective-permute-start | bytes 393224 | tf_op jit(solution)/shard_map/ppermute | solution.py:343
  38.6 0.4 collective-permute-done.18.cross1
  39.0 3.7 %collective-permute-done.17.cross0 = bf16[2,8,4096]{2,1,0:T(8,128)(2,1)S(1)} collective-permute-done((bf16[2,8,4096]{2,1,0:T(8,128)(2,1)S(1)}, bf16[2,8,4096]{2,1,0:T(8,128)(2,1)S(1)}, u32[]{:S(2)}, u32[]{:S(2)}) %collective-permute-start.17) | collective-permute-done | bytes 131104 | tf_op jit(solution)/shard_map/ppermute | solution.py:343
  42.7 0.4 shard_map.58
  43.2 1.7 %collective-permute-start.19 = (bf16[2,8,4096]{2,1,0:T(8,128)(2,1)S(1)}, bf16[2,8,4096]{2,1,0:T(8,128)(2,1)S(1)}, u32[]{:S(2)}, u32[]{:S(2)}) collective-permute-start(bf16[2,8,4096]{2,1,0:T(8,128)(2,1)S(1)} %get-tuple-element.47.refs_1_), channel_id=1, source_target_pairs={{0,2},{1,15},{2,4},{3,1},{4,6},{5,3},{6,8},{7,5},{8,10},{9,7},{10,... | collective-permute-start | bytes 393224 | tf_op jit(solution)/shard_map/ppermute | solution.py:343
  44.9 1.2 %collective-permute-start.25 = (bf16[2,8,4096]{2,1,0:T(8,128)(2,1)S(1)}, bf16[2,8,4096]{2,1,0:T(8,128)(2,1)S(1)}, u32[]{:S(2)}, u32[]{:S(2)}) collective-permute-start(bf16[2,8,4096]{2,1,0:T(8,128)(2,1)S(1)} %get-tuple-element.50.refs_3_), channel_id=1, source_target_pairs={{0,2},{1,15},{2,4},{3,1},{4,6},{5,3},{6,8},{7,5},{8,10},{9,7},{10,... | collective-permute-start | bytes 393224 | tf_op jit(solution)/shard_map/ppermute | solution.py:343
  46.1 0.8 %collective-permute-start.26 = (bf16[2,8,4096]{2,1,0:T(8,128)(2,1)S(1)}, bf16[2,8,4096]{2,1,0:T(8,128)(2,1)S(1)}, u32[]{:S(2)}, u32[]{:S(2)}) collective-permute-start(bf16[2,8,4096]{2,1,0:T(8,128)(2,1)S(1)} %get-tuple-element.51.refs_4_), channel_id=1, source_target_pairs={{0,2},{1,15},{2,4},{3,1},{4,6},{5,3},{6,8},{7,5},{8,10},{9,7},{10,... | collective-permute-start | bytes 393224 | tf_op jit(solution)/shard_map/ppermute | solution.py:343
  46.9 0.1 collective-permute-done.19.refs_5_.refs_0_
  47.1 2.8 %collective-permute-start.20 = (bf16[2,8,4096]{2,1,0:T(8,128)(2,1)S(1)}, bf16[2,8,4096]{2,1,0:T(8,128)(2,1)S(1)}, u32[]{:S(2)}, u32[]{:S(2)}) collective-permute-start(bf16[2,8,4096]{2,1,0:T(8,128)(2,1)S(1)} %collective-permute-done.19.refs_5_.refs_0_), channel_id=1, source_target_pairs={{0,2},{1,15},{2,4},{3,1},{4,6},{5,3},{6,8},{7,5},{8,10},{9,7},{10,... | collective-permute-start | bytes 393224 | tf_op jit(solution)/shard_map/ppermute | solution.py:343
  49.9 1.4 %collective-permute-start.28 = (bf16[2,8,4096]{2,1,0:T(8,128)(2,1)S(1)}, bf16[2,8,4096]{2,1,0:T(8,128)(2,1)S(1)}, u32[]{:S(2)}, u32[]{:S(2)}) collective-permute-start(bf16[2,8,4096]{2,1,0:T(8,128)(2,1)S(1)} %collective-permute-done.24.refs_6_.refs_1_), channel_id=1, source_target_pairs={{0,2},{1,15},{2,4},{3,1},{4,6},{5,3},{6,8},{7,5},{8,10},{9,7},{10,... | collective-permute-start | bytes 393224 | tf_op jit(solution)/shard_map/ppermute | solution.py:343
  51.3 1.4 %collective-permute-start.29 = (bf16[2,8,4096]{2,1,0:T(8,128)(2,1)S(1)}, bf16[2,8,4096]{2,1,0:T(8,128)(2,1)S(1)}, u32[]{:S(2)}, u32[]{:S(2)}) collective-permute-start(bf16[2,8,4096]{2,1,0:T(8,128)(2,1)S(1)} %collective-permute-done.25.refs_1_.refs_7_.refs_2_), channel_id=1, source_target_pairs={{0,2},{1,15},{2,4},{3,1},{4,6},{5,3},{6,8},{7,5},{8,10},{9,7},{10,... | collective-permute-start | bytes 393224 | tf_op jit(solution)/shard_map/ppermute | solution.py:343
  52.7 1.4 %collective-permute-start.27 = (bf16[4,8,4096]{2,1,0:T(8,128)(2,1)S(1)}, bf16[4,8,4096]{2,1,0:T(8,128)(2,1)S(1)}, u32[]{:S(2)}, u32[]{:S(2)}) collective-permute-start(bf16[4,8,4096]{2,1,0:T(8,128)(2,1)S(1)} %shard_map.60), channel_id=1, source_target_pairs={{0,16},{16,32},{32,48},{48,64},{64,80},{80,96},{96,112},{112,128},... | collective-permute-start | bytes 786440 | tf_op jit(solution)/shard_map/ppermute | solution.py:384
  54.1 1.4 %collective-permute-start.21 = (bf16[2,8,4096]{2,1,0:T(8,128)(2,1)S(1)}, bf16[2,8,4096]{2,1,0:T(8,128)(2,1)S(1)}, u32[]{:S(2)}, u32[]{:S(2)}) collective-permute-start(bf16[2,8,4096]{2,1,0:T(8,128)(2,1)S(1)} %collective-permute-done.20.refs_10_.refs_4_), channel_id=1, source_target_pairs={{0,2},{1,15},{2,4},{3,1},{4,6},{5,3},{6,8},{7,5},{8,10},{9,7},{10,... | collective-permute-start | bytes 393224 | tf_op jit(solution)/shard_map/ppermute | solution.py:343
  55.5 0.5 collective-permute-done.29.refs_12_.refs_6_
  56.0 2.3 %collective-permute-start.32 = (bf16[2,8,4096]{2,1,0:T(8,128)(2,1)S(1)}, bf16[2,8,4096]{2,1,0:T(8,128)(2,1)S(1)}, u32[]{:S(2)}, u32[]{:S(2)}) collective-permute-start(bf16[2,8,4096]{2,1,0:T(8,128)(2,1)S(1)} %collective-permute-done.29.refs_12_.refs_6_), channel_id=1, source_target_pairs={{0,2},{1,15},{2,4},{3,1},{4,6},{5,3},{6,8},{7,5},{8,10},{9,7},{10,... | collective-permute-start | bytes 393224 | tf_op jit(solution)/shard_map/ppermute | solution.py:343
  58.4 2.3 %collective-permute-start.35 = (bf16[16,8,4096]{2,1,0:T(8,128)(2,1)S(1)}, bf16[16,8,4096]{2,1,0:T(8,128)(2,1)S(1)}, u32[]{:S(2)}, u32[]{:S(2)}) collective-permute-start(bf16[16,8,4096]{2,1,0:T(8,128)(2,1)S(1)} %shard_map.63), channel_id=1, source_target_pairs={{0,1},{1,0},{2,3},{3,2},{4,5},{5,4},{6,7},{7,6},{8,9},{9,8},{10,11... | collective-permute-start | bytes 3145736 | tf_op jit(solution)/shard_map/ppermute | solution.py:346
  60.7 1.7 %collective-permute-start.31 = (bf16[2,8,4096]{2,1,0:T(8,128)(2,1)S(1)}, bf16[2,8,4096]{2,1,0:T(8,128)(2,1)S(1)}, u32[]{:S(2)}, u32[]{:S(2)}) collective-permute-start(bf16[2,8,4096]{2,1,0:T(8,128)(2,1)S(1)} %collective-permute-done.28.refs_11_.refs_5_), channel_id=1, source_target_pairs={{0,2},{1,15},{2,4},{3,1},{4,6},{5,3},{6,8},{7,5},{8,10},{9,7},{10,... | collective-permute-start | bytes 393224 | tf_op jit(solution)/shard_map/ppermute | solution.py:343
  62.4 0.3 collective-permute-start.22
  62.8 0.8 %collective-permute-start.33 = (bf16[2,8,4096]{2,1,0:T(8,128)(2,1)S(1)}, bf16[2,8,4096]{2,1,0:T(8,128)(2,1)S(1)}, u32[]{:S(2)}, u32[]{:S(2)}) collective-permute-start(bf16[2,8,4096]{2,1,0:T(8,128)(2,1)S(1)} %collective-permute-done.30.refs_13_.refs_7_), channel_id=1, source_target_pairs={{0,2},{1,15},{2,4},{3,1},{4,6},{5,3},{6,8},{7,5},{8,10},{9,7},{10,... | collective-permute-start | bytes 393224 | tf_op jit(solution)/shard_map/ppermute | solution.py:343
  63.6 0.6 collective-permute-done.27.refs_9_.refs_1_
  64.4 2.2 %collective-permute-done.22.refs_0_.refs_5_.refs_4_ = bf16[2,8,4096]{2,1,0:T(8,128)(2,1)S(1)} collective-permute-done((bf16[2,8,4096]{2,1,0:T(8,128)(2,1)S(1)}, bf16[2,8,4096]{2,1,0:T(8,128)(2,1)S(1)}, u32[]{:S(2)}, u32[]{:S(2)}) %collective-permute-start.22) | collective-permute-done | bytes 131104 | tf_op jit(solution)/shard_map/ppermute | solution.py:343
  66.5 1.4 %shard_map.61 = (bf16[1,8,16384]{2,1,0:T(8,128)(2,1)}, f32[8,128]{1,0:T(8,128)S(1)}, bf16[16,8,16384]{2,1,0:T(8,128)(2,1)}) custom-call(bf16[2,8,4096]{2,1,0:T(8,128)(2,1)S(1)} %collective-permute-done.22.refs_0_.refs_5_.refs_4_, bf16[2,8,4096]{2,1,0:T(8,128)(2,1)S(1)} %get-tuple-element.47.refs_1_, bf16[2,8,4096]{2,1,0:T(8,128)(2,1)S(1)} %get-tuple-element.48.refs_2_, ...), custom_call_target="tpu_custom_call" | custom-call | flops 1 | bytes 1 | tf_op jit(solution)/shard_map/pallas_call | solution.py:324
  68.0 1.0 %collective-permute-done.34.refs_6_.refs_5_ = bf16[2,8,4096]{2,1,0:T(8,128)(2,1)S(1)} collective-permute-done((bf16[2,8,4096]{2,1,0:T(8,128)(2,1)S(1)}, bf16[2,8,4096]{2,1,0:T(8,128)(2,1)S(1)}, u32[]{:S(2)}, u32[]{:S(2)}) %collective-permute-start.34) | collective-permute-done | bytes 131104 | tf_op jit(solution)/shard_map/ppermute | solution.py:343
  69.1 3.6 %collective-permute-start.36 = (bf16[12,8,4096]{2,1,0:T(8,128)(2,1)S(1)}, bf16[12,8,4096]{2,1,0:T(8,128)(2,1)S(1)}, u32[]{:S(2)}, u32[]{:S(2)}) collective-permute-start(bf16[12,8,4096]{2,1,0:T(8,128)(2,1)S(1)} %shard_map.65), channel_id=1, source_target_pairs={{0,1},{1,0},{2,3},{3,2},{4,5},{5,4},{6,7},{7,6},{8,9},{9,8},{10,11... | collective-permute-start | bytes 2359304 | tf_op jit(solution)/shard_map/ppermute | solution.py:346
  72.8 2.0 %shard_map.64 = (f32[8,128]{1,0:T(8,128)}, bf16[16,8,16384]{2,1,0:T(8,128)(2,1)}) custom-call(bf16[16,8,16384]{2,1,0:T(8,128)(2,1)} %get-tuple-element.53.refs_0_, bf16[2,8,4096]{2,1,0:T(8,128)(2,1)S(1)} %collective-permute-done.21.refs_1_.refs_0_, bf16[2,8,4096]{2,1,0:T(8,128)(2,1)S(1)} %collective-permute-done.31.refs_2_.refs_1_, ...), custom_call_target="tpu_custom_call", output_to_operand_aliasing={{1}: (0, {})} | custom-call | flops 1 | bytes 1 | tf_op jit(solution)/shard_map/pallas_call | solution.py:324
  74.8 1.6 %shard_map.66 = (f32[8,128]{1,0:T(8,128)}, bf16[16,8,16384]{2,1,0:T(8,128)(2,1)}) custom-call(bf16[16,8,16384]{2,1,0:T(8,128)(2,1)} %get-tuple-element.54.refs_0_, bf16[12,8,4096]{2,1,0:T(8,128)(2,1)S(1)} %collective-permute-done.36.refs_1_), custom_call_target="tpu_custom_call", output_to_operand_aliasing={{1}: (0, {})} | custom-call | flops 1 | bytes 1 | tf_op jit(solution)/shard_map/pallas_call | solution.py:324
  (52 shorter events, 1.4 us)
Async XLA Ops:
  4.4 11.8 %collective-permute-start.3 = (bf16[4,16,4096]{2,1,0:T(8,128)(2,1)S(1)}, bf16[4,16,4096]{2,1,0:T(8,128)(2,1)S(1)}, u32[]{:S(2)}, u32[]{:S(2)}) collective-permute-start(bf16[4,16,4096]{2,1,0:T(8,128)(2,1)S(1)} %get-tuple-element.33._), channel_id=1, source_target_pairs={{0,1},{1,0},{2,3},{3,2},{4,5},{5,4},{6,7},{7,6},{8,9},{9,8},{10,11... | collective-permute-start | bytes 1572872 | tf_op jit(solution)/shard_map/ppermute | solution.py:346
  9.0 12.8 %collective-permute-start.2 = (bf16[4,16,4096]{2,1,0:T(8,128)(2,1)S(1)}, bf16[4,16,4096]{2,1,0:T(8,128)(2,1)S(1)}, u32[]{:S(2)}, u32[]{:S(2)}) collective-permute-start(bf16[4,16,4096]{2,1,0:T(8,128)(2,1)S(1)} %get-tuple-element.34._), channel_id=1, source_target_pairs={{0,1},{1,0},{2,3},{3,2},{4,5},{5,4},{6,7},{7,6},{8,9},{9,8},{10,11... | collective-permute-start | bytes 1572872 | tf_op jit(solution)/shard_map/ppermute | solution.py:346
  9.1 2.3 %collective-permute-start.4 = (bf16[2,16,4096]{2,1,0:T(8,128)(2,1)S(1)}, bf16[2,16,4096]{2,1,0:T(8,128)(2,1)S(1)}, u32[]{:S(2)}, u32[]{:S(2)}) collective-permute-start(bf16[2,16,4096]{2,1,0:T(8,128)(2,1)S(1)} %get-tuple-element.32._), channel_id=1, source_target_pairs={{0,1},{1,0},{2,3},{3,2},{4,5},{5,4},{6,7},{7,6},{8,9},{9,8},{10,11... | collective-permute-start | bytes 786440 | tf_op jit(solution)/shard_map/ppermute | solution.py:346
  10.9 17.4 %collective-permute-start.1 = (bf16[4,16,4096]{2,1,0:T(8,128)(2,1)S(1)}, bf16[4,16,4096]{2,1,0:T(8,128)(2,1)S(1)}, u32[]{:S(2)}, u32[]{:S(2)}) collective-permute-start(bf16[4,16,4096]{2,1,0:T(8,128)(2,1)S(1)} %get-tuple-element.35._), channel_id=1, source_target_pairs={{0,1},{1,0},{2,3},{3,2},{4,5},{5,4},{6,7},{7,6},{8,9},{9,8},{10,11... | collective-permute-start | bytes 1572872 | tf_op jit(solution)/shard_map/ppermute | solution.py:346
  11.4 5.9 %collective-permute-start.5 = (bf16[16,4096]{1,0:T(8,128)(2,1)S(1)}, bf16[16,4096]{1,0:T(8,128)(2,1)S(1)}, u32[]{:S(2)}, u32[]{:S(2)}) collective-permute-start(bf16[16,4096]{1,0:T(8,128)(2,1)S(1)} %shard_map.46), channel_id=1, source_target_pairs={{0,2},{1,15},{2,4},{3,1},{4,6},{5,3},{6,8},{7,5},{8,10},{9,7},{10,... | collective-permute-start | bytes 393224 | tf_op jit(solution)/shard_map/ppermute | solution.py:343
  15.4 5.0 %collective-permute-start.8 = (bf16[16,4096]{1,0:T(8,128)(2,1)S(1)}, bf16[16,4096]{1,0:T(8,128)(2,1)S(1)}, u32[]{:S(2)}, u32[]{:S(2)}) collective-permute-start(bf16[16,4096]{1,0:T(8,128)(2,1)S(1)} %shard_map.49), channel_id=1, source_target_pairs={{0,2},{1,15},{2,4},{3,1},{4,6},{5,3},{6,8},{7,5},{8,10},{9,7},{10,... | collective-permute-start | bytes 393224 | tf_op jit(solution)/shard_map/ppermute | solution.py:343
  16.2 5.7 %collective-permute-start.12 = (bf16[16,4096]{1,0:T(8,128)(2,1)S(1)}, bf16[16,4096]{1,0:T(8,128)(2,1)S(1)}, u32[]{:S(2)}, u32[]{:S(2)}) collective-permute-start(bf16[16,4096]{1,0:T(8,128)(2,1)S(1)} %shard_map.53), channel_id=1, source_target_pairs={{0,2},{1,15},{2,4},{3,1},{4,6},{5,3},{6,8},{7,5},{8,10},{9,7},{10,... | collective-permute-start | bytes 393224 | tf_op jit(solution)/shard_map/ppermute | solution.py:343
  17.3 6.2 %collective-permute-start.14 = (bf16[16,4096]{1,0:T(8,128)(2,1)S(1)}, bf16[16,4096]{1,0:T(8,128)(2,1)S(1)}, u32[]{:S(2)}, u32[]{:S(2)}) collective-permute-start(bf16[16,4096]{1,0:T(8,128)(2,1)S(1)} %shard_map.55), channel_id=1, source_target_pairs={{0,2},{1,15},{2,4},{3,1},{4,6},{5,3},{6,8},{7,5},{8,10},{9,7},{10,... | collective-permute-start | bytes 393224 | tf_op jit(solution)/shard_map/ppermute | solution.py:343
  20.4 6.0 %collective-permute-start.6 = (bf16[16,4096]{1,0:T(8,128)(2,1)S(1)}, bf16[16,4096]{1,0:T(8,128)(2,1)S(1)}, u32[]{:S(2)}, u32[]{:S(2)}) collective-permute-start(bf16[16,4096]{1,0:T(8,128)(2,1)S(1)} %shard_map.47), channel_id=1, source_target_pairs={{0,2},{1,15},{2,4},{3,1},{4,6},{5,3},{6,8},{7,5},{8,10},{9,7},{10,... | collective-permute-start | bytes 393224 | tf_op jit(solution)/shard_map/ppermute | solution.py:343
  21.8 5.1 %collective-permute-start.9 = (bf16[16,4096]{1,0:T(8,128)(2,1)S(1)}, bf16[16,4096]{1,0:T(8,128)(2,1)S(1)}, u32[]{:S(2)}, u32[]{:S(2)}) collective-permute-start(bf16[16,4096]{1,0:T(8,128)(2,1)S(1)} %shard_map.50), channel_id=1, source_target_pairs={{0,2},{1,15},{2,4},{3,1},{4,6},{5,3},{6,8},{7,5},{8,10},{9,7},{10,... | collective-permute-start | bytes 393224 | tf_op jit(solution)/shard_map/ppermute | solution.py:343
  22.0 7.4 %collective-permute-start.13 = (bf16[16,4096]{1,0:T(8,128)(2,1)S(1)}, bf16[16,4096]{1,0:T(8,128)(2,1)S(1)}, u32[]{:S(2)}, u32[]{:S(2)}) collective-permute-start(bf16[16,4096]{1,0:T(8,128)(2,1)S(1)} %shard_map.54), channel_id=1, source_target_pairs={{0,2},{1,15},{2,4},{3,1},{4,6},{5,3},{6,8},{7,5},{8,10},{9,7},{10,... | collective-permute-start | bytes 393224 | tf_op jit(solution)/shard_map/ppermute | solution.py:343
  23.6 5.8 %collective-permute-start.15 = (bf16[16,4096]{1,0:T(8,128)(2,1)S(1)}, bf16[16,4096]{1,0:T(8,128)(2,1)S(1)}, u32[]{:S(2)}, u32[]{:S(2)}) collective-permute-start(bf16[16,4096]{1,0:T(8,128)(2,1)S(1)} %shard_map.56), channel_id=1, source_target_pairs={{0,2},{1,15},{2,4},{3,1},{4,6},{5,3},{6,8},{7,5},{8,10},{9,7},{10,... | collective-permute-start | bytes 393224 | tf_op jit(solution)/shard_map/ppermute | solution.py:343
  26.5 8.4 %collective-permute-start.7 = (bf16[16,4096]{1,0:T(8,128)(2,1)S(1)}, bf16[16,4096]{1,0:T(8,128)(2,1)S(1)}, u32[]{:S(2)}, u32[]{:S(2)}) collective-permute-start(bf16[16,4096]{1,0:T(8,128)(2,1)S(1)} %shard_map.48), channel_id=1, source_target_pairs={{0,2},{1,15},{2,4},{3,1},{4,6},{5,3},{6,8},{7,5},{8,10},{9,7},{10,... | collective-permute-start | bytes 393224 | tf_op jit(solution)/shard_map/ppermute | solution.py:343
  27.0 7.9 %collective-permute-start.10 = (bf16[16,4096]{1,0:T(8,128)(2,1)S(1)}, bf16[16,4096]{1,0:T(8,128)(2,1)S(1)}, u32[]{:S(2)}, u32[]{:S(2)}) collective-permute-start(bf16[16,4096]{1,0:T(8,128)(2,1)S(1)} %shard_map.51), channel_id=1, source_target_pairs={{0,2},{1,15},{2,4},{3,1},{4,6},{5,3},{6,8},{7,5},{8,10},{9,7},{10,... | collective-permute-start | bytes 393224 | tf_op jit(solution)/shard_map/ppermute | solution.py:343
  28.4 10.3 %collective-permute-start = (bf16[4,8,4096]{2,1,0:T(8,128)(2,1)S(1)}, bf16[4,8,4096]{2,1,0:T(8,128)(2,1)S(1)}, u32[]{:S(2)}, u32[]{:S(2)}) collective-permute-start(bf16[4,8,4096]{2,1,0:T(8,128)(2,1)S(1)} %get-tuple-element.38), channel_id=1, source_target_pairs={{0,1},{1,0},{2,3},{3,2},{4,5},{5,4},{6,7},{7,6},{8,9},{9,8},{10,11... | collective-permute-start | bytes 786440 | tf_op jit(solution)/shard_map/ppermute | solution.py:346
  29.5 9.1 %collective-permute-start.16 = (bf16[2,8,4096]{2,1,0:T(8,128)(2,1)S(1)}, bf16[2,8,4096]{2,1,0:T(8,128)(2,1)S(1)}, u32[]{:S(2)}, u32[]{:S(2)}) collective-permute-start(bf16[2,8,4096]{2,1,0:T(8,128)(2,1)S(1)} %get-tuple-element.44), channel_id=1, source_target_pairs={{0,2},{1,15},{2,4},{3,1},{4,6},{5,3},{6,8},{7,5},{8,10},{9,7},{10,... | collective-permute-start | bytes 393224 | tf_op jit(solution)/shard_map/ppermute | solution.py:343
  31.4 7.6 %collective-permute-start.18 = (bf16[2,8,4096]{2,1,0:T(8,128)(2,1)S(1)}, bf16[2,8,4096]{2,1,0:T(8,128)(2,1)S(1)}, u32[]{:S(2)}, u32[]{:S(2)}) collective-permute-start(bf16[2,8,4096]{2,1,0:T(8,128)(2,1)S(1)} %get-tuple-element.46), channel_id=1, source_target_pairs={{0,3},{1,14},{2,5},{3,0},{4,7},{5,2},{6,9},{7,4},{8,11},{9,6},{10,... | collective-permute-start | bytes 393224 | tf_op jit(solution)/shard_map/ppermute | solution.py:343
  35.0 3.9 %collective-permute-start.11 = (bf16[2,8,4096]{2,1,0:T(8,128)(2,1)S(1)}, bf16[2,8,4096]{2,1,0:T(8,128)(2,1)S(1)}, u32[]{:S(2)}, u32[]{:S(2)}) collective-permute-start(bf16[2,8,4096]{2,1,0:T(8,128)(2,1)S(1)} %get-tuple-element.43), channel_id=1, source_target_pairs={{0,2},{1,15},{2,4},{3,1},{4,6},{5,3},{6,8},{7,5},{8,10},{9,7},{10,... | collective-permute-start | bytes 393224 | tf_op jit(solution)/shard_map/ppermute | solution.py:343
  35.1 7.5 %collective-permute-start.17 = (bf16[2,8,4096]{2,1,0:T(8,128)(2,1)S(1)}, bf16[2,8,4096]{2,1,0:T(8,128)(2,1)S(1)}, u32[]{:S(2)}, u32[]{:S(2)}) collective-permute-start(bf16[2,8,4096]{2,1,0:T(8,128)(2,1)S(1)} %get-tuple-element.45), channel_id=1, source_target_pairs={{0,3},{1,14},{2,5},{3,0},{4,7},{5,2},{6,9},{7,4},{8,11},{9,6},{10,... | collective-permute-start | bytes 393224 | tf_op jit(solution)/shard_map/ppermute | solution.py:343
  43.1 1.8 %collective-permute-start.23 = (bf16[4,8,4096]{2,1,0:T(8,128)(2,1)S(1)}, bf16[4,8,4096]{2,1,0:T(8,128)(2,1)S(1)}, u32[]{:S(2)}, u32[]{:S(2)}) collective-permute-start(bf16[4,8,4096]{2,1,0:T(8,128)(2,1)S(1)} %get-tuple-element.49), channel_id=1, source_target_pairs={{0,1},{1,0},{2,3},{3,2},{4,5},{5,4},{6,7},{7,6},{8,9},{9,8},{10,11... | collective-permute-start | bytes 786440 | tf_op jit(solution)/shard_map/ppermute | solution.py:346
  43.2 3.9 %collective-permute-start.19 = (bf16[2,8,4096]{2,1,0:T(8,128)(2,1)S(1)}, bf16[2,8,4096]{2,1,0:T(8,128)(2,1)S(1)}, u32[]{:S(2)}, u32[]{:S(2)}) collective-permute-start(bf16[2,8,4096]{2,1,0:T(8,128)(2,1)S(1)} %get-tuple-element.47.refs_1_), channel_id=1, source_target_pairs={{0,2},{1,15},{2,4},{3,1},{4,6},{5,3},{6,8},{7,5},{8,10},{9,7},{10,... | collective-permute-start | bytes 393224 | tf_op jit(solution)/shard_map/ppermute | solution.py:343
  44.8 5.0 %collective-permute-start.24 = (bf16[2,8,4096]{2,1,0:T(8,128)(2,1)S(1)}, bf16[2,8,4096]{2,1,0:T(8,128)(2,1)S(1)}, u32[]{:S(2)}, u32[]{:S(2)}) collective-permute-start(bf16[2,8,4096]{2,1,0:T(8,128)(2,1)S(1)} %get-tuple-element.48.refs_2_), channel_id=1, source_target_pairs={{0,2},{1,15},{2,4},{3,1},{4,6},{5,3},{6,8},{7,5},{8,10},{9,7},{10,... | collective-permute-start | bytes 393224 | tf_op jit(solution)/shard_map/ppermute | solution.py:343
  44.9 6.4 %collective-permute-start.25 = (bf16[2,8,4096]{2,1,0:T(8,128)(2,1)S(1)}, bf16[2,8,4096]{2,1,0:T(8,128)(2,1)S(1)}, u32[]{:S(2)}, u32[]{:S(2)}) collective-permute-start(bf16[2,8,4096]{2,1,0:T(8,128)(2,1)S(1)} %get-tuple-element.50.refs_3_), channel_id=1, source_target_pairs={{0,2},{1,15},{2,4},{3,1},{4,6},{5,3},{6,8},{7,5},{8,10},{9,7},{10,... | collective-permute-start | bytes 393224 | tf_op jit(solution)/shard_map/ppermute | solution.py:343
  46.1 8.0 %collective-permute-start.26 = (bf16[2,8,4096]{2,1,0:T(8,128)(2,1)S(1)}, bf16[2,8,4096]{2,1,0:T(8,128)(2,1)S(1)}, u32[]{:S(2)}, u32[]{:S(2)}) collective-permute-start(bf16[2,8,4096]{2,1,0:T(8,128)(2,1)S(1)} %get-tuple-element.51.refs_4_), channel_id=1, source_target_pairs={{0,2},{1,15},{2,4},{3,1},{4,6},{5,3},{6,8},{7,5},{8,10},{9,7},{10,... | collective-permute-start | bytes 393224 | tf_op jit(solution)/shard_map/ppermute | solution.py:343
  47.1 7.0 %collective-permute-start.20 = (bf16[2,8,4096]{2,1,0:T(8,128)(2,1)S(1)}, bf16[2,8,4096]{2,1,0:T(8,128)(2,1)S(1)}, u32[]{:S(2)}, u32[]{:S(2)}) collective-permute-start(bf16[2,8,4096]{2,1,0:T(8,128)(2,1)S(1)} %collective-permute-done.19.refs_5_.refs_0_), channel_id=1, source_target_pairs={{0,2},{1,15},{2,4},{3,1},{4,6},{5,3},{6,8},{7,5},{8,10},{9,7},{10,... | collective-permute-start | bytes 393224 | tf_op jit(solution)/shard_map/ppermute | solution.py:343
  49.9 8.4 %collective-permute-start.28 = (bf16[2,8,4096]{2,1,0:T(8,128)(2,1)S(1)}, bf16[2,8,4096]{2,1,0:T(8,128)(2,1)S(1)}, u32[]{:S(2)}, u32[]{:S(2)}) collective-permute-start(bf16[2,8,4096]{2,1,0:T(8,128)(2,1)S(1)} %collective-permute-done.24.refs_6_.refs_1_), channel_id=1, source_target_pairs={{0,2},{1,15},{2,4},{3,1},{4,6},{5,3},{6,8},{7,5},{8,10},{9,7},{10,... | collective-permute-start | bytes 393224 | tf_op jit(solution)/shard_map/ppermute | solution.py:343
  51.3 4.7 %collective-permute-start.29 = (bf16[2,8,4096]{2,1,0:T(8,128)(2,1)S(1)}, bf16[2,8,4096]{2,1,0:T(8,128)(2,1)S(1)}, u32[]{:S(2)}, u32[]{:S(2)}) collective-permute-start(bf16[2,8,4096]{2,1,0:T(8,128)(2,1)S(1)} %collective-permute-done.25.refs_1_.refs_7_.refs_2_), channel_id=1, source_target_pairs={{0,2},{1,15},{2,4},{3,1},{4,6},{5,3},{6,8},{7,5},{8,10},{9,7},{10,... | collective-permute-start | bytes 393224 | tf_op jit(solution)/shard_map/ppermute | solution.py:343
  52.7 11.6 %collective-permute-start.27 = (bf16[4,8,4096]{2,1,0:T(8,128)(2,1)S(1)}, bf16[4,8,4096]{2,1,0:T(8,128)(2,1)S(1)}, u32[]{:S(2)}, u32[]{:S(2)}) collective-permute-start(bf16[4,8,4096]{2,1,0:T(8,128)(2,1)S(1)} %shard_map.60), channel_id=1, source_target_pairs={{0,16},{16,32},{32,48},{48,64},{64,80},{80,96},{96,112},{112,128},... | collective-permute-start | bytes 786440 | tf_op jit(solution)/shard_map/ppermute | solution.py:384
  54.1 4.2 %collective-permute-start.30 = (bf16[2,8,4096]{2,1,0:T(8,128)(2,1)S(1)}, bf16[2,8,4096]{2,1,0:T(8,128)(2,1)S(1)}, u32[]{:S(2)}, u32[]{:S(2)}) collective-permute-start(bf16[2,8,4096]{2,1,0:T(8,128)(2,1)S(1)} %collective-permute-done.26.refs_8_.refs_3_), channel_id=1, source_target_pairs={{0,2},{1,15},{2,4},{3,1},{4,6},{5,3},{6,8},{7,5},{8,10},{9,7},{10,... | collective-permute-start | bytes 393224 | tf_op jit(solution)/shard_map/ppermute | solution.py:343
  54.1 8.4 %collective-permute-start.21 = (bf16[2,8,4096]{2,1,0:T(8,128)(2,1)S(1)}, bf16[2,8,4096]{2,1,0:T(8,128)(2,1)S(1)}, u32[]{:S(2)}, u32[]{:S(2)}) collective-permute-start(bf16[2,8,4096]{2,1,0:T(8,128)(2,1)S(1)} %collective-permute-done.20.refs_10_.refs_4_), channel_id=1, source_target_pairs={{0,2},{1,15},{2,4},{3,1},{4,6},{5,3},{6,8},{7,5},{8,10},{9,7},{10,... | collective-permute-start | bytes 393224 | tf_op jit(solution)/shard_map/ppermute | solution.py:343
  56.0 6.8 %collective-permute-start.32 = (bf16[2,8,4096]{2,1,0:T(8,128)(2,1)S(1)}, bf16[2,8,4096]{2,1,0:T(8,128)(2,1)S(1)}, u32[]{:S(2)}, u32[]{:S(2)}) collective-permute-start(bf16[2,8,4096]{2,1,0:T(8,128)(2,1)S(1)} %collective-permute-done.29.refs_12_.refs_6_), channel_id=1, source_target_pairs={{0,2},{1,15},{2,4},{3,1},{4,6},{5,3},{6,8},{7,5},{8,10},{9,7},{10,... | collective-permute-start | bytes 393224 | tf_op jit(solution)/shard_map/ppermute | solution.py:343
  58.4 14.4 %collective-permute-start.35 = (bf16[16,8,4096]{2,1,0:T(8,128)(2,1)S(1)}, bf16[16,8,4096]{2,1,0:T(8,128)(2,1)S(1)}, u32[]{:S(2)}, u32[]{:S(2)}) collective-permute-start(bf16[16,8,4096]{2,1,0:T(8,128)(2,1)S(1)} %shard_map.63), channel_id=1, source_target_pairs={{0,1},{1,0},{2,3},{3,2},{4,5},{5,4},{6,7},{7,6},{8,9},{9,8},{10,11... | collective-permute-start | bytes 3145736 | tf_op jit(solution)/shard_map/ppermute | solution.py:346
  60.7 7.3 %collective-permute-start.31 = (bf16[2,8,4096]{2,1,0:T(8,128)(2,1)S(1)}, bf16[2,8,4096]{2,1,0:T(8,128)(2,1)S(1)}, u32[]{:S(2)}, u32[]{:S(2)}) collective-permute-start(bf16[2,8,4096]{2,1,0:T(8,128)(2,1)S(1)} %collective-permute-done.28.refs_11_.refs_5_), channel_id=1, source_target_pairs={{0,2},{1,15},{2,4},{3,1},{4,6},{5,3},{6,8},{7,5},{8,10},{9,7},{10,... | collective-permute-start | bytes 393224 | tf_op jit(solution)/shard_map/ppermute | solution.py:343
  62.4 4.1 %collective-permute-start.22 = (bf16[2,8,4096]{2,1,0:T(8,128)(2,1)S(1)}, bf16[2,8,4096]{2,1,0:T(8,128)(2,1)S(1)}, u32[]{:S(2)}, u32[]{:S(2)}) collective-permute-start(bf16[2,8,4096]{2,1,0:T(8,128)(2,1)S(1)} %collective-permute-done.21.refs_1_.refs_0_), channel_id=1, source_target_pairs={{0,2},{1,15},{2,4},{3,1},{4,6},{5,3},{6,8},{7,5},{8,10},{9,7},{10,... | collective-permute-start | bytes 393224 | tf_op jit(solution)/shard_map/ppermute | solution.py:343
  62.8 5.2 %collective-permute-start.33 = (bf16[2,8,4096]{2,1,0:T(8,128)(2,1)S(1)}, bf16[2,8,4096]{2,1,0:T(8,128)(2,1)S(1)}, u32[]{:S(2)}, u32[]{:S(2)}) collective-permute-start(bf16[2,8,4096]{2,1,0:T(8,128)(2,1)S(1)} %collective-permute-done.30.refs_13_.refs_7_), channel_id=1, source_target_pairs={{0,2},{1,15},{2,4},{3,1},{4,6},{5,3},{6,8},{7,5},{8,10},{9,7},{10,... | collective-permute-start | bytes 393224 | tf_op jit(solution)/shard_map/ppermute | solution.py:343
  64.3 4.8 %collective-permute-start.34 = (bf16[2,8,4096]{2,1,0:T(8,128)(2,1)S(1)}, bf16[2,8,4096]{2,1,0:T(8,128)(2,1)S(1)}, u32[]{:S(2)}, u32[]{:S(2)}) collective-permute-start(bf16[2,8,4096]{2,1,0:T(8,128)(2,1)S(1)} %shard_map.62), channel_id=1, source_target_pairs={{0,2},{1,15},{2,4},{3,1},{4,6},{5,3},{6,8},{7,5},{8,10},{9,7},{10,... | collective-permute-start | bytes 393224 | tf_op jit(solution)/shard_map/ppermute | solution.py:343
  69.1 5.7 %collective-permute-start.36 = (bf16[12,8,4096]{2,1,0:T(8,128)(2,1)S(1)}, bf16[12,8,4096]{2,1,0:T(8,128)(2,1)S(1)}, u32[]{:S(2)}, u32[]{:S(2)}) collective-permute-start(bf16[12,8,4096]{2,1,0:T(8,128)(2,1)S(1)} %shard_map.65), channel_id=1, source_target_pairs={{0,1},{1,0},{2,3},{3,2},{4,5},{5,4},{6,7},{7,6},{8,9},{9,8},{10,11... | collective-permute-start | bytes 2359304 | tf_op jit(solution)/shard_map/ppermute | solution.py:346

commit v3 on v2

--- a/solution.py
+++ b/solution.py
@@ -9,7 +9,7 @@
 BLOCK = 128
 D = 16384
 HALF = D // 2
-PIECES = 2
+PIECES = 1
 COLS = HALF // PIECES
 CHIPS = 8
 FAR = CHIPS // 2

time: 76.7 us -> 75.7 us (0.987)
    ppermute x8, starting transfers between devices: 11.2 us -> 10.4 us  [other_core(): return lax.ppermute(block, 'tp', [(i, i ^ 1) for i in range(n)])]
    ppermute x28 -> x23, starting transfers between devices: 40.3 us -> 41.1 us  [onward(): lax.ppermute(block, 'tp', [(i, j ^ 1) if cross else (i, j) for i, j in ro...]
    ppermute x28 -> x23, waiting for transfers between devices: 8.15 us -> 8.38 us  [onward(): lax.ppermute(block, 'tp', [(i, j ^ 1) if cross else (i, j) for i, j in ro...]
  transfers between devices with their start and end apart: 37 -> 32, of which waited for: 9 -> 8; matrix products, arithmetic and copies ran while one was open for 0% -> 0% of each run, Pallas kernels for 10% -> 10%
where the time goes in v3:
time: 75.7 us; the launch traced here: 75.6 us
  starting transfers between devices  52.9 us (70%)
  Pallas kernels  13.3 us (18%)
  waiting for transfers between devices  8.42 us (11%)
  between operations  1.02 us (1%)
    ppermute x23, starting transfers between devices, onward(): lax.ppermute(block, 'tp', [(i, j ^ 1) if cross else (i, j) for i, j in ro...  41.1 us
    ppermute x8, starting transfers between devices, other_core(): return lax.ppermute(block, 'tp', [(i, i ^ 1) for i in range(n)])  10.4 us
    ppermute x23, waiting for transfers between devices, onward(): lax.ppermute(block, 'tp', [(i, j ^ 1) if cross else (i, j) for i, j in ro...  8.38 us
    pallas_call x3, Pallas kernels, put(): pl.pallas_call(lambda *refs: put_kernel(places, len(held) + len(after), *...  4.79 us
    pallas_call x3, Pallas kernels, code_rows(): pl.pallas_call(lambda held_ref, _, *refs: code_kernel(k, held_ref, *refs)...  3.85 us
    pallas_call x1, Pallas kernels, code_far(): pl.pallas_call(far_kernel, out_shape=(part, part, whole, rows), in_specs=...  2.47 us
  transfers between devices with their start and end apart: 32, of which 8 were waited for; matrix products, arithmetic and copies ran while one was open for 0% of the time, Pallas kernels for 10%

profile of v3, /device:TPU:1, one launch (start us, length us, event | category | flops | bytes accessed | tf_op | source)
XLA Modules:
  0.0 75.6 jit_solution(8122672148017821144)
XLA Ops:
  0.6 2.5 %shard_map.41 = (bf16[1,16,8192]{2,1,0:T(8,128)(2,1)S(1)}, bf16[1,16,8192]{2,1,0:T(8,128)(2,1)S(1)}, bf16[16,16,8192]{2,1,0:T(8,128)(2,1)S(1)}, bf16[2,16,8192]{2,1,0:T(8,128)(2,1)S(1)}) custom-call(bf16[128,16384]{1,0:T(8,128)(2,1)} %bitcast.4, bf16[128,16384]{1,0:T(8,128)(2,1)} %bitcast.5), custom_call_target="tpu_custom_call" | custom-call | flops 1 | bytes 1 | tf_op jit(solution)/shard_map/pallas_call | solution.py:113
  3.1 1.3 %shard_map.42 = (bf16[2,16,8192]{2,1,0:T(8,128)(2,1)S(1)}, bf16[2,16,8192]{2,1,0:T(8,128)(2,1)S(1)}) custom-call(bf16[16,16,8192]{2,1,0:T(8,128)(2,1)S(1)} %get-tuple-element.30.held_ref, bf16[1,16,8192]{2,1,0:T(8,128)(2,1)S(1)} %get-tuple-element.32._), custom_call_target="tpu_custom_call" | custom-call | flops 1 | bytes 1 | tf_op jit(solution)/shard_map/pallas_call | solution.py:132
  4.4 3.3 %collective-permute-start.3 = (bf16[2,16,8192]{2,1,0:T(8,128)(2,1)S(1)}, bf16[2,16,8192]{2,1,0:T(8,128)(2,1)S(1)}, u32[]{:S(2)}, u32[]{:S(2)}) collective-permute-start(bf16[2,16,8192]{2,1,0:T(8,128)(2,1)S(1)} %get-tuple-element.33._), channel_id=1, source_target_pairs={{0,1},{1,0},{2,3},{3,2},{4,5},{5,4},{6,7},{7,6},{8,9},{9,8},{10,11... | collective-permute-start | bytes 1572872 | tf_op jit(solution)/shard_map/ppermute | solution.py:346
  7.7 0.1 collective-permute-start.4
  7.8 1.3 %shard_map.43 = (bf16[2,16,8192]{2,1,0:T(8,128)(2,1)S(1)}, bf16[2,16,8192]{2,1,0:T(8,128)(2,1)S(1)}) custom-call(bf16[16,16,8192]{2,1,0:T(8,128)(2,1)S(1)} %get-tuple-element.30.held_ref, bf16[2,16,8192]{2,1,0:T(8,128)(2,1)S(1)} %get-tuple-element.33._), custom_call_target="tpu_custom_call" | custom-call | flops 1 | bytes 1 | tf_op jit(solution)/shard_map/pallas_call | solution.py:132
  9.1 0.5 collective-permute-start.2
  9.7 3.9 %collective-permute-start.5 = (bf16[16,8192]{1,0:T(8,128)(2,1)S(1)}, bf16[16,8192]{1,0:T(8,128)(2,1)S(1)}, u32[]{:S(2)}, u32[]{:S(2)}) collective-permute-start(bf16[16,8192]{1,0:T(8,128)(2,1)S(1)} %shard_map.46), channel_id=1, source_target_pairs={{0,2},{1,15},{2,4},{3,1},{4,6},{5,3},{6,8},{7,5},{8,10},{9,7},{10,... | collective-permute-start | bytes 786440 | tf_op jit(solution)/shard_map/ppermute | solution.py:343
  13.6 1.3 %shard_map.44 = (bf16[2,16,8192]{2,1,0:T(8,128)(2,1)S(1)}, bf16[2,16,8192]{2,1,0:T(8,128)(2,1)S(1)}) custom-call(bf16[16,16,8192]{2,1,0:T(8,128)(2,1)S(1)} %get-tuple-element.30.held_ref, bf16[2,16,8192]{2,1,0:T(8,128)(2,1)S(1)} %get-tuple-element.34._), custom_call_target="tpu_custom_call" | custom-call | flops 1 | bytes 1 | tf_op jit(solution)/shard_map/pallas_call | solution.py:132
  15.0 0.8 %collective-permute-start.9 = (bf16[16,8192]{1,0:T(8,128)(2,1)S(1)}, bf16[16,8192]{1,0:T(8,128)(2,1)S(1)}, u32[]{:S(2)}, u32[]{:S(2)}) collective-permute-start(bf16[16,8192]{1,0:T(8,128)(2,1)S(1)} %shard_map.50), channel_id=1, source_target_pairs={{0,2},{1,15},{2,4},{3,1},{4,6},{5,3},{6,8},{7,5},{8,10},{9,7},{10,... | collective-permute-start | bytes 786440 | tf_op jit(solution)/shard_map/ppermute | solution.py:343
  15.8 1.1 %collective-permute-done.5.refs_2_ = bf16[16,8192]{1,0:T(8,128)(2,1)S(1)} collective-permute-done((bf16[16,8192]{1,0:T(8,128)(2,1)S(1)}, bf16[16,8192]{1,0:T(8,128)(2,1)S(1)}, u32[]{:S(2)}, u32[]{:S(2)}) %collective-permute-start.5) | collective-permute-done | bytes 262176 | tf_op jit(solution)/shard_map/ppermute | solution.py:343
  16.9 0.1 shard_map.47
  17.0 3.2 %collective-permute-start.6 = (bf16[16,8192]{1,0:T(8,128)(2,1)S(1)}, bf16[16,8192]{1,0:T(8,128)(2,1)S(1)}, u32[]{:S(2)}, u32[]{:S(2)}) collective-permute-start(bf16[16,8192]{1,0:T(8,128)(2,1)S(1)} %shard_map.47), channel_id=1, source_target_pairs={{0,2},{1,15},{2,4},{3,1},{4,6},{5,3},{6,8},{7,5},{8,10},{9,7},{10,... | collective-permute-start | bytes 786440 | tf_op jit(solution)/shard_map/ppermute | solution.py:343
  20.2 0.4 collective-permute-done.9.refs_2_
  20.6 0.1 shard_map.51
  20.7 2.3 %collective-permute-start.10 = (bf16[16,8192]{1,0:T(8,128)(2,1)S(1)}, bf16[16,8192]{1,0:T(8,128)(2,1)S(1)}, u32[]{:S(2)}, u32[]{:S(2)}) collective-permute-start(bf16[16,8192]{1,0:T(8,128)(2,1)S(1)} %shard_map.51), channel_id=1, source_target_pairs={{0,2},{1,15},{2,4},{3,1},{4,6},{5,3},{6,8},{7,5},{8,10},{9,7},{10,... | collective-permute-start | bytes 786440 | tf_op jit(solution)/shard_map/ppermute | solution.py:343
  23.0 0.5 collective-permute-done.6.refs_2_
  23.6 0.1 shard_map.48
  23.7 3.4 %collective-permute-start.7 = (bf16[16,8192]{1,0:T(8,128)(2,1)S(1)}, bf16[16,8192]{1,0:T(8,128)(2,1)S(1)}, u32[]{:S(2)}, u32[]{:S(2)}) collective-permute-start(bf16[16,8192]{1,0:T(8,128)(2,1)S(1)} %shard_map.48), channel_id=1, source_target_pairs={{0,2},{1,15},{2,4},{3,1},{4,6},{5,3},{6,8},{7,5},{8,10},{9,7},{10,... | collective-permute-start | bytes 786440 | tf_op jit(solution)/shard_map/ppermute | solution.py:343
  27.0 0.9 %shard_map.45 = (bf16[2,8,8192]{2,1,0:T(8,128)(2,1)S(1)}, bf16[2,8,8192]{2,1,0:T(8,128)(2,1)S(1)}, bf16[2,8,8192]{2,1,0:T(8,128)(2,1)S(1)}) custom-call(bf16[16,16,8192]{2,1,0:T(8,128)(2,1)S(1)} %get-tuple-element.30.held_ref, bf16[2,16,8192]{2,1,0:T(8,128)(2,1)S(1)} %get-tuple-element.31.stream_ref, bf16[2,16,8192]{2,1,0:T(8,128)(2,1)S(1)} %get-tuple-element.35._), custom_call_target="tpu_custom_call" | custom-call | flops 1 | bytes 1 | tf_op jit(solution)/shard_map/pallas_call | solution.py:163
  28.0 0.1 shard_map.52
  28.2 2.7 %collective-permute-start.11 = (bf16[1,8,8192]{2,1,0:T(8,128)(2,1)S(1)}, bf16[1,8,8192]{2,1,0:T(8,128)(2,1)S(1)}, u32[]{:S(2)}, u32[]{:S(2)}) collective-permute-start(bf16[1,8,8192]{2,1,0:T(8,128)(2,1)S(1)} %get-tuple-element.44), channel_id=1, source_target_pairs={{0,2},{1,15},{2,4},{3,1},{4,6},{5,3},{6,8},{7,5},{8,10},{9,7},{10,... | collective-permute-start | bytes 393224 | tf_op jit(solution)/shard_map/ppermute | solution.py:343
  30.9 1.4 %collective-permute-start.13 = (bf16[1,8,8192]{2,1,0:T(8,128)(2,1)S(1)}, bf16[1,8,8192]{2,1,0:T(8,128)(2,1)S(1)}, u32[]{:S(2)}, u32[]{:S(2)}) collective-permute-start(bf16[1,8,8192]{2,1,0:T(8,128)(2,1)S(1)} %get-tuple-element.46), channel_id=1, source_target_pairs={{0,3},{1,14},{2,5},{3,0},{4,7},{5,2},{6,9},{7,4},{8,11},{9,6},{10,... | collective-permute-start | bytes 393224 | tf_op jit(solution)/shard_map/ppermute | solution.py:343
  32.2 0.1 shard_map.49
  32.4 1.3 %collective-permute-start.8 = (bf16[1,8,8192]{2,1,0:T(8,128)(2,1)S(1)}, bf16[1,8,8192]{2,1,0:T(8,128)(2,1)S(1)}, u32[]{:S(2)}, u32[]{:S(2)}) collective-permute-start(bf16[1,8,8192]{2,1,0:T(8,128)(2,1)S(1)} %get-tuple-element.43), channel_id=1, source_target_pairs={{0,2},{1,15},{2,4},{3,1},{4,6},{5,3},{6,8},{7,5},{8,10},{9,7},{10,... | collective-permute-start | bytes 393224 | tf_op jit(solution)/shard_map/ppermute | solution.py:343
  33.7 3.7 %collective-permute-start.12 = (bf16[1,8,8192]{2,1,0:T(8,128)(2,1)S(1)}, bf16[1,8,8192]{2,1,0:T(8,128)(2,1)S(1)}, u32[]{:S(2)}, u32[]{:S(2)}) collective-permute-start(bf16[1,8,8192]{2,1,0:T(8,128)(2,1)S(1)} %get-tuple-element.45), channel_id=1, source_target_pairs={{0,3},{1,14},{2,5},{3,0},{4,7},{5,2},{6,9},{7,4},{8,11},{9,6},{10,... | collective-permute-start | bytes 393224 | tf_op jit(solution)/shard_map/ppermute | solution.py:343
  37.4 4.0 %collective-permute-done.12.cross0 = bf16[1,8,8192]{2,1,0:T(8,128)(2,1)S(1)} collective-permute-done((bf16[1,8,8192]{2,1,0:T(8,128)(2,1)S(1)}, bf16[1,8,8192]{2,1,0:T(8,128)(2,1)S(1)}, u32[]{:S(2)}, u32[]{:S(2)}) %collective-permute-start.12) | collective-permute-done | bytes 131104 | tf_op jit(solution)/shard_map/ppermute | solution.py:343
  41.4 0.5 shard_map.53
  42.0 1.7 %collective-permute-start.14 = (bf16[1,8,8192]{2,1,0:T(8,128)(2,1)S(1)}, bf16[1,8,8192]{2,1,0:T(8,128)(2,1)S(1)}, u32[]{:S(2)}, u32[]{:S(2)}) collective-permute-start(bf16[1,8,8192]{2,1,0:T(8,128)(2,1)S(1)} %get-tuple-element.47.refs_1_), channel_id=1, source_target_pairs={{0,2},{1,15},{2,4},{3,1},{4,6},{5,3},{6,8},{7,5},{8,10},{9,7},{10,... | collective-permute-start | bytes 393224 | tf_op jit(solution)/shard_map/ppermute | solution.py:343
  43.7 1.2 %collective-permute-start.20 = (bf16[1,8,8192]{2,1,0:T(8,128)(2,1)S(1)}, bf16[1,8,8192]{2,1,0:T(8,128)(2,1)S(1)}, u32[]{:S(2)}, u32[]{:S(2)}) collective-permute-start(bf16[1,8,8192]{2,1,0:T(8,128)(2,1)S(1)} %get-tuple-element.50.refs_3_), channel_id=1, source_target_pairs={{0,2},{1,15},{2,4},{3,1},{4,6},{5,3},{6,8},{7,5},{8,10},{9,7},{10,... | collective-permute-start | bytes 393224 | tf_op jit(solution)/shard_map/ppermute | solution.py:343
  45.1 2.3 %collective-permute-start.21 = (bf16[1,8,8192]{2,1,0:T(8,128)(2,1)S(1)}, bf16[1,8,8192]{2,1,0:T(8,128)(2,1)S(1)}, u32[]{:S(2)}, u32[]{:S(2)}) collective-permute-start(bf16[1,8,8192]{2,1,0:T(8,128)(2,1)S(1)} %get-tuple-element.51.refs_4_), channel_id=1, source_target_pairs={{0,2},{1,15},{2,4},{3,1},{4,6},{5,3},{6,8},{7,5},{8,10},{9,7},{10,... | collective-permute-start | bytes 393224 | tf_op jit(solution)/shard_map/ppermute | solution.py:343
  47.4 1.6 %collective-permute-start.15 = (bf16[1,8,8192]{2,1,0:T(8,128)(2,1)S(1)}, bf16[1,8,8192]{2,1,0:T(8,128)(2,1)S(1)}, u32[]{:S(2)}, u32[]{:S(2)}) collective-permute-start(bf16[1,8,8192]{2,1,0:T(8,128)(2,1)S(1)} %collective-permute-done.14.refs_5_.refs_0_), channel_id=1, source_target_pairs={{0,2},{1,15},{2,4},{3,1},{4,6},{5,3},{6,8},{7,5},{8,10},{9,7},{10,... | collective-permute-start | bytes 393224 | tf_op jit(solution)/shard_map/ppermute | solution.py:343
  49.0 1.4 %collective-permute-start.22 = (bf16[2,8,8192]{2,1,0:T(8,128)(2,1)S(1)}, bf16[2,8,8192]{2,1,0:T(8,128)(2,1)S(1)}, u32[]{:S(2)}, u32[]{:S(2)}) collective-permute-start(bf16[2,8,8192]{2,1,0:T(8,128)(2,1)S(1)} %shard_map.55), channel_id=1, source_target_pairs={{0,16},{16,32},{32,48},{48,64},{64,80},{80,96},{96,112},{112,128},... | collective-permute-start | bytes 786440 | tf_op jit(solution)/shard_map/ppermute | solution.py:384
  50.3 1.2 %collective-permute-start.24 = (bf16[1,8,8192]{2,1,0:T(8,128)(2,1)S(1)}, bf16[1,8,8192]{2,1,0:T(8,128)(2,1)S(1)}, u32[]{:S(2)}, u32[]{:S(2)}) collective-permute-start(bf16[1,8,8192]{2,1,0:T(8,128)(2,1)S(1)} %collective-permute-done.20.refs_1_.refs_7_.refs_2_), channel_id=1, source_target_pairs={{0,2},{1,15},{2,4},{3,1},{4,6},{5,3},{6,8},{7,5},{8,10},{9,7},{10,... | collective-permute-start | bytes 393224 | tf_op jit(solution)/shard_map/ppermute | solution.py:343
  51.6 1.3 %collective-permute-start.25 = (bf16[1,8,8192]{2,1,0:T(8,128)(2,1)S(1)}, bf16[1,8,8192]{2,1,0:T(8,128)(2,1)S(1)}, u32[]{:S(2)}, u32[]{:S(2)}) collective-permute-start(bf16[1,8,8192]{2,1,0:T(8,128)(2,1)S(1)} %collective-permute-done.21.refs_8_.refs_3_), channel_id=1, source_target_pairs={{0,2},{1,15},{2,4},{3,1},{4,6},{5,3},{6,8},{7,5},{8,10},{9,7},{10,... | collective-permute-start | bytes 393224 | tf_op jit(solution)/shard_map/ppermute | solution.py:343
  52.9 2.3 %collective-permute-start.16 = (bf16[1,8,8192]{2,1,0:T(8,128)(2,1)S(1)}, bf16[1,8,8192]{2,1,0:T(8,128)(2,1)S(1)}, u32[]{:S(2)}, u32[]{:S(2)}) collective-permute-start(bf16[1,8,8192]{2,1,0:T(8,128)(2,1)S(1)} %collective-permute-done.15.refs_10_.refs_4_), channel_id=1, source_target_pairs={{0,2},{1,15},{2,4},{3,1},{4,6},{5,3},{6,8},{7,5},{8,10},{9,7},{10,... | collective-permute-start | bytes 393224 | tf_op jit(solution)/shard_map/ppermute | solution.py:343
  55.3 1.4 %collective-permute-start.27 = (bf16[1,8,8192]{2,1,0:T(8,128)(2,1)S(1)}, bf16[1,8,8192]{2,1,0:T(8,128)(2,1)S(1)}, u32[]{:S(2)}, u32[]{:S(2)}) collective-permute-start(bf16[1,8,8192]{2,1,0:T(8,128)(2,1)S(1)} %collective-permute-done.24.refs_12_.refs_6_), channel_id=1, source_target_pairs={{0,2},{1,15},{2,4},{3,1},{4,6},{5,3},{6,8},{7,5},{8,10},{9,7},{10,... | collective-permute-start | bytes 393224 | tf_op jit(solution)/shard_map/ppermute | solution.py:343
  56.7 0.6 collective-permute-done.25.refs_13_.refs_7_
  57.3 3.6 %collective-permute-start.30 = (bf16[8,8,8192]{2,1,0:T(8,128)(2,1)S(1)}, bf16[8,8,8192]{2,1,0:T(8,128)(2,1)S(1)}, u32[]{:S(2)}, u32[]{:S(2)}) collective-permute-start(bf16[8,8,8192]{2,1,0:T(8,128)(2,1)S(1)} %shard_map.58), channel_id=1, source_target_pairs={{0,1},{1,0},{2,3},{3,2},{4,5},{5,4},{6,7},{7,6},{8,9},{9,8},{10,11... | collective-permute-start | bytes 3145736 | tf_op jit(solution)/shard_map/ppermute | solution.py:346
  61.0 0.5 collective-permute-start.26
  61.5 0.3 collective-permute-start.17
  61.8 1.3 %collective-permute-start.28 = (bf16[1,8,8192]{2,1,0:T(8,128)(2,1)S(1)}, bf16[1,8,8192]{2,1,0:T(8,128)(2,1)S(1)}, u32[]{:S(2)}, u32[]{:S(2)}) collective-permute-start(bf16[1,8,8192]{2,1,0:T(8,128)(2,1)S(1)} %collective-permute-done.25.refs_13_.refs_7_), channel_id=1, source_target_pairs={{0,2},{1,15},{2,4},{3,1},{4,6},{5,3},{6,8},{7,5},{8,10},{9,7},{10,... | collective-permute-start | bytes 393224 | tf_op jit(solution)/shard_map/ppermute | solution.py:343
  63.2 3.0 %collective-permute-start.29 = (bf16[1,8,8192]{2,1,0:T(8,128)(2,1)S(1)}, bf16[1,8,8192]{2,1,0:T(8,128)(2,1)S(1)}, u32[]{:S(2)}, u32[]{:S(2)}) collective-permute-start(bf16[1,8,8192]{2,1,0:T(8,128)(2,1)S(1)} %shard_map.57), channel_id=1, source_target_pairs={{0,2},{1,15},{2,4},{3,1},{4,6},{5,3},{6,8},{7,5},{8,10},{9,7},{10,... | collective-permute-start | bytes 393224 | tf_op jit(solution)/shard_map/ppermute | solution.py:343
  66.2 0.3 collective-permute-done.17.refs_0_.refs_5_.refs_4_
  66.5 1.3 %shard_map.56 = (bf16[1,8,16384]{2,1,0:T(8,128)(2,1)}, f32[8,128]{1,0:T(8,128)S(1)}, bf16[16,8,16384]{2,1,0:T(8,128)(2,1)}) custom-call(bf16[1,8,8192]{2,1,0:T(8,128)(2,1)S(1)} %collective-permute-done.17.refs_0_.refs_5_.refs_4_, bf16[1,8,8192]{2,1,0:T(8,128)(2,1)S(1)} %get-tuple-element.47.refs_1_, bf16[1,8,8192]{2,1,0:T(8,128)(2,1)S(1)} %get-tuple-element.48.refs_2_, ...), custom_call_target="tpu_custom_call" | custom-call | flops 1 | bytes 1 | tf_op jit(solution)/shard_map/pallas_call | solution.py:324
  67.9 1.4 %collective-permute-done.29.refs_6_.refs_5_ = bf16[1,8,8192]{2,1,0:T(8,128)(2,1)S(1)} collective-permute-done((bf16[1,8,8192]{2,1,0:T(8,128)(2,1)S(1)}, bf16[1,8,8192]{2,1,0:T(8,128)(2,1)S(1)}, u32[]{:S(2)}, u32[]{:S(2)}) %collective-permute-start.29) | collective-permute-done | bytes 131104 | tf_op jit(solution)/shard_map/ppermute | solution.py:343
  69.3 2.6 %collective-permute-start.31 = (bf16[6,8,8192]{2,1,0:T(8,128)(2,1)S(1)}, bf16[6,8,8192]{2,1,0:T(8,128)(2,1)S(1)}, u32[]{:S(2)}, u32[]{:S(2)}) collective-permute-start(bf16[6,8,8192]{2,1,0:T(8,128)(2,1)S(1)} %shard_map.60), channel_id=1, source_target_pairs={{0,1},{1,0},{2,3},{3,2},{4,5},{5,4},{6,7},{7,6},{8,9},{9,8},{10,11... | collective-permute-start | bytes 2359304 | tf_op jit(solution)/shard_map/ppermute | solution.py:346
  72.0 1.9 %shard_map.59 = (f32[8,128]{1,0:T(8,128)}, bf16[16,8,16384]{2,1,0:T(8,128)(2,1)}) custom-call(bf16[16,8,16384]{2,1,0:T(8,128)(2,1)} %get-tuple-element.53.refs_0_, bf16[1,8,8192]{2,1,0:T(8,128)(2,1)S(1)} %collective-permute-done.16.refs_1_.refs_0_, bf16[1,8,8192]{2,1,0:T(8,128)(2,1)S(1)} %collective-permute-done.26.refs_2_.refs_1_, ...), custom_call_target="tpu_custom_call", output_to_operand_aliasing={{1}: (0, {})} | custom-call | flops 1 | bytes 1 | tf_op jit(solution)/shard_map/pallas_call | solution.py:324
  73.9 1.5 %shard_map.61 = (f32[8,128]{1,0:T(8,128)}, bf16[16,8,16384]{2,1,0:T(8,128)(2,1)}) custom-call(bf16[16,8,16384]{2,1,0:T(8,128)(2,1)} %get-tuple-element.54.refs_0_, bf16[6,8,8192]{2,1,0:T(8,128)(2,1)S(1)} %collective-permute-done.31.refs_1_), custom_call_target="tpu_custom_call", output_to_operand_aliasing={{1}: (0, {})} | custom-call | flops 1 | bytes 1 | tf_op jit(solution)/shard_map/pallas_call | solution.py:324
  (37 shorter events, 0.8 us)
Async XLA Ops:
  4.4 10.5 %collective-permute-start.3 = (bf16[2,16,8192]{2,1,0:T(8,128)(2,1)S(1)}, bf16[2,16,8192]{2,1,0:T(8,128)(2,1)S(1)}, u32[]{:S(2)}, u32[]{:S(2)}) collective-permute-start(bf16[2,16,8192]{2,1,0:T(8,128)(2,1)S(1)} %get-tuple-element.33._), channel_id=1, source_target_pairs={{0,1},{1,0},{2,3},{3,2},{4,5},{5,4},{6,7},{7,6},{8,9},{9,8},{10,11... | collective-permute-start | bytes 1572872 | tf_op jit(solution)/shard_map/ppermute | solution.py:346
  7.7 1.9 %collective-permute-start.4 = (bf16[1,16,8192]{2,1,0:T(8,128)(2,1)S(1)}, bf16[1,16,8192]{2,1,0:T(8,128)(2,1)S(1)}, u32[]{:S(2)}, u32[]{:S(2)}) collective-permute-start(bf16[1,16,8192]{2,1,0:T(8,128)(2,1)S(1)} %get-tuple-element.32._), channel_id=1, source_target_pairs={{0,1},{1,0},{2,3},{3,2},{4,5},{5,4},{6,7},{7,6},{8,9},{9,8},{10,11... | collective-permute-start | bytes 786440 | tf_op jit(solution)/shard_map/ppermute | solution.py:346
  9.1 11.1 %collective-permute-start.2 = (bf16[2,16,8192]{2,1,0:T(8,128)(2,1)S(1)}, bf16[2,16,8192]{2,1,0:T(8,128)(2,1)S(1)}, u32[]{:S(2)}, u32[]{:S(2)}) collective-permute-start(bf16[2,16,8192]{2,1,0:T(8,128)(2,1)S(1)} %get-tuple-element.34._), channel_id=1, source_target_pairs={{0,1},{1,0},{2,3},{3,2},{4,5},{5,4},{6,7},{7,6},{8,9},{9,8},{10,11... | collective-permute-start | bytes 1572872 | tf_op jit(solution)/shard_map/ppermute | solution.py:346
  9.7 7.2 %collective-permute-start.5 = (bf16[16,8192]{1,0:T(8,128)(2,1)S(1)}, bf16[16,8192]{1,0:T(8,128)(2,1)S(1)}, u32[]{:S(2)}, u32[]{:S(2)}) collective-permute-start(bf16[16,8192]{1,0:T(8,128)(2,1)S(1)} %shard_map.46), channel_id=1, source_target_pairs={{0,2},{1,15},{2,4},{3,1},{4,6},{5,3},{6,8},{7,5},{8,10},{9,7},{10,... | collective-permute-start | bytes 786440 | tf_op jit(solution)/shard_map/ppermute | solution.py:343
  15.0 5.6 %collective-permute-start.9 = (bf16[16,8192]{1,0:T(8,128)(2,1)S(1)}, bf16[16,8192]{1,0:T(8,128)(2,1)S(1)}, u32[]{:S(2)}, u32[]{:S(2)}) collective-permute-start(bf16[16,8192]{1,0:T(8,128)(2,1)S(1)} %shard_map.50), channel_id=1, source_target_pairs={{0,2},{1,15},{2,4},{3,1},{4,6},{5,3},{6,8},{7,5},{8,10},{9,7},{10,... | collective-permute-start | bytes 786440 | tf_op jit(solution)/shard_map/ppermute | solution.py:343
  15.8 12.2 %collective-permute-start.1 = (bf16[2,16,8192]{2,1,0:T(8,128)(2,1)S(1)}, bf16[2,16,8192]{2,1,0:T(8,128)(2,1)S(1)}, u32[]{:S(2)}, u32[]{:S(2)}) collective-permute-start(bf16[2,16,8192]{2,1,0:T(8,128)(2,1)S(1)} %get-tuple-element.35._), channel_id=1, source_target_pairs={{0,1},{1,0},{2,3},{3,2},{4,5},{5,4},{6,7},{7,6},{8,9},{9,8},{10,11... | collective-permute-start | bytes 1572872 | tf_op jit(solution)/shard_map/ppermute | solution.py:346
  17.0 6.5 %collective-permute-start.6 = (bf16[16,8192]{1,0:T(8,128)(2,1)S(1)}, bf16[16,8192]{1,0:T(8,128)(2,1)S(1)}, u32[]{:S(2)}, u32[]{:S(2)}) collective-permute-start(bf16[16,8192]{1,0:T(8,128)(2,1)S(1)} %shard_map.47), channel_id=1, source_target_pairs={{0,2},{1,15},{2,4},{3,1},{4,6},{5,3},{6,8},{7,5},{8,10},{9,7},{10,... | collective-permute-start | bytes 786440 | tf_op jit(solution)/shard_map/ppermute | solution.py:343
  20.7 7.3 %collective-permute-start.10 = (bf16[16,8192]{1,0:T(8,128)(2,1)S(1)}, bf16[16,8192]{1,0:T(8,128)(2,1)S(1)}, u32[]{:S(2)}, u32[]{:S(2)}) collective-permute-start(bf16[16,8192]{1,0:T(8,128)(2,1)S(1)} %shard_map.51), channel_id=1, source_target_pairs={{0,2},{1,15},{2,4},{3,1},{4,6},{5,3},{6,8},{7,5},{8,10},{9,7},{10,... | collective-permute-start | bytes 786440 | tf_op jit(solution)/shard_map/ppermute | solution.py:343
  23.7 8.6 %collective-permute-start.7 = (bf16[16,8192]{1,0:T(8,128)(2,1)S(1)}, bf16[16,8192]{1,0:T(8,128)(2,1)S(1)}, u32[]{:S(2)}, u32[]{:S(2)}) collective-permute-start(bf16[16,8192]{1,0:T(8,128)(2,1)S(1)} %shard_map.48), channel_id=1, source_target_pairs={{0,2},{1,15},{2,4},{3,1},{4,6},{5,3},{6,8},{7,5},{8,10},{9,7},{10,... | collective-permute-start | bytes 786440 | tf_op jit(solution)/shard_map/ppermute | solution.py:343
  27.9 9.5 %collective-permute-start = (bf16[2,8,8192]{2,1,0:T(8,128)(2,1)S(1)}, bf16[2,8,8192]{2,1,0:T(8,128)(2,1)S(1)}, u32[]{:S(2)}, u32[]{:S(2)}) collective-permute-start(bf16[2,8,8192]{2,1,0:T(8,128)(2,1)S(1)} %get-tuple-element.38), channel_id=1, source_target_pairs={{0,1},{1,0},{2,3},{3,2},{4,5},{5,4},{6,7},{7,6},{8,9},{9,8},{10,11... | collective-permute-start | bytes 786440 | tf_op jit(solution)/shard_map/ppermute | solution.py:346
  28.2 9.2 %collective-permute-start.11 = (bf16[1,8,8192]{2,1,0:T(8,128)(2,1)S(1)}, bf16[1,8,8192]{2,1,0:T(8,128)(2,1)S(1)}, u32[]{:S(2)}, u32[]{:S(2)}) collective-permute-start(bf16[1,8,8192]{2,1,0:T(8,128)(2,1)S(1)} %get-tuple-element.44), channel_id=1, source_target_pairs={{0,2},{1,15},{2,4},{3,1},{4,6},{5,3},{6,8},{7,5},{8,10},{9,7},{10,... | collective-permute-start | bytes 393224 | tf_op jit(solution)/shard_map/ppermute | solution.py:343
  30.9 6.5 %collective-permute-start.13 = (bf16[1,8,8192]{2,1,0:T(8,128)(2,1)S(1)}, bf16[1,8,8192]{2,1,0:T(8,128)(2,1)S(1)}, u32[]{:S(2)}, u32[]{:S(2)}) collective-permute-start(bf16[1,8,8192]{2,1,0:T(8,128)(2,1)S(1)} %get-tuple-element.46), channel_id=1, source_target_pairs={{0,3},{1,14},{2,5},{3,0},{4,7},{5,2},{6,9},{7,4},{8,11},{9,6},{10,... | collective-permute-start | bytes 393224 | tf_op jit(solution)/shard_map/ppermute | solution.py:343
  32.4 5.0 %collective-permute-start.8 = (bf16[1,8,8192]{2,1,0:T(8,128)(2,1)S(1)}, bf16[1,8,8192]{2,1,0:T(8,128)(2,1)S(1)}, u32[]{:S(2)}, u32[]{:S(2)}) collective-permute-start(bf16[1,8,8192]{2,1,0:T(8,128)(2,1)S(1)} %get-tuple-element.43), channel_id=1, source_target_pairs={{0,2},{1,15},{2,4},{3,1},{4,6},{5,3},{6,8},{7,5},{8,10},{9,7},{10,... | collective-permute-start | bytes 393224 | tf_op jit(solution)/shard_map/ppermute | solution.py:343
  33.7 7.8 %collective-permute-start.12 = (bf16[1,8,8192]{2,1,0:T(8,128)(2,1)S(1)}, bf16[1,8,8192]{2,1,0:T(8,128)(2,1)S(1)}, u32[]{:S(2)}, u32[]{:S(2)}) collective-permute-start(bf16[1,8,8192]{2,1,0:T(8,128)(2,1)S(1)} %get-tuple-element.45), channel_id=1, source_target_pairs={{0,3},{1,14},{2,5},{3,0},{4,7},{5,2},{6,9},{7,4},{8,11},{9,6},{10,... | collective-permute-start | bytes 393224 | tf_op jit(solution)/shard_map/ppermute | solution.py:343
  41.9 1.8 %collective-permute-start.18 = (bf16[2,8,8192]{2,1,0:T(8,128)(2,1)S(1)}, bf16[2,8,8192]{2,1,0:T(8,128)(2,1)S(1)}, u32[]{:S(2)}, u32[]{:S(2)}) collective-permute-start(bf16[2,8,8192]{2,1,0:T(8,128)(2,1)S(1)} %get-tuple-element.49), channel_id=1, source_target_pairs={{0,1},{1,0},{2,3},{3,2},{4,5},{5,4},{6,7},{7,6},{8,9},{9,8},{10,11... | collective-permute-start | bytes 786440 | tf_op jit(solution)/shard_map/ppermute | solution.py:346
  42.0 5.3 %collective-permute-start.14 = (bf16[1,8,8192]{2,1,0:T(8,128)(2,1)S(1)}, bf16[1,8,8192]{2,1,0:T(8,128)(2,1)S(1)}, u32[]{:S(2)}, u32[]{:S(2)}) collective-permute-start(bf16[1,8,8192]{2,1,0:T(8,128)(2,1)S(1)} %get-tuple-element.47.refs_1_), channel_id=1, source_target_pairs={{0,2},{1,15},{2,4},{3,1},{4,6},{5,3},{6,8},{7,5},{8,10},{9,7},{10,... | collective-permute-start | bytes 393224 | tf_op jit(solution)/shard_map/ppermute | solution.py:343
  43.7 5.2 %collective-permute-start.20 = (bf16[1,8,8192]{2,1,0:T(8,128)(2,1)S(1)}, bf16[1,8,8192]{2,1,0:T(8,128)(2,1)S(1)}, u32[]{:S(2)}, u32[]{:S(2)}) collective-permute-start(bf16[1,8,8192]{2,1,0:T(8,128)(2,1)S(1)} %get-tuple-element.50.refs_3_), channel_id=1, source_target_pairs={{0,2},{1,15},{2,4},{3,1},{4,6},{5,3},{6,8},{7,5},{8,10},{9,7},{10,... | collective-permute-start | bytes 393224 | tf_op jit(solution)/shard_map/ppermute | solution.py:343
  45.0 6.6 %collective-permute-start.19 = (bf16[1,8,8192]{2,1,0:T(8,128)(2,1)S(1)}, bf16[1,8,8192]{2,1,0:T(8,128)(2,1)S(1)}, u32[]{:S(2)}, u32[]{:S(2)}) collective-permute-start(bf16[1,8,8192]{2,1,0:T(8,128)(2,1)S(1)} %get-tuple-element.48.refs_2_), channel_id=1, source_target_pairs={{0,2},{1,15},{2,4},{3,1},{4,6},{5,3},{6,8},{7,5},{8,10},{9,7},{10,... | collective-permute-start | bytes 393224 | tf_op jit(solution)/shard_map/ppermute | solution.py:343
  45.1 6.5 %collective-permute-start.21 = (bf16[1,8,8192]{2,1,0:T(8,128)(2,1)S(1)}, bf16[1,8,8192]{2,1,0:T(8,128)(2,1)S(1)}, u32[]{:S(2)}, u32[]{:S(2)}) collective-permute-start(bf16[1,8,8192]{2,1,0:T(8,128)(2,1)S(1)} %get-tuple-element.51.refs_4_), channel_id=1, source_target_pairs={{0,2},{1,15},{2,4},{3,1},{4,6},{5,3},{6,8},{7,5},{8,10},{9,7},{10,... | collective-permute-start | bytes 393224 | tf_op jit(solution)/shard_map/ppermute | solution.py:343
  47.4 5.6 %collective-permute-start.15 = (bf16[1,8,8192]{2,1,0:T(8,128)(2,1)S(1)}, bf16[1,8,8192]{2,1,0:T(8,128)(2,1)S(1)}, u32[]{:S(2)}, u32[]{:S(2)}) collective-permute-start(bf16[1,8,8192]{2,1,0:T(8,128)(2,1)S(1)} %collective-permute-done.14.refs_5_.refs_0_), channel_id=1, source_target_pairs={{0,2},{1,15},{2,4},{3,1},{4,6},{5,3},{6,8},{7,5},{8,10},{9,7},{10,... | collective-permute-start | bytes 393224 | tf_op jit(solution)/shard_map/ppermute | solution.py:343
  49.0 12.9 %collective-permute-start.22 = (bf16[2,8,8192]{2,1,0:T(8,128)(2,1)S(1)}, bf16[2,8,8192]{2,1,0:T(8,128)(2,1)S(1)}, u32[]{:S(2)}, u32[]{:S(2)}) collective-permute-start(bf16[2,8,8192]{2,1,0:T(8,128)(2,1)S(1)} %shard_map.55), channel_id=1, source_target_pairs={{0,16},{16,32},{32,48},{48,64},{64,80},{80,96},{96,112},{112,128},... | collective-permute-start | bytes 786440 | tf_op jit(solution)/shard_map/ppermute | solution.py:384
  50.3 4.9 %collective-permute-start.24 = (bf16[1,8,8192]{2,1,0:T(8,128)(2,1)S(1)}, bf16[1,8,8192]{2,1,0:T(8,128)(2,1)S(1)}, u32[]{:S(2)}, u32[]{:S(2)}) collective-permute-start(bf16[1,8,8192]{2,1,0:T(8,128)(2,1)S(1)} %collective-permute-done.20.refs_1_.refs_7_.refs_2_), channel_id=1, source_target_pairs={{0,2},{1,15},{2,4},{3,1},{4,6},{5,3},{6,8},{7,5},{8,10},{9,7},{10,... | collective-permute-start | bytes 393224 | tf_op jit(solution)/shard_map/ppermute | solution.py:343
  51.5 5.2 %collective-permute-start.23 = (bf16[1,8,8192]{2,1,0:T(8,128)(2,1)S(1)}, bf16[1,8,8192]{2,1,0:T(8,128)(2,1)S(1)}, u32[]{:S(2)}, u32[]{:S(2)}) collective-permute-start(bf16[1,8,8192]{2,1,0:T(8,128)(2,1)S(1)} %collective-permute-done.19.refs_6_.refs_1_), channel_id=1, source_target_pairs={{0,2},{1,15},{2,4},{3,1},{4,6},{5,3},{6,8},{7,5},{8,10},{9,7},{10,... | collective-permute-start | bytes 393224 | tf_op jit(solution)/shard_map/ppermute | solution.py:343
  51.6 5.7 %collective-permute-start.25 = (bf16[1,8,8192]{2,1,0:T(8,128)(2,1)S(1)}, bf16[1,8,8192]{2,1,0:T(8,128)(2,1)S(1)}, u32[]{:S(2)}, u32[]{:S(2)}) collective-permute-start(bf16[1,8,8192]{2,1,0:T(8,128)(2,1)S(1)} %collective-permute-done.21.refs_8_.refs_3_), channel_id=1, source_target_pairs={{0,2},{1,15},{2,4},{3,1},{4,6},{5,3},{6,8},{7,5},{8,10},{9,7},{10,... | collective-permute-start | bytes 393224 | tf_op jit(solution)/shard_map/ppermute | solution.py:343
  52.9 8.5 %collective-permute-start.16 = (bf16[1,8,8192]{2,1,0:T(8,128)(2,1)S(1)}, bf16[1,8,8192]{2,1,0:T(8,128)(2,1)S(1)}, u32[]{:S(2)}, u32[]{:S(2)}) collective-permute-start(bf16[1,8,8192]{2,1,0:T(8,128)(2,1)S(1)} %collective-permute-done.15.refs_10_.refs_4_), channel_id=1, source_target_pairs={{0,2},{1,15},{2,4},{3,1},{4,6},{5,3},{6,8},{7,5},{8,10},{9,7},{10,... | collective-permute-start | bytes 393224 | tf_op jit(solution)/shard_map/ppermute | solution.py:343
  55.3 7.9 %collective-permute-start.27 = (bf16[1,8,8192]{2,1,0:T(8,128)(2,1)S(1)}, bf16[1,8,8192]{2,1,0:T(8,128)(2,1)S(1)}, u32[]{:S(2)}, u32[]{:S(2)}) collective-permute-start(bf16[1,8,8192]{2,1,0:T(8,128)(2,1)S(1)} %collective-permute-done.24.refs_12_.refs_6_), channel_id=1, source_target_pairs={{0,2},{1,15},{2,4},{3,1},{4,6},{5,3},{6,8},{7,5},{8,10},{9,7},{10,... | collective-permute-start | bytes 393224 | tf_op jit(solution)/shard_map/ppermute | solution.py:343
  57.3 14.6 %collective-permute-start.30 = (bf16[8,8,8192]{2,1,0:T(8,128)(2,1)S(1)}, bf16[8,8,8192]{2,1,0:T(8,128)(2,1)S(1)}, u32[]{:S(2)}, u32[]{:S(2)}) collective-permute-start(bf16[8,8,8192]{2,1,0:T(8,128)(2,1)S(1)} %shard_map.58), channel_id=1, source_target_pairs={{0,1},{1,0},{2,3},{3,2},{4,5},{5,4},{6,7},{7,6},{8,9},{9,8},{10,11... | collective-permute-start | bytes 3145736 | tf_op jit(solution)/shard_map/ppermute | solution.py:346
  61.0 6.9 %collective-permute-start.26 = (bf16[1,8,8192]{2,1,0:T(8,128)(2,1)S(1)}, bf16[1,8,8192]{2,1,0:T(8,128)(2,1)S(1)}, u32[]{:S(2)}, u32[]{:S(2)}) collective-permute-start(bf16[1,8,8192]{2,1,0:T(8,128)(2,1)S(1)} %collective-permute-done.23.refs_11_.refs_5_), channel_id=1, source_target_pairs={{0,2},{1,15},{2,4},{3,1},{4,6},{5,3},{6,8},{7,5},{8,10},{9,7},{10,... | collective-permute-start | bytes 393224 | tf_op jit(solution)/shard_map/ppermute | solution.py:343
  61.5 5.0 %collective-permute-start.17 = (bf16[1,8,8192]{2,1,0:T(8,128)(2,1)S(1)}, bf16[1,8,8192]{2,1,0:T(8,128)(2,1)S(1)}, u32[]{:S(2)}, u32[]{:S(2)}) collective-permute-start(bf16[1,8,8192]{2,1,0:T(8,128)(2,1)S(1)} %collective-permute-done.16.refs_1_.refs_0_), channel_id=1, source_target_pairs={{0,2},{1,15},{2,4},{3,1},{4,6},{5,3},{6,8},{7,5},{8,10},{9,7},{10,... | collective-permute-start | bytes 393224 | tf_op jit(solution)/shard_map/ppermute | solution.py:343
  61.8 6.0 %collective-permute-start.28 = (bf16[1,8,8192]{2,1,0:T(8,128)(2,1)S(1)}, bf16[1,8,8192]{2,1,0:T(8,128)(2,1)S(1)}, u32[]{:S(2)}, u32[]{:S(2)}) collective-permute-start(bf16[1,8,8192]{2,1,0:T(8,128)(2,1)S(1)} %collective-permute-done.25.refs_13_.refs_7_), channel_id=1, source_target_pairs={{0,2},{1,15},{2,4},{3,1},{4,6},{5,3},{6,8},{7,5},{8,10},{9,7},{10,... | collective-permute-start | bytes 393224 | tf_op jit(solution)/shard_map/ppermute | solution.py:343
  63.2 6.1 %collective-permute-start.29 = (bf16[1,8,8192]{2,1,0:T(8,128)(2,1)S(1)}, bf16[1,8,8192]{2,1,0:T(8,128)(2,1)S(1)}, u32[]{:S(2)}, u32[]{:S(2)}) collective-permute-start(bf16[1,8,8192]{2,1,0:T(8,128)(2,1)S(1)} %shard_map.57), channel_id=1, source_target_pairs={{0,2},{1,15},{2,4},{3,1},{4,6},{5,3},{6,8},{7,5},{8,10},{9,7},{10,... | collective-permute-start | bytes 393224 | tf_op jit(solution)/shard_map/ppermute | solution.py:343
  69.3 4.6 %collective-permute-start.31 = (bf16[6,8,8192]{2,1,0:T(8,128)(2,1)S(1)}, bf16[6,8,8192]{2,1,0:T(8,128)(2,1)S(1)}, u32[]{:S(2)}, u32[]{:S(2)}) collective-permute-start(bf16[6,8,8192]{2,1,0:T(8,128)(2,1)S(1)} %shard_map.60), channel_id=1, source_target_pairs={{0,1},{1,0},{2,3},{3,2},{4,5},{5,4},{6,7},{7,6},{8,9},{9,8},{10,11... | collective-permute-start | bytes 2359304 | tf_op jit(solution)/shard_map/ppermute | solution.py:346

commit v4 on v3

--- a/solution.py
+++ b/solution.py
@@ -59,8 +59,7 @@
     return wide - (wide - nudged)
 
 
-def coded_half(held, slot, store):
-    h = hadamard()
+def coded_half(h, held, slot, store):
     for start in range(0, HALF, UNIT):
         cols = range(start, start + UNIT, BLOCK)
         x = jnp.concatenate([held[slot, :, b : b + BLOCK] for b in cols], axis=0)
@@ -70,13 +69,13 @@
             store(b // COLS, at, values[i * GROUP : (i + 1) * GROUP])
 
 
-def code_group(held, group, out, first, halves):
+def code_group(h, held, group, out, first, halves):
     for i in range(halves):
 
         def store(piece, at, values, base=i * PIECES):
             out[base + piece, :, at] = values.astype(jnp.bfloat16)
 
-        coded_half(held, 2 * group + (first + i) % 2, store)
+        coded_half(h, held, 2 * group + (first + i) % 2, store)
 
 
 def far_kernel(x_ref, stream_ref, keep, send, held, rows, arrived):
@@ -98,10 +97,11 @@
         copies.append(fetch(stream_ref, chip, half, rows.at[half], len(copies)))
     for copy in copies:
         copy.start()
+    h = hadamard()
     for copy in copies[:2]:
         copy.wait()
-    code_group(held, far, keep, core, 1)
-    code_group(held, far, send, 1 - core, 1)
+    code_group(h, held, far, keep, core, 1)
+    code_group(h, held, far, send, 1 - core, 1)
     for copy in copies[2:]:
         copy.wait()
 
@@ -123,8 +123,9 @@
 
 def code_kernel(k, held, keep, send):
     chip, core, way = position()
-    code_group(held, chip_at(chip, way * k), keep, core, 2)
-    code_group(held, chip_at(chip, -way * k), send, 1 - core, 2)
+    h = hadamard()
+    code_group(h, held, chip_at(chip, way * k), keep, core, 2)
+    code_group(h, held, chip_at(chip, -way * k), send, 1 - core, 2)
 
 
 def code_rows(held, k, after):
@@ -142,6 +143,7 @@
 def own_kernel(held, stream, near_ref, send_ref, rows_ref):
     chip, core, _ = position()
     first = core == 0
+    h = hadamard()
     for half in range(2):
 
         def store(piece, at, values, half=half):
@@ -151,7 +153,7 @@
             near_ref[((half + core) % 2) * PIECES + piece, :, at] = mine
             send_ref[((half + 1 - core) % 2) * PIECES + piece, :, at] = theirs
 
-        coded_half(held, 2 * chip + half, store)
+        coded_half(h, held, 2 * chip + half, store)
         for i in range(PIECES):
             rows = stream[half, :, i * COLS : (i + 1) * COLS].astype(jnp.float32)
             rows = jnp.where(first, rows[:OWN], rows[OWN:])

time: 75.7 us -> 75.7 us (level)
  no operation moved by 1% of the time
where the time goes in v4:
time: 75.7 us; the launch traced here: 75.6 us
  starting transfers between devices  52.9 us (70%)
  Pallas kernels  13.3 us (18%)
  waiting for transfers between devices  8.42 us (11%)
  between operations  1.02 us (1%)
    ppermute x23, starting transfers between devices, onward(): lax.ppermute(block, 'tp', [(i, j ^ 1) if cross else (i, j) for i, j in ro...  41.1 us
    ppermute x8, starting transfers between devices, other_core(): return lax.ppermute(block, 'tp', [(i, i ^ 1) for i in range(n)])  10.4 us
    ppermute x23, waiting for transfers between devices, onward(): lax.ppermute(block, 'tp', [(i, j ^ 1) if cross else (i, j) for i, j in ro...  8.38 us
    pallas_call x3, Pallas kernels, put(): pl.pallas_call(lambda *refs: put_kernel(places, len(held) + len(after), *...  4.79 us
    pallas_call x3, Pallas kernels, code_rows(): pl.pallas_call(lambda held_ref, _, *refs: code_kernel(k, held_ref, *refs)...  3.85 us
    pallas_call x1, Pallas kernels, code_far(): pl.pallas_call(far_kernel, out_shape=(part, part, whole, rows), in_specs=...  2.47 us
  transfers between devices with their start and end apart: 32, of which 8 were waited for; matrix products, arithmetic and copies ran while one was open for 0% of the time, Pallas kernels for 10%

profile of v4, /device:TPU:1, one launch (start us, length us, event | category | flops | bytes accessed | tf_op | source)
XLA Modules:
  0.0 75.6 jit_solution(1231814948221020712)
XLA Ops:
  0.6 2.5 %shard_map.41 = (bf16[1,16,8192]{2,1,0:T(8,128)(2,1)S(1)}, bf16[1,16,8192]{2,1,0:T(8,128)(2,1)S(1)}, bf16[16,16,8192]{2,1,0:T(8,128)(2,1)S(1)}, bf16[2,16,8192]{2,1,0:T(8,128)(2,1)S(1)}) custom-call(bf16[128,16384]{1,0:T(8,128)(2,1)} %bitcast.4, bf16[128,16384]{1,0:T(8,128)(2,1)} %bitcast.5), custom_call_target="tpu_custom_call" | custom-call | flops 1 | bytes 1 | tf_op jit(solution)/shard_map/pallas_call | solution.py:113
  3.1 1.3 %shard_map.42 = (bf16[2,16,8192]{2,1,0:T(8,128)(2,1)S(1)}, bf16[2,16,8192]{2,1,0:T(8,128)(2,1)S(1)}) custom-call(bf16[16,16,8192]{2,1,0:T(8,128)(2,1)S(1)} %get-tuple-element.30.held_ref, bf16[1,16,8192]{2,1,0:T(8,128)(2,1)S(1)} %get-tuple-element.32._), custom_call_target="tpu_custom_call" | custom-call | flops 1 | bytes 1 | tf_op jit(solution)/shard_map/pallas_call | solution.py:133
  4.4 3.3 %collective-permute-start.3 = (bf16[2,16,8192]{2,1,0:T(8,128)(2,1)S(1)}, bf16[2,16,8192]{2,1,0:T(8,128)(2,1)S(1)}, u32[]{:S(2)}, u32[]{:S(2)}) collective-permute-start(bf16[2,16,8192]{2,1,0:T(8,128)(2,1)S(1)} %get-tuple-element.33._), channel_id=1, source_target_pairs={{0,1},{1,0},{2,3},{3,2},{4,5},{5,4},{6,7},{7,6},{8,9},{9,8},{10,11... | collective-permute-start | bytes 1572872 | tf_op jit(solution)/shard_map/ppermute | solution.py:348
  7.7 0.1 collective-permute-start.4
  7.8 1.3 %shard_map.43 = (bf16[2,16,8192]{2,1,0:T(8,128)(2,1)S(1)}, bf16[2,16,8192]{2,1,0:T(8,128)(2,1)S(1)}) custom-call(bf16[16,16,8192]{2,1,0:T(8,128)(2,1)S(1)} %get-tuple-element.30.held_ref, bf16[2,16,8192]{2,1,0:T(8,128)(2,1)S(1)} %get-tuple-element.33._), custom_call_target="tpu_custom_call" | custom-call | flops 1 | bytes 1 | tf_op jit(solution)/shard_map/pallas_call | solution.py:133
  9.1 0.5 collective-permute-start.2
  9.7 3.9 %collective-permute-start.5 = (bf16[16,8192]{1,0:T(8,128)(2,1)S(1)}, bf16[16,8192]{1,0:T(8,128)(2,1)S(1)}, u32[]{:S(2)}, u32[]{:S(2)}) collective-permute-start(bf16[16,8192]{1,0:T(8,128)(2,1)S(1)} %shard_map.46), channel_id=1, source_target_pairs={{0,2},{1,15},{2,4},{3,1},{4,6},{5,3},{6,8},{7,5},{8,10},{9,7},{10,... | collective-permute-start | bytes 786440 | tf_op jit(solution)/shard_map/ppermute | solution.py:345
  13.6 1.3 %shard_map.44 = (bf16[2,16,8192]{2,1,0:T(8,128)(2,1)S(1)}, bf16[2,16,8192]{2,1,0:T(8,128)(2,1)S(1)}) custom-call(bf16[16,16,8192]{2,1,0:T(8,128)(2,1)S(1)} %get-tuple-element.30.held_ref, bf16[2,16,8192]{2,1,0:T(8,128)(2,1)S(1)} %get-tuple-element.34._), custom_call_target="tpu_custom_call" | custom-call | flops 1 | bytes 1 | tf_op jit(solution)/shard_map/pallas_call | solution.py:133
  15.0 0.8 %collective-permute-start.9 = (bf16[16,8192]{1,0:T(8,128)(2,1)S(1)}, bf16[16,8192]{1,0:T(8,128)(2,1)S(1)}, u32[]{:S(2)}, u32[]{:S(2)}) collective-permute-start(bf16[16,8192]{1,0:T(8,128)(2,1)S(1)} %shard_map.50), channel_id=1, source_target_pairs={{0,2},{1,15},{2,4},{3,1},{4,6},{5,3},{6,8},{7,5},{8,10},{9,7},{10,... | collective-permute-start | bytes 786440 | tf_op jit(solution)/shard_map/ppermute | solution.py:345
  15.8 1.1 %collective-permute-done.5.refs_2_ = bf16[16,8192]{1,0:T(8,128)(2,1)S(1)} collective-permute-done((bf16[16,8192]{1,0:T(8,128)(2,1)S(1)}, bf16[16,8192]{1,0:T(8,128)(2,1)S(1)}, u32[]{:S(2)}, u32[]{:S(2)}) %collective-permute-start.5) | collective-permute-done | bytes 262176 | tf_op jit(solution)/shard_map/ppermute | solution.py:345
  16.9 0.1 shard_map.47
  17.0 3.2 %collective-permute-start.6 = (bf16[16,8192]{1,0:T(8,128)(2,1)S(1)}, bf16[16,8192]{1,0:T(8,128)(2,1)S(1)}, u32[]{:S(2)}, u32[]{:S(2)}) collective-permute-start(bf16[16,8192]{1,0:T(8,128)(2,1)S(1)} %shard_map.47), channel_id=1, source_target_pairs={{0,2},{1,15},{2,4},{3,1},{4,6},{5,3},{6,8},{7,5},{8,10},{9,7},{10,... | collective-permute-start | bytes 786440 | tf_op jit(solution)/shard_map/ppermute | solution.py:345
  20.2 0.4 collective-permute-done.9.refs_2_
  20.6 0.1 shard_map.51
  20.7 2.3 %collective-permute-start.10 = (bf16[16,8192]{1,0:T(8,128)(2,1)S(1)}, bf16[16,8192]{1,0:T(8,128)(2,1)S(1)}, u32[]{:S(2)}, u32[]{:S(2)}) collective-permute-start(bf16[16,8192]{1,0:T(8,128)(2,1)S(1)} %shard_map.51), channel_id=1, source_target_pairs={{0,2},{1,15},{2,4},{3,1},{4,6},{5,3},{6,8},{7,5},{8,10},{9,7},{10,... | collective-permute-start | bytes 786440 | tf_op jit(solution)/shard_map/ppermute | solution.py:345
  23.0 0.5 collective-permute-done.6.refs_2_
  23.6 0.1 shard_map.48
  23.7 3.4 %collective-permute-start.7 = (bf16[16,8192]{1,0:T(8,128)(2,1)S(1)}, bf16[16,8192]{1,0:T(8,128)(2,1)S(1)}, u32[]{:S(2)}, u32[]{:S(2)}) collective-permute-start(bf16[16,8192]{1,0:T(8,128)(2,1)S(1)} %shard_map.48), channel_id=1, source_target_pairs={{0,2},{1,15},{2,4},{3,1},{4,6},{5,3},{6,8},{7,5},{8,10},{9,7},{10,... | collective-permute-start | bytes 786440 | tf_op jit(solution)/shard_map/ppermute | solution.py:345
  27.0 0.9 %shard_map.45 = (bf16[2,8,8192]{2,1,0:T(8,128)(2,1)S(1)}, bf16[2,8,8192]{2,1,0:T(8,128)(2,1)S(1)}, bf16[2,8,8192]{2,1,0:T(8,128)(2,1)S(1)}) custom-call(bf16[16,16,8192]{2,1,0:T(8,128)(2,1)S(1)} %get-tuple-element.30.held_ref, bf16[2,16,8192]{2,1,0:T(8,128)(2,1)S(1)} %get-tuple-element.31.stream_ref, bf16[2,16,8192]{2,1,0:T(8,128)(2,1)S(1)} %get-tuple-element.35._), custom_call_target="tpu_custom_call" | custom-call | flops 1 | bytes 1 | tf_op jit(solution)/shard_map/pallas_call | solution.py:165
  28.0 0.1 shard_map.52
  28.2 2.7 %collective-permute-start.11 = (bf16[1,8,8192]{2,1,0:T(8,128)(2,1)S(1)}, bf16[1,8,8192]{2,1,0:T(8,128)(2,1)S(1)}, u32[]{:S(2)}, u32[]{:S(2)}) collective-permute-start(bf16[1,8,8192]{2,1,0:T(8,128)(2,1)S(1)} %get-tuple-element.44), channel_id=1, source_target_pairs={{0,2},{1,15},{2,4},{3,1},{4,6},{5,3},{6,8},{7,5},{8,10},{9,7},{10,... | collective-permute-start | bytes 393224 | tf_op jit(solution)/shard_map/ppermute | solution.py:345
  30.9 1.4 %collective-permute-start.13 = (bf16[1,8,8192]{2,1,0:T(8,128)(2,1)S(1)}, bf16[1,8,8192]{2,1,0:T(8,128)(2,1)S(1)}, u32[]{:S(2)}, u32[]{:S(2)}) collective-permute-start(bf16[1,8,8192]{2,1,0:T(8,128)(2,1)S(1)} %get-tuple-element.46), channel_id=1, source_target_pairs={{0,3},{1,14},{2,5},{3,0},{4,7},{5,2},{6,9},{7,4},{8,11},{9,6},{10,... | collective-permute-start | bytes 393224 | tf_op jit(solution)/shard_map/ppermute | solution.py:345
  32.2 0.1 shard_map.49
  32.4 1.3 %collective-permute-start.8 = (bf16[1,8,8192]{2,1,0:T(8,128)(2,1)S(1)}, bf16[1,8,8192]{2,1,0:T(8,128)(2,1)S(1)}, u32[]{:S(2)}, u32[]{:S(2)}) collective-permute-start(bf16[1,8,8192]{2,1,0:T(8,128)(2,1)S(1)} %get-tuple-element.43), channel_id=1, source_target_pairs={{0,2},{1,15},{2,4},{3,1},{4,6},{5,3},{6,8},{7,5},{8,10},{9,7},{10,... | collective-permute-start | bytes 393224 | tf_op jit(solution)/shard_map/ppermute | solution.py:345
  33.7 3.7 %collective-permute-start.12 = (bf16[1,8,8192]{2,1,0:T(8,128)(2,1)S(1)}, bf16[1,8,8192]{2,1,0:T(8,128)(2,1)S(1)}, u32[]{:S(2)}, u32[]{:S(2)}) collective-permute-start(bf16[1,8,8192]{2,1,0:T(8,128)(2,1)S(1)} %get-tuple-element.45), channel_id=1, source_target_pairs={{0,3},{1,14},{2,5},{3,0},{4,7},{5,2},{6,9},{7,4},{8,11},{9,6},{10,... | collective-permute-start | bytes 393224 | tf_op jit(solution)/shard_map/ppermute | solution.py:345
  37.4 4.0 %collective-permute-done.12.cross0 = bf16[1,8,8192]{2,1,0:T(8,128)(2,1)S(1)} collective-permute-done((bf16[1,8,8192]{2,1,0:T(8,128)(2,1)S(1)}, bf16[1,8,8192]{2,1,0:T(8,128)(2,1)S(1)}, u32[]{:S(2)}, u32[]{:S(2)}) %collective-permute-start.12) | collective-permute-done | bytes 131104 | tf_op jit(solution)/shard_map/ppermute | solution.py:345
  41.4 0.5 shard_map.53
  42.0 1.7 %collective-permute-start.14 = (bf16[1,8,8192]{2,1,0:T(8,128)(2,1)S(1)}, bf16[1,8,8192]{2,1,0:T(8,128)(2,1)S(1)}, u32[]{:S(2)}, u32[]{:S(2)}) collective-permute-start(bf16[1,8,8192]{2,1,0:T(8,128)(2,1)S(1)} %get-tuple-element.47.refs_1_), channel_id=1, source_target_pairs={{0,2},{1,15},{2,4},{3,1},{4,6},{5,3},{6,8},{7,5},{8,10},{9,7},{10,... | collective-permute-start | bytes 393224 | tf_op jit(solution)/shard_map/ppermute | solution.py:345
  43.7 1.2 %collective-permute-start.20 = (bf16[1,8,8192]{2,1,0:T(8,128)(2,1)S(1)}, bf16[1,8,8192]{2,1,0:T(8,128)(2,1)S(1)}, u32[]{:S(2)}, u32[]{:S(2)}) collective-permute-start(bf16[1,8,8192]{2,1,0:T(8,128)(2,1)S(1)} %get-tuple-element.50.refs_3_), channel_id=1, source_target_pairs={{0,2},{1,15},{2,4},{3,1},{4,6},{5,3},{6,8},{7,5},{8,10},{9,7},{10,... | collective-permute-start | bytes 393224 | tf_op jit(solution)/shard_map/ppermute | solution.py:345
  45.1 2.3 %collective-permute-start.21 = (bf16[1,8,8192]{2,1,0:T(8,128)(2,1)S(1)}, bf16[1,8,8192]{2,1,0:T(8,128)(2,1)S(1)}, u32[]{:S(2)}, u32[]{:S(2)}) collective-permute-start(bf16[1,8,8192]{2,1,0:T(8,128)(2,1)S(1)} %get-tuple-element.51.refs_4_), channel_id=1, source_target_pairs={{0,2},{1,15},{2,4},{3,1},{4,6},{5,3},{6,8},{7,5},{8,10},{9,7},{10,... | collective-permute-start | bytes 393224 | tf_op jit(solution)/shard_map/ppermute | solution.py:345
  47.4 1.6 %collective-permute-start.15 = (bf16[1,8,8192]{2,1,0:T(8,128)(2,1)S(1)}, bf16[1,8,8192]{2,1,0:T(8,128)(2,1)S(1)}, u32[]{:S(2)}, u32[]{:S(2)}) collective-permute-start(bf16[1,8,8192]{2,1,0:T(8,128)(2,1)S(1)} %collective-permute-done.14.refs_5_.refs_0_), channel_id=1, source_target_pairs={{0,2},{1,15},{2,4},{3,1},{4,6},{5,3},{6,8},{7,5},{8,10},{9,7},{10,... | collective-permute-start | bytes 393224 | tf_op jit(solution)/shard_map/ppermute | solution.py:345
  49.0 1.4 %collective-permute-start.22 = (bf16[2,8,8192]{2,1,0:T(8,128)(2,1)S(1)}, bf16[2,8,8192]{2,1,0:T(8,128)(2,1)S(1)}, u32[]{:S(2)}, u32[]{:S(2)}) collective-permute-start(bf16[2,8,8192]{2,1,0:T(8,128)(2,1)S(1)} %shard_map.55), channel_id=1, source_target_pairs={{0,16},{16,32},{32,48},{48,64},{64,80},{80,96},{96,112},{112,128},... | collective-permute-start | bytes 786440 | tf_op jit(solution)/shard_map/ppermute | solution.py:386
  50.3 1.2 %collective-permute-start.24 = (bf16[1,8,8192]{2,1,0:T(8,128)(2,1)S(1)}, bf16[1,8,8192]{2,1,0:T(8,128)(2,1)S(1)}, u32[]{:S(2)}, u32[]{:S(2)}) collective-permute-start(bf16[1,8,8192]{2,1,0:T(8,128)(2,1)S(1)} %collective-permute-done.20.refs_1_.refs_7_.refs_2_), channel_id=1, source_target_pairs={{0,2},{1,15},{2,4},{3,1},{4,6},{5,3},{6,8},{7,5},{8,10},{9,7},{10,... | collective-permute-start | bytes 393224 | tf_op jit(solution)/shard_map/ppermute | solution.py:345
  51.6 1.3 %collective-permute-start.25 = (bf16[1,8,8192]{2,1,0:T(8,128)(2,1)S(1)}, bf16[1,8,8192]{2,1,0:T(8,128)(2,1)S(1)}, u32[]{:S(2)}, u32[]{:S(2)}) collective-permute-start(bf16[1,8,8192]{2,1,0:T(8,128)(2,1)S(1)} %collective-permute-done.21.refs_8_.refs_3_), channel_id=1, source_target_pairs={{0,2},{1,15},{2,4},{3,1},{4,6},{5,3},{6,8},{7,5},{8,10},{9,7},{10,... | collective-permute-start | bytes 393224 | tf_op jit(solution)/shard_map/ppermute | solution.py:345
  52.9 2.3 %collective-permute-start.16 = (bf16[1,8,8192]{2,1,0:T(8,128)(2,1)S(1)}, bf16[1,8,8192]{2,1,0:T(8,128)(2,1)S(1)}, u32[]{:S(2)}, u32[]{:S(2)}) collective-permute-start(bf16[1,8,8192]{2,1,0:T(8,128)(2,1)S(1)} %collective-permute-done.15.refs_10_.refs_4_), channel_id=1, source_target_pairs={{0,2},{1,15},{2,4},{3,1},{4,6},{5,3},{6,8},{7,5},{8,10},{9,7},{10,... | collective-permute-start | bytes 393224 | tf_op jit(solution)/shard_map/ppermute | solution.py:345
  55.3 1.4 %collective-permute-start.27 = (bf16[1,8,8192]{2,1,0:T(8,128)(2,1)S(1)}, bf16[1,8,8192]{2,1,0:T(8,128)(2,1)S(1)}, u32[]{:S(2)}, u32[]{:S(2)}) collective-permute-start(bf16[1,8,8192]{2,1,0:T(8,128)(2,1)S(1)} %collective-permute-done.24.refs_12_.refs_6_), channel_id=1, source_target_pairs={{0,2},{1,15},{2,4},{3,1},{4,6},{5,3},{6,8},{7,5},{8,10},{9,7},{10,... | collective-permute-start | bytes 393224 | tf_op jit(solution)/shard_map/ppermute | solution.py:345
  56.7 0.6 collective-permute-done.25.refs_13_.refs_7_
  57.3 3.6 %collective-permute-start.30 = (bf16[8,8,8192]{2,1,0:T(8,128)(2,1)S(1)}, bf16[8,8,8192]{2,1,0:T(8,128)(2,1)S(1)}, u32[]{:S(2)}, u32[]{:S(2)}) collective-permute-start(bf16[8,8,8192]{2,1,0:T(8,128)(2,1)S(1)} %shard_map.58), channel_id=1, source_target_pairs={{0,1},{1,0},{2,3},{3,2},{4,5},{5,4},{6,7},{7,6},{8,9},{9,8},{10,11... | collective-permute-start | bytes 3145736 | tf_op jit(solution)/shard_map/ppermute | solution.py:348
  61.0 0.5 collective-permute-start.26
  61.5 0.3 collective-permute-start.17
  61.8 1.3 %collective-permute-start.28 = (bf16[1,8,8192]{2,1,0:T(8,128)(2,1)S(1)}, bf16[1,8,8192]{2,1,0:T(8,128)(2,1)S(1)}, u32[]{:S(2)}, u32[]{:S(2)}) collective-permute-start(bf16[1,8,8192]{2,1,0:T(8,128)(2,1)S(1)} %collective-permute-done.25.refs_13_.refs_7_), channel_id=1, source_target_pairs={{0,2},{1,15},{2,4},{3,1},{4,6},{5,3},{6,8},{7,5},{8,10},{9,7},{10,... | collective-permute-start | bytes 393224 | tf_op jit(solution)/shard_map/ppermute | solution.py:345
  63.2 3.0 %collective-permute-start.29 = (bf16[1,8,8192]{2,1,0:T(8,128)(2,1)S(1)}, bf16[1,8,8192]{2,1,0:T(8,128)(2,1)S(1)}, u32[]{:S(2)}, u32[]{:S(2)}) collective-permute-start(bf16[1,8,8192]{2,1,0:T(8,128)(2,1)S(1)} %shard_map.57), channel_id=1, source_target_pairs={{0,2},{1,15},{2,4},{3,1},{4,6},{5,3},{6,8},{7,5},{8,10},{9,7},{10,... | collective-permute-start | bytes 393224 | tf_op jit(solution)/shard_map/ppermute | solution.py:345
  66.2 0.3 collective-permute-done.17.refs_0_.refs_5_.refs_4_
  66.5 1.3 %shard_map.56 = (bf16[1,8,16384]{2,1,0:T(8,128)(2,1)}, f32[8,128]{1,0:T(8,128)S(1)}, bf16[16,8,16384]{2,1,0:T(8,128)(2,1)}) custom-call(bf16[1,8,8192]{2,1,0:T(8,128)(2,1)S(1)} %collective-permute-done.17.refs_0_.refs_5_.refs_4_, bf16[1,8,8192]{2,1,0:T(8,128)(2,1)S(1)} %get-tuple-element.47.refs_1_, bf16[1,8,8192]{2,1,0:T(8,128)(2,1)S(1)} %get-tuple-element.48.refs_2_, ...), custom_call_target="tpu_custom_call" | custom-call | flops 1 | bytes 1 | tf_op jit(solution)/shard_map/pallas_call | solution.py:326
  67.9 1.4 %collective-permute-done.29.refs_6_.refs_5_ = bf16[1,8,8192]{2,1,0:T(8,128)(2,1)S(1)} collective-permute-done((bf16[1,8,8192]{2,1,0:T(8,128)(2,1)S(1)}, bf16[1,8,8192]{2,1,0:T(8,128)(2,1)S(1)}, u32[]{:S(2)}, u32[]{:S(2)}) %collective-permute-start.29) | collective-permute-done | bytes 131104 | tf_op jit(solution)/shard_map/ppermute | solution.py:345
  69.3 2.6 %collective-permute-start.31 = (bf16[6,8,8192]{2,1,0:T(8,128)(2,1)S(1)}, bf16[6,8,8192]{2,1,0:T(8,128)(2,1)S(1)}, u32[]{:S(2)}, u32[]{:S(2)}) collective-permute-start(bf16[6,8,8192]{2,1,0:T(8,128)(2,1)S(1)} %shard_map.60), channel_id=1, source_target_pairs={{0,1},{1,0},{2,3},{3,2},{4,5},{5,4},{6,7},{7,6},{8,9},{9,8},{10,11... | collective-permute-start | bytes 2359304 | tf_op jit(solution)/shard_map/ppermute | solution.py:348
  72.0 1.9 %shard_map.59 = (f32[8,128]{1,0:T(8,128)}, bf16[16,8,16384]{2,1,0:T(8,128)(2,1)}) custom-call(bf16[16,8,16384]{2,1,0:T(8,128)(2,1)} %get-tuple-element.53.refs_0_, bf16[1,8,8192]{2,1,0:T(8,128)(2,1)S(1)} %collective-permute-done.16.refs_1_.refs_0_, bf16[1,8,8192]{2,1,0:T(8,128)(2,1)S(1)} %collective-permute-done.26.refs_2_.refs_1_, ...), custom_call_target="tpu_custom_call", output_to_operand_aliasing={{1}: (0, {})} | custom-call | flops 1 | bytes 1 | tf_op jit(solution)/shard_map/pallas_call | solution.py:326
  73.9 1.5 %shard_map.61 = (f32[8,128]{1,0:T(8,128)}, bf16[16,8,16384]{2,1,0:T(8,128)(2,1)}) custom-call(bf16[16,8,16384]{2,1,0:T(8,128)(2,1)} %get-tuple-element.54.refs_0_, bf16[6,8,8192]{2,1,0:T(8,128)(2,1)S(1)} %collective-permute-done.31.refs_1_), custom_call_target="tpu_custom_call", output_to_operand_aliasing={{1}: (0, {})} | custom-call | flops 1 | bytes 1 | tf_op jit(solution)/shard_map/pallas_call | solution.py:326
  (37 shorter events, 0.8 us)
Async XLA Ops:
  4.4 10.5 %collective-permute-start.3 = (bf16[2,16,8192]{2,1,0:T(8,128)(2,1)S(1)}, bf16[2,16,8192]{2,1,0:T(8,128)(2,1)S(1)}, u32[]{:S(2)}, u32[]{:S(2)}) collective-permute-start(bf16[2,16,8192]{2,1,0:T(8,128)(2,1)S(1)} %get-tuple-element.33._), channel_id=1, source_target_pairs={{0,1},{1,0},{2,3},{3,2},{4,5},{5,4},{6,7},{7,6},{8,9},{9,8},{10,11... | collective-permute-start | bytes 1572872 | tf_op jit(solution)/shard_map/ppermute | solution.py:348
  7.7 1.9 %collective-permute-start.4 = (bf16[1,16,8192]{2,1,0:T(8,128)(2,1)S(1)}, bf16[1,16,8192]{2,1,0:T(8,128)(2,1)S(1)}, u32[]{:S(2)}, u32[]{:S(2)}) collective-permute-start(bf16[1,16,8192]{2,1,0:T(8,128)(2,1)S(1)} %get-tuple-element.32._), channel_id=1, source_target_pairs={{0,1},{1,0},{2,3},{3,2},{4,5},{5,4},{6,7},{7,6},{8,9},{9,8},{10,11... | collective-permute-start | bytes 786440 | tf_op jit(solution)/shard_map/ppermute | solution.py:348
  9.1 11.1 %collective-permute-start.2 = (bf16[2,16,8192]{2,1,0:T(8,128)(2,1)S(1)}, bf16[2,16,8192]{2,1,0:T(8,128)(2,1)S(1)}, u32[]{:S(2)}, u32[]{:S(2)}) collective-permute-start(bf16[2,16,8192]{2,1,0:T(8,128)(2,1)S(1)} %get-tuple-element.34._), channel_id=1, source_target_pairs={{0,1},{1,0},{2,3},{3,2},{4,5},{5,4},{6,7},{7,6},{8,9},{9,8},{10,11... | collective-permute-start | bytes 1572872 | tf_op jit(solution)/shard_map/ppermute | solution.py:348
  9.7 7.2 %collective-permute-start.5 = (bf16[16,8192]{1,0:T(8,128)(2,1)S(1)}, bf16[16,8192]{1,0:T(8,128)(2,1)S(1)}, u32[]{:S(2)}, u32[]{:S(2)}) collective-permute-start(bf16[16,8192]{1,0:T(8,128)(2,1)S(1)} %shard_map.46), channel_id=1, source_target_pairs={{0,2},{1,15},{2,4},{3,1},{4,6},{5,3},{6,8},{7,5},{8,10},{9,7},{10,... | collective-permute-start | bytes 786440 | tf_op jit(solution)/shard_map/ppermute | solution.py:345
  15.0 5.6 %collective-permute-start.9 = (bf16[16,8192]{1,0:T(8,128)(2,1)S(1)}, bf16[16,8192]{1,0:T(8,128)(2,1)S(1)}, u32[]{:S(2)}, u32[]{:S(2)}) collective-permute-start(bf16[16,8192]{1,0:T(8,128)(2,1)S(1)} %shard_map.50), channel_id=1, source_target_pairs={{0,2},{1,15},{2,4},{3,1},{4,6},{5,3},{6,8},{7,5},{8,10},{9,7},{10,... | collective-permute-start | bytes 786440 | tf_op jit(solution)/shard_map/ppermute | solution.py:345
  15.8 12.2 %collective-permute-start.1 = (bf16[2,16,8192]{2,1,0:T(8,128)(2,1)S(1)}, bf16[2,16,8192]{2,1,0:T(8,128)(2,1)S(1)}, u32[]{:S(2)}, u32[]{:S(2)}) collective-permute-start(bf16[2,16,8192]{2,1,0:T(8,128)(2,1)S(1)} %get-tuple-element.35._), channel_id=1, source_target_pairs={{0,1},{1,0},{2,3},{3,2},{4,5},{5,4},{6,7},{7,6},{8,9},{9,8},{10,11... | collective-permute-start | bytes 1572872 | tf_op jit(solution)/shard_map/ppermute | solution.py:348
  17.0 6.5 %collective-permute-start.6 = (bf16[16,8192]{1,0:T(8,128)(2,1)S(1)}, bf16[16,8192]{1,0:T(8,128)(2,1)S(1)}, u32[]{:S(2)}, u32[]{:S(2)}) collective-permute-start(bf16[16,8192]{1,0:T(8,128)(2,1)S(1)} %shard_map.47), channel_id=1, source_target_pairs={{0,2},{1,15},{2,4},{3,1},{4,6},{5,3},{6,8},{7,5},{8,10},{9,7},{10,... | collective-permute-start | bytes 786440 | tf_op jit(solution)/shard_map/ppermute | solution.py:345
  20.7 7.3 %collective-permute-start.10 = (bf16[16,8192]{1,0:T(8,128)(2,1)S(1)}, bf16[16,8192]{1,0:T(8,128)(2,1)S(1)}, u32[]{:S(2)}, u32[]{:S(2)}) collective-permute-start(bf16[16,8192]{1,0:T(8,128)(2,1)S(1)} %shard_map.51), channel_id=1, source_target_pairs={{0,2},{1,15},{2,4},{3,1},{4,6},{5,3},{6,8},{7,5},{8,10},{9,7},{10,... | collective-permute-start | bytes 786440 | tf_op jit(solution)/shard_map/ppermute | solution.py:345
  23.7 8.6 %collective-permute-start.7 = (bf16[16,8192]{1,0:T(8,128)(2,1)S(1)}, bf16[16,8192]{1,0:T(8,128)(2,1)S(1)}, u32[]{:S(2)}, u32[]{:S(2)}) collective-permute-start(bf16[16,8192]{1,0:T(8,128)(2,1)S(1)} %shard_map.48), channel_id=1, source_target_pairs={{0,2},{1,15},{2,4},{3,1},{4,6},{5,3},{6,8},{7,5},{8,10},{9,7},{10,... | collective-permute-start | bytes 786440 | tf_op jit(solution)/shard_map/ppermute | solution.py:345
  27.9 9.5 %collective-permute-start = (bf16[2,8,8192]{2,1,0:T(8,128)(2,1)S(1)}, bf16[2,8,8192]{2,1,0:T(8,128)(2,1)S(1)}, u32[]{:S(2)}, u32[]{:S(2)}) collective-permute-start(bf16[2,8,8192]{2,1,0:T(8,128)(2,1)S(1)} %get-tuple-element.38), channel_id=1, source_target_pairs={{0,1},{1,0},{2,3},{3,2},{4,5},{5,4},{6,7},{7,6},{8,9},{9,8},{10,11... | collective-permute-start | bytes 786440 | tf_op jit(solution)/shard_map/ppermute | solution.py:348
  28.2 9.2 %collective-permute-start.11 = (bf16[1,8,8192]{2,1,0:T(8,128)(2,1)S(1)}, bf16[1,8,8192]{2,1,0:T(8,128)(2,1)S(1)}, u32[]{:S(2)}, u32[]{:S(2)}) collective-permute-start(bf16[1,8,8192]{2,1,0:T(8,128)(2,1)S(1)} %get-tuple-element.44), channel_id=1, source_target_pairs={{0,2},{1,15},{2,4},{3,1},{4,6},{5,3},{6,8},{7,5},{8,10},{9,7},{10,... | collective-permute-start | bytes 393224 | tf_op jit(solution)/shard_map/ppermute | solution.py:345
  30.9 6.5 %collective-permute-start.13 = (bf16[1,8,8192]{2,1,0:T(8,128)(2,1)S(1)}, bf16[1,8,8192]{2,1,0:T(8,128)(2,1)S(1)}, u32[]{:S(2)}, u32[]{:S(2)}) collective-permute-start(bf16[1,8,8192]{2,1,0:T(8,128)(2,1)S(1)} %get-tuple-element.46), channel_id=1, source_target_pairs={{0,3},{1,14},{2,5},{3,0},{4,7},{5,2},{6,9},{7,4},{8,11},{9,6},{10,... | collective-permute-start | bytes 393224 | tf_op jit(solution)/shard_map/ppermute | solution.py:345
  32.4 5.0 %collective-permute-start.8 = (bf16[1,8,8192]{2,1,0:T(8,128)(2,1)S(1)}, bf16[1,8,8192]{2,1,0:T(8,128)(2,1)S(1)}, u32[]{:S(2)}, u32[]{:S(2)}) collective-permute-start(bf16[1,8,8192]{2,1,0:T(8,128)(2,1)S(1)} %get-tuple-element.43), channel_id=1, source_target_pairs={{0,2},{1,15},{2,4},{3,1},{4,6},{5,3},{6,8},{7,5},{8,10},{9,7},{10,... | collective-permute-start | bytes 393224 | tf_op jit(solution)/shard_map/ppermute | solution.py:345
  33.7 7.8 %collective-permute-start.12 = (bf16[1,8,8192]{2,1,0:T(8,128)(2,1)S(1)}, bf16[1,8,8192]{2,1,0:T(8,128)(2,1)S(1)}, u32[]{:S(2)}, u32[]{:S(2)}) collective-permute-start(bf16[1,8,8192]{2,1,0:T(8,128)(2,1)S(1)} %get-tuple-element.45), channel_id=1, source_target_pairs={{0,3},{1,14},{2,5},{3,0},{4,7},{5,2},{6,9},{7,4},{8,11},{9,6},{10,... | collective-permute-start | bytes 393224 | tf_op jit(solution)/shard_map/ppermute | solution.py:345
  41.9 1.8 %collective-permute-start.18 = (bf16[2,8,8192]{2,1,0:T(8,128)(2,1)S(1)}, bf16[2,8,8192]{2,1,0:T(8,128)(2,1)S(1)}, u32[]{:S(2)}, u32[]{:S(2)}) collective-permute-start(bf16[2,8,8192]{2,1,0:T(8,128)(2,1)S(1)} %get-tuple-element.49), channel_id=1, source_target_pairs={{0,1},{1,0},{2,3},{3,2},{4,5},{5,4},{6,7},{7,6},{8,9},{9,8},{10,11... | collective-permute-start | bytes 786440 | tf_op jit(solution)/shard_map/ppermute | solution.py:348
  42.0 5.3 %collective-permute-start.14 = (bf16[1,8,8192]{2,1,0:T(8,128)(2,1)S(1)}, bf16[1,8,8192]{2,1,0:T(8,128)(2,1)S(1)}, u32[]{:S(2)}, u32[]{:S(2)}) collective-permute-start(bf16[1,8,8192]{2,1,0:T(8,128)(2,1)S(1)} %get-tuple-element.47.refs_1_), channel_id=1, source_target_pairs={{0,2},{1,15},{2,4},{3,1},{4,6},{5,3},{6,8},{7,5},{8,10},{9,7},{10,... | collective-permute-start | bytes 393224 | tf_op jit(solution)/shard_map/ppermute | solution.py:345
  43.7 5.2 %collective-permute-start.20 = (bf16[1,8,8192]{2,1,0:T(8,128)(2,1)S(1)}, bf16[1,8,8192]{2,1,0:T(8,128)(2,1)S(1)}, u32[]{:S(2)}, u32[]{:S(2)}) collective-permute-start(bf16[1,8,8192]{2,1,0:T(8,128)(2,1)S(1)} %get-tuple-element.50.refs_3_), channel_id=1, source_target_pairs={{0,2},{1,15},{2,4},{3,1},{4,6},{5,3},{6,8},{7,5},{8,10},{9,7},{10,... | collective-permute-start | bytes 393224 | tf_op jit(solution)/shard_map/ppermute | solution.py:345
  45.0 6.6 %collective-permute-start.19 = (bf16[1,8,8192]{2,1,0:T(8,128)(2,1)S(1)}, bf16[1,8,8192]{2,1,0:T(8,128)(2,1)S(1)}, u32[]{:S(2)}, u32[]{:S(2)}) collective-permute-start(bf16[1,8,8192]{2,1,0:T(8,128)(2,1)S(1)} %get-tuple-element.48.refs_2_), channel_id=1, source_target_pairs={{0,2},{1,15},{2,4},{3,1},{4,6},{5,3},{6,8},{7,5},{8,10},{9,7},{10,... | collective-permute-start | bytes 393224 | tf_op jit(solution)/shard_map/ppermute | solution.py:345
  45.1 6.5 %collective-permute-start.21 = (bf16[1,8,8192]{2,1,0:T(8,128)(2,1)S(1)}, bf16[1,8,8192]{2,1,0:T(8,128)(2,1)S(1)}, u32[]{:S(2)}, u32[]{:S(2)}) collective-permute-start(bf16[1,8,8192]{2,1,0:T(8,128)(2,1)S(1)} %get-tuple-element.51.refs_4_), channel_id=1, source_target_pairs={{0,2},{1,15},{2,4},{3,1},{4,6},{5,3},{6,8},{7,5},{8,10},{9,7},{10,... | collective-permute-start | bytes 393224 | tf_op jit(solution)/shard_map/ppermute | solution.py:345
  47.4 5.6 %collective-permute-start.15 = (bf16[1,8,8192]{2,1,0:T(8,128)(2,1)S(1)}, bf16[1,8,8192]{2,1,0:T(8,128)(2,1)S(1)}, u32[]{:S(2)}, u32[]{:S(2)}) collective-permute-start(bf16[1,8,8192]{2,1,0:T(8,128)(2,1)S(1)} %collective-permute-done.14.refs_5_.refs_0_), channel_id=1, source_target_pairs={{0,2},{1,15},{2,4},{3,1},{4,6},{5,3},{6,8},{7,5},{8,10},{9,7},{10,... | collective-permute-start | bytes 393224 | tf_op jit(solution)/shard_map/ppermute | solution.py:345
  49.0 12.9 %collective-permute-start.22 = (bf16[2,8,8192]{2,1,0:T(8,128)(2,1)S(1)}, bf16[2,8,8192]{2,1,0:T(8,128)(2,1)S(1)}, u32[]{:S(2)}, u32[]{:S(2)}) collective-permute-start(bf16[2,8,8192]{2,1,0:T(8,128)(2,1)S(1)} %shard_map.55), channel_id=1, source_target_pairs={{0,16},{16,32},{32,48},{48,64},{64,80},{80,96},{96,112},{112,128},... | collective-permute-start | bytes 786440 | tf_op jit(solution)/shard_map/ppermute | solution.py:386
  50.3 4.9 %collective-permute-start.24 = (bf16[1,8,8192]{2,1,0:T(8,128)(2,1)S(1)}, bf16[1,8,8192]{2,1,0:T(8,128)(2,1)S(1)}, u32[]{:S(2)}, u32[]{:S(2)}) collective-permute-start(bf16[1,8,8192]{2,1,0:T(8,128)(2,1)S(1)} %collective-permute-done.20.refs_1_.refs_7_.refs_2_), channel_id=1, source_target_pairs={{0,2},{1,15},{2,4},{3,1},{4,6},{5,3},{6,8},{7,5},{8,10},{9,7},{10,... | collective-permute-start | bytes 393224 | tf_op jit(solution)/shard_map/ppermute | solution.py:345
  51.5 5.2 %collective-permute-start.23 = (bf16[1,8,8192]{2,1,0:T(8,128)(2,1)S(1)}, bf16[1,8,8192]{2,1,0:T(8,128)(2,1)S(1)}, u32[]{:S(2)}, u32[]{:S(2)}) collective-permute-start(bf16[1,8,8192]{2,1,0:T(8,128)(2,1)S(1)} %collective-permute-done.19.refs_6_.refs_1_), channel_id=1, source_target_pairs={{0,2},{1,15},{2,4},{3,1},{4,6},{5,3},{6,8},{7,5},{8,10},{9,7},{10,... | collective-permute-start | bytes 393224 | tf_op jit(solution)/shard_map/ppermute | solution.py:345
  51.6 5.7 %collective-permute-start.25 = (bf16[1,8,8192]{2,1,0:T(8,128)(2,1)S(1)}, bf16[1,8,8192]{2,1,0:T(8,128)(2,1)S(1)}, u32[]{:S(2)}, u32[]{:S(2)}) collective-permute-start(bf16[1,8,8192]{2,1,0:T(8,128)(2,1)S(1)} %collective-permute-done.21.refs_8_.refs_3_), channel_id=1, source_target_pairs={{0,2},{1,15},{2,4},{3,1},{4,6},{5,3},{6,8},{7,5},{8,10},{9,7},{10,... | collective-permute-start | bytes 393224 | tf_op jit(solution)/shard_map/ppermute | solution.py:345
  52.9 8.5 %collective-permute-start.16 = (bf16[1,8,8192]{2,1,0:T(8,128)(2,1)S(1)}, bf16[1,8,8192]{2,1,0:T(8,128)(2,1)S(1)}, u32[]{:S(2)}, u32[]{:S(2)}) collective-permute-start(bf16[1,8,8192]{2,1,0:T(8,128)(2,1)S(1)} %collective-permute-done.15.refs_10_.refs_4_), channel_id=1, source_target_pairs={{0,2},{1,15},{2,4},{3,1},{4,6},{5,3},{6,8},{7,5},{8,10},{9,7},{10,... | collective-permute-start | bytes 393224 | tf_op jit(solution)/shard_map/ppermute | solution.py:345
  55.3 7.9 %collective-permute-start.27 = (bf16[1,8,8192]{2,1,0:T(8,128)(2,1)S(1)}, bf16[1,8,8192]{2,1,0:T(8,128)(2,1)S(1)}, u32[]{:S(2)}, u32[]{:S(2)}) collective-permute-start(bf16[1,8,8192]{2,1,0:T(8,128)(2,1)S(1)} %collective-permute-done.24.refs_12_.refs_6_), channel_id=1, source_target_pairs={{0,2},{1,15},{2,4},{3,1},{4,6},{5,3},{6,8},{7,5},{8,10},{9,7},{10,... | collective-permute-start | bytes 393224 | tf_op jit(solution)/shard_map/ppermute | solution.py:345
  57.3 14.6 %collective-permute-start.30 = (bf16[8,8,8192]{2,1,0:T(8,128)(2,1)S(1)}, bf16[8,8,8192]{2,1,0:T(8,128)(2,1)S(1)}, u32[]{:S(2)}, u32[]{:S(2)}) collective-permute-start(bf16[8,8,8192]{2,1,0:T(8,128)(2,1)S(1)} %shard_map.58), channel_id=1, source_target_pairs={{0,1},{1,0},{2,3},{3,2},{4,5},{5,4},{6,7},{7,6},{8,9},{9,8},{10,11... | collective-permute-start | bytes 3145736 | tf_op jit(solution)/shard_map/ppermute | solution.py:348
  61.0 6.9 %collective-permute-start.26 = (bf16[1,8,8192]{2,1,0:T(8,128)(2,1)S(1)}, bf16[1,8,8192]{2,1,0:T(8,128)(2,1)S(1)}, u32[]{:S(2)}, u32[]{:S(2)}) collective-permute-start(bf16[1,8,8192]{2,1,0:T(8,128)(2,1)S(1)} %collective-permute-done.23.refs_11_.refs_5_), channel_id=1, source_target_pairs={{0,2},{1,15},{2,4},{3,1},{4,6},{5,3},{6,8},{7,5},{8,10},{9,7},{10,... | collective-permute-start | bytes 393224 | tf_op jit(solution)/shard_map/ppermute | solution.py:345
  61.5 5.0 %collective-permute-start.17 = (bf16[1,8,8192]{2,1,0:T(8,128)(2,1)S(1)}, bf16[1,8,8192]{2,1,0:T(8,128)(2,1)S(1)}, u32[]{:S(2)}, u32[]{:S(2)}) collective-permute-start(bf16[1,8,8192]{2,1,0:T(8,128)(2,1)S(1)} %collective-permute-done.16.refs_1_.refs_0_), channel_id=1, source_target_pairs={{0,2},{1,15},{2,4},{3,1},{4,6},{5,3},{6,8},{7,5},{8,10},{9,7},{10,... | collective-permute-start | bytes 393224 | tf_op jit(solution)/shard_map/ppermute | solution.py:345
  61.8 6.0 %collective-permute-start.28 = (bf16[1,8,8192]{2,1,0:T(8,128)(2,1)S(1)}, bf16[1,8,8192]{2,1,0:T(8,128)(2,1)S(1)}, u32[]{:S(2)}, u32[]{:S(2)}) collective-permute-start(bf16[1,8,8192]{2,1,0:T(8,128)(2,1)S(1)} %collective-permute-done.25.refs_13_.refs_7_), channel_id=1, source_target_pairs={{0,2},{1,15},{2,4},{3,1},{4,6},{5,3},{6,8},{7,5},{8,10},{9,7},{10,... | collective-permute-start | bytes 393224 | tf_op jit(solution)/shard_map/ppermute | solution.py:345
  63.2 6.1 %collective-permute-start.29 = (bf16[1,8,8192]{2,1,0:T(8,128)(2,1)S(1)}, bf16[1,8,8192]{2,1,0:T(8,128)(2,1)S(1)}, u32[]{:S(2)}, u32[]{:S(2)}) collective-permute-start(bf16[1,8,8192]{2,1,0:T(8,128)(2,1)S(1)} %shard_map.57), channel_id=1, source_target_pairs={{0,2},{1,15},{2,4},{3,1},{4,6},{5,3},{6,8},{7,5},{8,10},{9,7},{10,... | collective-permute-start | bytes 393224 | tf_op jit(solution)/shard_map/ppermute | solution.py:345
  69.3 4.6 %collective-permute-start.31 = (bf16[6,8,8192]{2,1,0:T(8,128)(2,1)S(1)}, bf16[6,8,8192]{2,1,0:T(8,128)(2,1)S(1)}, u32[]{:S(2)}, u32[]{:S(2)}) collective-permute-start(bf16[6,8,8192]{2,1,0:T(8,128)(2,1)S(1)} %shard_map.60), channel_id=1, source_target_pairs={{0,1},{1,0},{2,3},{3,2},{4,5},{5,4},{6,7},{7,6},{8,9},{9,8},{10,11... | collective-permute-start | bytes 2359304 | tf_op jit(solution)/shard_map/ppermute | solution.py:348
